TPU v7x, 32 devices: a whole 2x2x4 slice. The times are simulated.
32 devices in a mesh: ctx: 8 (over z, x), tp: 4 (over y, core).
Axes of the slice: x: 2, y: 2, z: 4, core: 2. Of those that a mesh axis runs over, the one named last changes fastest.
Arguments:
- q_one: bfloat16 [2048, 4096], P('ctx', 'tp'), may hold values from -880 to 880
- k_one: bfloat16 [2048, 4096], P('ctx', 'tp'), may hold values from -6 to 6
- v_one: bfloat16 [2048, 4096], P('ctx', 'tp'), may hold values from -6 to 6
- q_two: bfloat16 [2048, 4096], P('ctx', 'tp'), may hold values from -6 to 6
- k_two: bfloat16 [2048, 4096], P('ctx', 'tp'), may hold values from -6 to 6
- short_taps: bfloat16 [3, 7, 256], P(None, None, 'tp'), may hold values from -2 to 2
- medium_taps: bfloat16 [128, 256], P(None, 'tp'), may hold values from -0.5 to 0.5
- long_taps: bfloat16 [256, 2048], P('tp', 'ctx'), may hold values from -0.125 to 0.125
- skip_gain: float32 [4096], P('tp'), may hold values from -4 to 4
- block_order: int32 [8], replicated, may hold values from 0 to 7, as said below
- prev_owner: int32 [8], replicated, may hold values from 0 to 7, as said below
Outputs:
- gated_out: bfloat16 [2048, 4096], P('ctx', 'tp')
Inputs may be any that keep to these rules, and one draw needn't show every extreme that they name: `block_order`: A permutation of the 8 sequence blocks over the devices of ctx. prev_owner[b] is the device d with block_order[d] = b - 1 for b > 0, and prev_owner[0] the device holding block 7.
All inputs are finite; a program needn't handle non-finite values.
Results may differ from a plain program's by a relative error of at most 0.008.
Values may be sent and summed in bfloat16 or wider, within the bound.
No kernel may reach another device: no remote copies, remote signals or barrier semaphores. Data moves between devices by JAX's collectives and lax.ppermute only.
A program may use at most 128 MiB of HBM per device.

v0:
```python
import math

import jax
import jax.numpy as jnp
from jax import lax
from jax.sharding import PartitionSpec as P

EPSILON = 1e-06
HIGHEST = lax.Precision.HIGHEST


def lanes_filter(signal, kernel_taps):
    flipped = jnp.transpose(kernel_taps[::-1])[:, None, :]
    result = lax.conv_general_dilated(
        signal[None],
        flipped,
        (1,),
        "VALID",
        dimension_numbers=("NCW", "OIW", "NCW"),
        feature_group_count=signal.shape[0],
        preferred_element_type=jnp.float32,
    )
    return result[0]


def angle_table(first_len, second_len, period):
    first = jnp.arange(first_len, dtype=jnp.int32)
    second = jnp.arange(second_len, dtype=jnp.int32)
    angle = 2.0 * math.pi / period * (first[:, None] * second[None, :] % period).astype(jnp.float32)
    return (jnp.cos(angle), jnp.sin(angle))


def forward_spectrum(signal, half_outer, tables):
    outer_cos, outer_sin, twist_cos, twist_sin, inner_cos, inner_sin = tables
    real_a = jnp.einsum("kn,bnm->bkm", outer_cos[:, :half_outer], signal, precision=HIGHEST)
    imag_a = -jnp.einsum("kn,bnm->bkm", outer_sin[:, :half_outer], signal, precision=HIGHEST)
    real_b = real_a * twist_cos + imag_a * twist_sin
    imag_b = imag_a * twist_cos - real_a * twist_sin
    real_c = jnp.einsum("bkm,mj->bkj", real_b, inner_cos, precision=HIGHEST) + jnp.einsum(
        "bkm,mj->bkj", imag_b, inner_sin, precision=HIGHEST
    )
    imag_c = jnp.einsum("bkm,mj->bkj", imag_b, inner_cos, precision=HIGHEST) - jnp.einsum(
        "bkm,mj->bkj", real_b, inner_sin, precision=HIGHEST
    )
    return (real_c, imag_c)


def inverse_spectrum(real_p, imag_p, half_outer, tables):
    outer_cos, outer_sin, twist_cos, twist_sin, inner_cos, inner_sin = tables
    real_q = jnp.einsum("bkj,jm->bkm", real_p, inner_cos, precision=HIGHEST) - jnp.einsum(
        "bkj,jm->bkm", imag_p, inner_sin, precision=HIGHEST
    )
    imag_q = jnp.einsum("bkj,jm->bkm", imag_p, inner_cos, precision=HIGHEST) + jnp.einsum(
        "bkj,jm->bkm", real_p, inner_sin, precision=HIGHEST
    )
    real_r = real_q * twist_cos - imag_q * twist_sin
    imag_r = imag_q * twist_cos + real_q * twist_sin
    return jnp.einsum(
        "nk,bkm->bnm", outer_cos[:half_outer], real_r, precision=HIGHEST
    ) - jnp.einsum("nk,bkm->bnm", outer_sin[:half_outer], imag_r, precision=HIGHEST)


def long_mix(values, long_rows, gain_local, block_rows):
    channels, length = values.shape
    outer_len = length // block_rows
    inner_len = 2 * block_rows
    half_outer = outer_len // 2
    padded_len = 2 * length
    outer_cos, outer_sin = angle_table(outer_len, outer_len, outer_len)
    twist_cos, twist_sin = angle_table(outer_len, inner_len, padded_len)
    inner_cos, inner_sin = angle_table(inner_len, inner_len, inner_len)
    tables = (outer_cos, outer_sin, twist_cos, twist_sin, inner_cos, inner_sin)
    value_float = values.astype(jnp.float32)
    real_x, imag_x = forward_spectrum(
        value_float.reshape(channels, half_outer, inner_len), half_outer, tables
    )
    real_h, imag_h = forward_spectrum(
        long_rows.astype(jnp.float32).reshape(long_rows.shape[0], half_outer, inner_len),
        half_outer,
        tables,
    )
    group_size = channels // long_rows.shape[0]
    real_h = jnp.repeat(real_h, group_size, axis=0)
    imag_h = jnp.repeat(imag_h, group_size, axis=0)
    real_p = real_x * real_h - imag_x * imag_h
    imag_p = real_x * imag_h + imag_x * real_h
    long_part = inverse_spectrum(real_p, imag_p, half_outer, tables) / padded_len
    return (long_part.reshape(channels, length) + gain_local[:, None] * value_float).astype(
        jnp.bfloat16
    )


def per_device(
    q_one,
    k_one,
    v_one,
    q_two,
    k_two,
    short_taps,
    medium_taps,
    long_taps,
    skip_gain,
    block_order,
    prev_owner,
):
    block_rows, local_width = q_one.shape
    ctx_count = lax.axis_size("ctx")
    device_pos = lax.axis_index("ctx")
    group_size = local_width // short_taps.shape[2]
    short_lead = short_taps.shape[1] - 1
    medium_reach = medium_taps.shape[0] - 1
    lane_width = local_width // ctx_count
    full_width = local_width * lax.axis_size("tp")
    short_lanes = jnp.repeat(short_taps, group_size, axis=2)
    medium_lanes = jnp.repeat(medium_taps, group_size, axis=1)
    lane_start = device_pos * lane_width
    slots = jnp.arange(ctx_count, dtype=jnp.int32)
    holder = jnp.sum(jnp.where(block_order[None, :] == slots[:, None], slots[None, :], 0), axis=1)

    def ordered(array):
        return jnp.take(array.reshape(lane_width, ctx_count, block_rows), holder, axis=1).reshape(
            lane_width, ctx_count * block_rows
        )

    moved = (
        lax.all_to_all(jnp.transpose(q_one), "ctx", split_axis=0, concat_axis=1, tiled=True),
        lax.all_to_all(jnp.transpose(k_one), "ctx", split_axis=0, concat_axis=1, tiled=True),
        lax.all_to_all(jnp.transpose(v_one), "ctx", split_axis=0, concat_axis=1, tiled=True),
        lax.all_to_all(jnp.transpose(k_two), "ctx", split_axis=0, concat_axis=1, tiled=True),
        lax.all_to_all(long_taps, "ctx", split_axis=0, concat_axis=1, tiled=True),
    )
    q_seq = ordered(moved[0])
    k_seq = ordered(moved[1])
    v_seq = ordered(moved[2])
    gate_seq = ordered(moved[3])
    long_rows = moved[4]
    short_local = lax.dynamic_slice_in_dim(short_lanes, lane_start, lane_width, axis=2)
    medium_local = lax.dynamic_slice_in_dim(medium_lanes, lane_start, lane_width, axis=1)
    q_feat = lanes_filter(jnp.pad(q_seq, ((0, 0), (short_lead, 0))), short_local[0])
    k_feat = lanes_filter(jnp.pad(k_seq, ((0, 0), (short_lead, 0))), short_local[1])
    v_feat = lanes_filter(jnp.pad(v_seq, ((0, 0), (short_lead, 0))), short_local[2])
    z_one = (k_feat * v_feat).astype(jnp.bfloat16)
    medium = lanes_filter(jnp.pad(z_one, ((0, 0), (medium_reach, 0))), medium_local)
    mixed = q_feat * medium
    energy = lax.psum(jnp.sum(mixed * mixed, axis=0), ("ctx", "tp"))
    values = (
        gate_seq.astype(jnp.float32) * mixed * lax.rsqrt(energy / full_width + EPSILON)[None, :]
    ).astype(jnp.bfloat16)
    gain_local = lax.dynamic_slice_in_dim(skip_gain, lane_start, lane_width)
    mixed_seq = long_mix(values, long_rows, gain_local, block_rows)
    device_major = jnp.take(
        mixed_seq.reshape(lane_width, ctx_count, block_rows), block_order, axis=1
    ).reshape(lane_width, ctx_count * block_rows)
    returned = lax.all_to_all(device_major, "ctx", split_axis=1, concat_axis=0, tiled=True)
    return (q_two.astype(jnp.float32) * jnp.transpose(returned).astype(jnp.float32)).astype(
        jnp.bfloat16
    )


def solution(mesh):
    in_specs = (
        P("ctx", "tp"),
        P("ctx", "tp"),
        P("ctx", "tp"),
        P("ctx", "tp"),
        P("ctx", "tp"),
        P(None, None, "tp"),
        P(None, "tp"),
        P("tp", "ctx"),
        P("tp"),
        P(),
        P(),
    )
    out_specs = P("ctx", "tp")
    return jax.shard_map(
        per_device, mesh=mesh, in_specs=in_specs, out_specs=out_specs, check_vma=False
    )
```

profile of v0, /device:TPU:0, one launch (start us, length us, event | category | flops | bytes accessed | tf_op | source)
XLA Modules:
  0.0 273.2 jit_solution(2574790516149780187)
XLA Ops:
  0.0 7.4 %all-to-all-start.4 = ((bf16[8,8,256]{2,1,0:T(8,128)(2,1)}), bf16[8,8,256]{2,1,0:T(8,128)(2,1)S(1)}, u32[]{:S(2)}, u32[]{:S(2)}) async-start(bf16[8,8,256]{2,1,0:T(8,128)(2,1)} %bitcast.215), calls=%async_computation.4 | async-start | bytes 65536 | tf_op jit(solution)/shard_map/all_to_all | solution.py:130
  7.4 2.1 copy.107
  9.5 4.6 %all-to-all-done.4 = bf16[8,8,256]{2,1,0:T(8,128)(2,1)S(1)} async-done(((bf16[8,8,256]{2,1,0:T(8,128)(2,1)}), bf16[8,8,256]{2,1,0:T(8,128)(2,1)S(1)}, u32[]{:S(2)}, u32[]{:S(2)}) %all-to-all-start.4) | async-done | bytes 32800 | tf_op jit(solution)/shard_map/all_to_all | solution.py:130
  14.1 3.6 %all-to-all-start = ((bf16[8,128,256]{2,1,0:T(8,128)(2,1)}), bf16[8,128,256]{2,1,0:T(8,128)(2,1)S(1)}, u32[]{:S(2)}, u32[]{:S(2)}) async-start(bf16[8,128,256]{2,1,0:T(8,128)(2,1)} %bitcast.1), calls=%async_computation | async-start | bytes 1048576 | tf_op jit(solution)/shard_map/all_to_all | solution.py:129
  17.7 1.0 copy.109
  18.9 12.1 %all-to-all-done = bf16[8,128,256]{2,1,0:T(8,128)(2,1)S(1)} async-done(((bf16[8,128,256]{2,1,0:T(8,128)(2,1)}), bf16[8,128,256]{2,1,0:T(8,128)(2,1)S(1)}, u32[]{:S(2)}, u32[]{:S(2)}) %all-to-all-start) | async-done | bytes 524320 | tf_op jit(solution)/shard_map/all_to_all | solution.py:129
  31.0 3.8 %all-to-all-start.1 = ((bf16[8,128,256]{2,1,0:T(8,128)(2,1)}), bf16[8,128,256]{2,1,0:T(8,128)(2,1)S(1)}, u32[]{:S(2)}, u32[]{:S(2)}) async-start(bf16[8,128,256]{2,1,0:T(8,128)(2,1)} %bitcast.6), calls=%async_computation.1 | async-start | bytes 1048576 | tf_op jit(solution)/shard_map/all_to_all | solution.py:126
  34.8 1.0 copy.115
  36.1 0.4 reshape.134
  36.7 11.9 %all-to-all-done.1 = bf16[8,128,256]{2,1,0:T(8,128)(2,1)S(1)} async-done(((bf16[8,128,256]{2,1,0:T(8,128)(2,1)}), bf16[8,128,256]{2,1,0:T(8,128)(2,1)S(1)}, u32[]{:S(2)}, u32[]{:S(2)}) %all-to-all-start.1) | async-done | bytes 524320 | tf_op jit(solution)/shard_map/all_to_all | solution.py:126
  48.6 3.6 %all-to-all-start.2 = ((bf16[8,128,256]{2,1,0:T(8,128)(2,1)}), bf16[8,128,256]{2,1,0:T(8,128)(2,1)S(1)}, u32[]{:S(2)}, u32[]{:S(2)}) async-start(bf16[8,128,256]{2,1,0:T(8,128)(2,1)} %bitcast.16), calls=%async_computation.2 | async-start | bytes 1048576 | tf_op jit(solution)/shard_map/all_to_all | solution.py:127
  52.3 1.0 copy.120
  53.4 0.8 copy.128
  54.2 0.8 dynamic_slice.11
  55.0 0.3 convolution_negate_fusion
  55.3 0.3 fusion.154
  55.6 10.5 %all-to-all-done.2 = bf16[8,128,256]{2,1,0:T(8,128)(2,1)S(1)} async-done(((bf16[8,128,256]{2,1,0:T(8,128)(2,1)}), bf16[8,128,256]{2,1,0:T(8,128)(2,1)S(1)}, u32[]{:S(2)}, u32[]{:S(2)}) %all-to-all-start.2) | async-done | bytes 524320 | tf_op jit(solution)/shard_map/all_to_all | solution.py:127
  66.1 3.8 %all-to-all-start.3 = ((bf16[8,128,256]{2,1,0:T(8,128)(2,1)}), bf16[8,128,256]{2,1,0:T(8,128)(2,1)S(1)}, u32[]{:S(2)}, u32[]{:S(2)}) async-start(bf16[8,128,256]{2,1,0:T(8,128)(2,1)} %bitcast.26), calls=%async_computation.3 | async-start | bytes 1048576 | tf_op jit(solution)/shard_map/all_to_all | solution.py:128
  69.9 4.7 %fusion.70 = f32[8,8,512]{2,1,0:T(8,128)S(1)} fusion(f32[8,8,512]{2,0,1:T(8,128)S(1)} %convolution_negate_fusion, f32[8,8,512]{2,0,1:T(8,128)S(1)} %fusion.154, f32[8,512]{1,0:T(8,128)S(1)} %get-tuple-element.19, f32[8,512]{1,0:T(8,128)S(1)} %get-tuple-element.20), kind=kOutput, calls=%fused_computation.83 | convolution fusion | flops 205094912 | bytes 425984 | tf_op jit(solution)/shard_map/bkm,mj->bkj/dot_general | solution.py:39
  74.7 4.8 %convolution_add_fusion = f32[8,8,512]{2,1,0:T(8,128)S(1)} fusion(f32[8,8,512]{2,1,0:T(8,128)S(1)} %fusion.70, f32[8,8,512]{2,0,1:T(8,128)S(1)} %fusion.154, f32[8,8,512]{2,0,1:T(8,128)S(1)} %convolution_negate_fusion, f32[8,512]{1,0:T(8,128)S(1)} %get-tuple-element.19, f32[8,512]{1,0:T(8,128)S(1)} %get-tuple-element.20), kind=kOutput, calls=%fused_computation.61 | convolution fusion | flops 205127680 | bytes 557056 | tf_op jit(solution)/shard_map/bkm,mj->bkj/dot_general | solution.py:39
  79.5 4.7 %fusion.67 = f32[8,8,512]{2,1,0:T(8,128)S(1)} fusion(f32[8,8,512]{2,0,1:T(8,128)S(1)} %fusion.154, f32[8,8,512]{2,0,1:T(8,128)S(1)} %convolution_negate_fusion, f32[8,512]{1,0:T(8,128)S(1)} %get-tuple-element.19, f32[8,512]{1,0:T(8,128)S(1)} %get-tuple-element.20), kind=kOutput, calls=%fused_computation.80 | convolution fusion | flops 205094912 | bytes 425984 | tf_op jit(solution)/shard_map/bkm,mj->bkj/dot_general | solution.py:42
  84.3 5.2 %convolution_subtract_fusion = f32[8,8,512]{2,1,0:T(8,128)S(1)} fusion(f32[8,8,512]{2,1,0:T(8,128)S(1)} %fusion.67, f32[8,8,512]{2,0,1:T(8,128)S(1)} %convolution_negate_fusion, f32[8,8,512]{2,0,1:T(8,128)S(1)} %fusion.154, f32[8,512]{1,0:T(8,128)S(1)} %get-tuple-element.19, f32[8,512]{1,0:T(8,128)S(1)} %get-tuple-element.20), kind=kOutput, calls=%fused_computation.60 | convolution fusion | flops 205127680 | bytes 557056 | tf_op jit(solution)/shard_map/bkm,mj->bkj/dot_general | solution.py:42
  89.5 0.6 gather_fusion
  90.1 0.6 gather_fusion.1
  90.7 0.6 gather_fusion.2
  91.3 0.8 copy-done.3
  92.1 1.6 gather_fusion.3
  93.7 1.4 bitcast_convert_fusion
  95.1 0.3 copy.116
  95.9 0.3 copy.121
  96.6 0.3 copy-done.13
  96.9 0.6 convolution_select_fusion.1
  97.5 2.4 fusion.51
  100.6 0.4 copy-done.9
  101.0 11.8 %convolution_select_fusion.3 = f32[8,272,128]{2,0,1:T(8,128)S(1)} fusion(bf16[128,1,128]{0,1,2:T(2,128)(2,1)S(1)} %copy-done.9, bf16[128,1,7,127]{0,2,3,1:T(8,128)(2,1)S(1)} %slice.56, bf16[128,1,8,272]{0,2,3,1:T(8,128)(2,1)S(1)} %copy.127, pred[8,272]{0,1:T(8,128)(4,1)S(1)} %copy-done.12), kind=kOutput, calls=%fused_computation.58 | convolution fusion | flops 74033152 | bytes 1933696 | tf_op jit(solution)/shard_map/conv_general_dilated | solution.py:14
  113.1 0.8 copy-done.2
  113.9 0.3 copy.110
  114.6 0.6 convolution_select_fusion.2
  115.5 1.1 reshape.165
  116.5 1.6 fusion.73
  118.1 40.9 %psum.7 = f32[2048]{0:T(1024)S(1)} all-reduce(f32[2048]{0:T(1024)S(1)} %get-tuple-element.6), channel_id=1, replica_groups=mesh['ctx'=8,'tp'=4] {'ctx','tp'}, use_global_device_ids=true, to_apply=%region_2.4 | all-reduce | flops 2048 | bytes 16384 | tf_op jit(solution)/shard_map/psum | solution.py:145
  159.0 1.6 copy.108
  160.6 1.1 fusion.75
  161.7 1.4 copy.130
  163.2 1.2 fusion.152
  164.4 1.6 fusion.2
  166.0 8.2 %fusion.20 = f32[128,8,512]{2,0,1:T(8,128)S(1)} fusion(f32[128,8,512]{2,1,0:T(8,128)S(1)} %get-tuple-element.11), kind=kOutput, calls=%fused_computation.33 | convolution fusion | flops 3224895488 | bytes 4194304 | tf_op jit(solution)/shard_map/bkm,mj->bkj/dot_general | solution.py:42
  174.1 8.4 %fusion.22 = f32[128,8,512]{2,0,1:T(8,128)S(1)} fusion(f32[128,8,512]{2,1,0:T(8,128)S(1)} %get-tuple-element.11), kind=kOutput, calls=%fused_computation.35 | convolution fusion | flops 3224895488 | bytes 4194304 | tf_op jit(solution)/shard_map/bkm,mj->bkj/dot_general | solution.py:39
  182.5 8.6 %fusion.32 = f32[128,8,512]{2,0,1:T(8,128)S(1)} fusion(f32[128,8,512]{2,0,1:T(8,128)S(1)} %fusion.20, f32[128,8,512]{2,1,0:T(8,128)S(1)} %get-tuple-element.10), kind=kOutput, calls=%fused_computation.44 | convolution fusion | flops 3225419776 | bytes 6291456 | tf_op jit(solution)/shard_map/bkm,mj->bkj/dot_general | solution.py:42
  191.1 10.5 %fusion = (f32[128,8,512]{2,0,1:T(8,128)}, f32[128,8,512]{2,0,1:T(8,128)S(1)}) fusion(f32[128,8,512]{2,0,1:T(8,128)S(1)} %fusion.32, f32[8,8,512]{2,0,1:T(8,128)S(1)} %copy.138, f32[8,8,512]{2,0,1:T(8,128)S(1)} %copy.135, f32[128,8,512]{2,0,1:T(8,128)S(1)} %fusion.22, f32[128,8,512]{2,1,0:T(8,128)S(1)} %get-tuple-element.10), kind=kOutput, calls=%fused_computation.9 | convolution fusion | flops 3228565504 | bytes 10747904 | tf_op jit(solution)/shard_map/bkm,mj->bkj/dot_general | solution.py:39
  201.6 10.3 %fusion.12 = f32[128,8,512]{2,1,0:T(8,128)} fusion(f32[128,8,512]{2,0,1:T(8,128)S(1)} %get-tuple-element.9), kind=kOutput, calls=%fused_computation.25 | convolution fusion | flops 3224895488 | bytes 4194304 | tf_op jit(solution)/shard_map/bkj,jm->bkm/dot_general | solution.py:53
  211.9 10.1 %fusion.14 = f32[128,8,512]{2,1,0:T(8,128)} fusion(f32[128,8,512]{2,0,1:T(8,128)S(1)} %get-tuple-element.9), kind=kOutput, calls=%fused_computation.27 | convolution fusion | flops 3224895488 | bytes 4194304 | tf_op jit(solution)/shard_map/bkj,jm->bkm/dot_general | solution.py:50
  222.0 12.2 %fusion.38 = f32[128,8,512]{2,1,0:T(8,128)S(1)} fusion(f32[128,8,512]{2,1,0:T(8,128)} %fusion.12, f32[128,8,512]{2,0,1:T(8,128)} %get-tuple-element.8), kind=kOutput, calls=%fused_computation.46 | convolution fusion | flops 3225419776 | bytes 6291456 | tf_op jit(solution)/shard_map/bkj,jm->bkm/dot_general | solution.py:53
  234.2 8.2 %fusion.35 = f32[128,8,512]{2,1,0:T(8,128)S(1)} fusion(f32[128,8,512]{2,1,0:T(8,128)S(1)} %copy-done.14, f32[128,8,512]{2,0,1:T(8,128)S(1)} %copy-done.4), kind=kOutput, calls=%fused_computation.45 | convolution fusion | flops 3225419776 | bytes 6291456 | tf_op jit(solution)/shard_map/bkj,jm->bkm/dot_general | solution.py:50
  242.4 2.1 fusion.4
  244.4 3.3 %fusion.48 = f32[128,4,512]{2,1,0:T(4,128)} fusion(f32[128,512,4]{1,2,0:T(4,128)S(1)} %fusion.4, f32[128,8,512]{2,1,0:T(8,128)S(1)} %fusion.38, f32[128,8,512]{2,1,0:T(8,128)S(1)} %fusion.35, f32[8,512]{1,0:T(8,128)S(1)} %get-tuple-element.19, f32[8,512]{1,0:T(8,128)S(1)} %get-tuple-element.20, f32[8,8]{0,1:T(8,128)S(1)} %fusion.159), kind=kOutput, calls=%fused_computation.56 | convolution fusion | flops 27262976 | bytes 6324480 | tf_op jit(solution)/shard_map/nk,bkm->bnm/dot_general | solution.py:58
  247.7 1.6 reshape.141
  249.4 1.3 copy.145
  250.7 1.7 fusion.76
  252.4 0.6 gather_fusion.4
  253.1 17.8 %all_to_all.90 = bf16[128,8,256]{2,0,1:T(8,128)(2,1)S(1)} all-to-all(bf16[128,8,256]{2,0,1:T(8,128)(2,1)S(1)} %select_bitcast_fusion), channel_id=1, replica_groups=mesh['ctx'=8,'tp'=4] {'ctx'}, dimensions={1} | all-to-all | bytes 1048576 | tf_op jit(solution)/shard_map/all_to_all | solution.py:154
  271.1 0.3 copy.147
  271.4 0.6 copy-done.8
  272.0 0.9 fusion.58
  (77 shorter events, 3.6 us)
Async XLA Ops:
  0.0 36.7 %copy-start = (bf16[128,64]{0,1:T(8,128)(2,1)S(1)}, bf16[128,64]{0,1:T(8,128)(2,1)}, u32[]{:S(2)}) copy-start(bf16[128,64]{0,1:T(8,128)(2,1)} %param.19) | copy-start | bytes 49156
  0.0 17.7 %copy-start.5 = (bf16[256,1024]{1,0:T(8,128)(2,1)S(1)}, bf16[256,1024]{1,0:T(8,128)(2,1)}, u32[]{:S(2)}) copy-start(bf16[256,1024]{1,0:T(8,128)(2,1)} %param.13) | copy-start | bytes 1572868
  0.0 18.8 %copy-start.11 = (s32[8]{0:T(128)S(1)}, s32[8]{0:T(128)}, u32[]{:S(2)}) copy-start(s32[8]{0:T(128)} %param.22) | copy-start | bytes 100
  0.0 14.1 %all-to-all-start.4 = ((bf16[8,8,256]{2,1,0:T(8,128)(2,1)}), bf16[8,8,256]{2,1,0:T(8,128)(2,1)S(1)}, u32[]{:S(2)}, u32[]{:S(2)}) async-start(bf16[8,8,256]{2,1,0:T(8,128)(2,1)} %bitcast.215), calls=%async_computation.4 | async-start | bytes 65536 | tf_op jit(solution)/shard_map/all_to_all | solution.py:130
  7.4 27.4 %copy-start.6 = (bf16[256,1024]{1,0:T(8,128)(2,1)S(1)}, bf16[256,1024]{1,0:T(8,128)(2,1)}, u32[]{:S(2)}) copy-start(bf16[256,1024]{1,0:T(8,128)(2,1)} %param.14) | copy-start | bytes 1572868
  14.1 21.8 %copy-start.10 = (bf16[3,7,64]{2,1,0:T(8,128)(2,1)S(1)}, bf16[3,7,64]{2,1,0:T(8,128)(2,1)}, u32[]{:S(2)}) copy-start(bf16[3,7,64]{2,1,0:T(8,128)(2,1)} %param.18) | copy-start | bytes 8068
  14.1 16.9 %all-to-all-start = ((bf16[8,128,256]{2,1,0:T(8,128)(2,1)}), bf16[8,128,256]{2,1,0:T(8,128)(2,1)S(1)}, u32[]{:S(2)}, u32[]{:S(2)}) async-start(bf16[8,128,256]{2,1,0:T(8,128)(2,1)} %bitcast.1), calls=%async_computation | async-start | bytes 1048576 | tf_op jit(solution)/shard_map/all_to_all | solution.py:129
  31.0 21.3 %copy-start.7 = (bf16[256,1024]{1,0:T(8,128)(2,1)S(1)}, bf16[256,1024]{1,0:T(8,128)(2,1)}, u32[]{:S(2)}) copy-start(bf16[256,1024]{1,0:T(8,128)(2,1)} %param.15) | copy-start | bytes 1572868
  31.0 17.6 %all-to-all-start.1 = ((bf16[8,128,256]{2,1,0:T(8,128)(2,1)}), bf16[8,128,256]{2,1,0:T(8,128)(2,1)S(1)}, u32[]{:S(2)}, u32[]{:S(2)}) async-start(bf16[8,128,256]{2,1,0:T(8,128)(2,1)} %bitcast.6), calls=%async_computation.1 | async-start | bytes 1048576 | tf_op jit(solution)/shard_map/all_to_all | solution.py:126
  48.6 17.4 %all-to-all-start.2 = ((bf16[8,128,256]{2,1,0:T(8,128)(2,1)}), bf16[8,128,256]{2,1,0:T(8,128)(2,1)S(1)}, u32[]{:S(2)}, u32[]{:S(2)}) async-start(bf16[8,128,256]{2,1,0:T(8,128)(2,1)} %bitcast.16), calls=%async_computation.2 | async-start | bytes 1048576 | tf_op jit(solution)/shard_map/all_to_all | solution.py:127
  66.1 25.2 %all-to-all-start.3 = ((bf16[8,128,256]{2,1,0:T(8,128)(2,1)}), bf16[8,128,256]{2,1,0:T(8,128)(2,1)S(1)}, u32[]{:S(2)}, u32[]{:S(2)}) async-start(bf16[8,128,256]{2,1,0:T(8,128)(2,1)} %bitcast.26), calls=%async_computation.3 | async-start | bytes 1048576 | tf_op jit(solution)/shard_map/all_to_all | solution.py:128
  91.3 0.8 copy-start.3
  96.1 0.8 copy-start.13
  100.2 0.8 copy-start.9
  100.2 0.8 copy-start.12
  112.8 1.0 copy-start.2
  222.0 12.2 %copy-start.4 = (f32[128,8,512]{2,0,1:T(8,128)S(1)}, f32[128,8,512]{2,0,1:T(8,128)}, u32[]{:S(2)}) copy-start(f32[128,8,512]{2,0,1:T(8,128)} %get-tuple-element.8) | copy-start | bytes 6291460
  222.0 12.2 %copy-start.14 = (f32[128,8,512]{2,1,0:T(8,128)S(1)}, f32[128,8,512]{2,1,0:T(8,128)}, u32[]{:S(2)}) copy-start(f32[128,8,512]{2,1,0:T(8,128)} %fusion.14) | copy-start | bytes 6291460
  270.9 1.0 copy-start.8
  271.0 1.9 copy-start.1
where the time goes:
time: 277 us; the launch traced here: 273 us
  matrix products  120 us (43%)
  blocking collectives  58.7 us (21%)
  waiting for transfers between devices  39 us (14%)
  local copies, waits for them, and re-layouts  25.2 us (9%)
  starting transfers between devices  22.3 us (8%)
  other arithmetic  7.29 us (3%)
    psum x1, blocking collectives, per_device(): energy = lax.psum(jnp.sum(mixed * mixed, axis=0), ('ctx', 'tp'))  40.9 us
    all_to_all x1, blocking collectives, per_device(): lax.all_to_all(device_major, 'ctx', split_axis=1, concat_axis=0, tiled=True)  17.8 us
    conv_general_dilated x4, matrix products, lanes_filter(): lax.conv_general_dilated(signal[None], flipped, (1,), 'VALID', dimension_...  15.4 us
    dot_general x2, matrix products, forward_spectrum(): jnp.einsum('bkm,mj->bkj', real_b, inner_cos, precision=HIGHEST)  15.3 us
    dot_general x2, matrix products, forward_spectrum(): jnp.einsum('bkm,mj->bkj', real_b, inner_sin, precision=HIGHEST)  13.8 us
    dot_general x2, matrix products, forward_spectrum(): jnp.einsum('bkm,mj->bkj', imag_b, inner_sin, precision=HIGHEST)  13.1 us
    dot_general x2, matrix products, forward_spectrum(): jnp.einsum('bkm,mj->bkj', imag_b, inner_cos, precision=HIGHEST)  12.9 us
    dot_general x1, matrix products, inverse_spectrum(): jnp.einsum('bkj,jm->bkm', real_p, inner_sin, precision=HIGHEST)  12.2 us
  transfers between devices with their start and end apart: 5, of which 4 were waited for; matrix products, arithmetic and copies ran while one was open for 11% of the time, Pallas kernels for 0%

commit v1 on v0

v1 whole, which is shorter than its diff:
```python
import jax
import jax.numpy as jnp
from jax import lax
from jax.experimental import pallas as pl
from jax.experimental.pallas import tpu as pltpu
from jax.sharding import PartitionSpec as P

EPSILON = 1e-06
LANES = 128
EDGE = 8
VMEM_BYTES = 56 * 1024 * 1024


def params(*semantics):
    return pltpu.CompilerParams(dimension_semantics=semantics, vmem_limit_bytes=VMEM_BYTES)


def short_filter(extended, taps, start, rows):
    total = extended[start : start + rows] * taps[0:1]
    for j in range(1, taps.shape[0]):
        total = total + extended[start - j : start - j + rows] * taps[j : j + 1]
    return total


def tail_kernel(q_ref, k_ref, v_ref, taps_ref, out_ref):
    rows = q_ref.shape[0]
    reach = out_ref.shape[1] - 4 * EDGE
    first = rows - reach - 16
    k_part = k_ref[first:, :].astype(jnp.float32)
    v_part = v_ref[first:, :].astype(jnp.float32)
    k_feat = short_filter(k_part, taps_ref[1], 16, reach)
    v_feat = short_filter(v_part, taps_ref[2], 16, reach)
    out_ref[0, :reach, :] = (k_feat * v_feat).astype(jnp.bfloat16)
    q_part = q_ref[rows - 16 :, :].astype(jnp.float32)
    edges = jnp.concatenate(
        [q_part[16 - EDGE :], k_part[-EDGE:], v_part[-EDGE:], jnp.zeros((EDGE, LANES), jnp.float32)],
        axis=0,
    )
    out_ref[0, reach:, :] = edges.astype(jnp.bfloat16)


def medium_table_kernel(base_ref, out_ref):
    reach, wide = out_ref.shape[1], base_ref.shape[2]
    for g in range(base_ref.shape[1]):
        row = jnp.broadcast_to(base_ref[0, g : g + 1, :], (reach, wide))
        out_ref[0, :, g * wide : (g + 1) * wide] = pltpu.roll(
            row, 0, 1, stride=1, stride_axis=0
        ).astype(jnp.bfloat16)


def long_table_kernel(base_ref, out_ref):
    lags, rows, _ = out_ref.shape[1:]
    strip = jnp.broadcast_to(base_ref[0], (rows, base_ref.shape[2]))
    strip = pltpu.roll(strip, 0, 1, stride=1, stride_axis=0)
    for lag in range(lags):
        out_ref[0, lag] = strip[:, (lag + 1) * rows : (lag + 2) * rows].astype(jnp.bfloat16)


def mix_kernel(
    first_ref, q_ref, k_ref, v_ref, gate_ref, halo_ref, taps_ref, table_ref, out_ref, energy_ref, squares_ref
):
    rows = q_ref.shape[0]
    reach = table_ref.shape[1]
    tile = pl.program_id(0)
    keep = jnp.where(first_ref[0] != 0, 0.0, 1.0)
    edges = halo_ref[0, reach:, :].astype(jnp.float32) * keep

    def feature(ref, which):
        extended = jnp.concatenate(
            [edges[which * EDGE : (which + 1) * EDGE], ref[...].astype(jnp.float32)], axis=0
        )
        return short_filter(extended, taps_ref[which], EDGE, rows)

    q_feat = feature(q_ref, 0)
    z_own = (feature(k_ref, 1) * feature(v_ref, 2)).astype(jnp.bfloat16)
    z_halo = (halo_ref[0, :reach, :].astype(jnp.float32) * keep).astype(jnp.bfloat16)
    window = jnp.concatenate(
        [jnp.concatenate([z_halo, z_own[:reach]], axis=0), z_own], axis=1
    )
    wide = window.shape[0]
    groups = table_ref.shape[2] // wide
    lane_group = lax.broadcasted_iota(jnp.int32, (1, 2 * LANES), 1) % LANES // (LANES // groups)
    medium = jnp.zeros((reach, 2 * LANES), jnp.float32)
    for g in range(groups):
        masked = window * (lane_group == g).astype(jnp.bfloat16)
        medium = medium + jnp.dot(
            table_ref[0, :, g * wide : (g + 1) * wide], masked, preferred_element_type=jnp.float32
        )
    mixed = q_feat * jnp.concatenate([medium[:, :LANES], medium[:, LANES:]], axis=0)
    out_ref[0] = jnp.transpose(mixed * gate_ref[...].astype(jnp.float32))

    @pl.when(tile == 0)
    def _():
        squares_ref[...] = mixed * mixed

    @pl.when(tile != 0)
    def _():
        squares_ref[...] += mixed * mixed

    @pl.when(tile == pl.num_programs(0) - 1)
    def _():
        energy_ref[...] = jnp.sum(jnp.transpose(squares_ref[...]), axis=0, keepdims=True)


def long_kernel(holder_ref, value_ref, table_ref, gain_ref, out_ref, ordered_ref, total_ref):
    blocks, size, rows = value_ref.shape
    lags = table_ref.shape[1]
    piece = pl.program_id(1)
    reach = blocks * size

    @pl.when(piece == 0)
    def _():
        ordered_ref[:reach] = jnp.zeros((reach, rows), jnp.bfloat16)
        for b in range(blocks):
            ordered_ref[reach + b * size : reach + (b + 1) * size] = value_ref[holder_ref[b]]
        total_ref[...] = ordered_ref[reach:].astype(jnp.float32) * gain_ref[0]

    def lagged(lag):
        if lags == blocks:
            return ordered_ref[(blocks - lag) * size : (2 * blocks - lag) * size]
        start = pl.multiple_of((blocks - piece * lags - lag) * size, size)
        return ordered_ref[pl.ds(start, reach)]

    left = jnp.concatenate([lagged(lag) for lag in range(lags)], axis=1)
    right = table_ref[0].reshape(lags * rows, rows)
    total_ref[...] += jnp.dot(left, right, preferred_element_type=jnp.float32)

    @pl.when(piece == pl.num_programs(1) - 1)
    def _():
        for b in range(blocks):
            out_ref[holder_ref[b]] = total_ref[b * size : (b + 1) * size].astype(jnp.bfloat16)


def gate_kernel(mixed_ref, gate_ref, out_ref):
    mixed = jnp.transpose(mixed_ref[0].astype(jnp.float32))
    out_ref[...] = (gate_ref[...].astype(jnp.float32) * mixed).astype(jnp.bfloat16)


def per_device(
    q_one,
    k_one,
    v_one,
    q_two,
    k_two,
    short_taps,
    medium_taps,
    long_taps,
    skip_gain,
    block_order,
    prev_owner,
):
    rows, width = q_one.shape
    ctx_count = lax.axis_size("ctx")
    tp_count = lax.axis_size("tp")
    me = lax.axis_index("ctx")
    local_groups = short_taps.shape[2]
    size = width // local_groups
    reach = medium_taps.shape[0]
    assert rows == 2 * reach and short_taps.shape[1] <= EDGE + 1
    tiles = width // LANES
    tile_groups = LANES // size
    shard = width // ctx_count
    shard_groups = shard // size
    full_width = width * tp_count

    slots = jnp.arange(ctx_count, dtype=jnp.int32)
    holder = jnp.sum(jnp.where(block_order[None, :] == slots[:, None], slots[None, :], 0), axis=1)
    source = jnp.take(prev_owner, block_order, mode="clip")
    is_first = (lax.dynamic_slice_in_dim(block_order, me, 1) == 0).astype(jnp.int32)
    short_lanes = jnp.repeat(short_taps, size, axis=2).astype(jnp.float32)

    column = pl.BlockSpec((rows, LANES), lambda i: (0, i))
    taps_spec = pl.BlockSpec((3, short_taps.shape[1], LANES), lambda i: (0, 0, i))
    tail_rows = reach + 4 * EDGE
    tail_spec = pl.BlockSpec((1, tail_rows, LANES), lambda i: (i, 0, 0))
    turned_spec = pl.BlockSpec((1, LANES, rows), lambda i: (i, 0, 0))

    tails = pl.pallas_call(
        tail_kernel,
        grid=(tiles,),
        in_specs=[column, column, column, taps_spec],
        out_specs=tail_spec,
        out_shape=jax.ShapeDtypeStruct((tiles, tail_rows, LANES), jnp.bfloat16),
        compiler_params=params("arbitrary"),
        name="tails",
    )(q_one, k_one, v_one, short_lanes)
    halo_rows = tiles * tail_rows // ctx_count
    taps_rows = shard_groups * rows // LANES
    payload = jnp.concatenate(
        [
            tails.reshape(ctx_count, halo_rows, LANES),
            long_taps.reshape(ctx_count, taps_rows, LANES),
        ],
        axis=1,
    )
    spread = lax.all_to_all(payload, "ctx", split_axis=0, concat_axis=0, tiled=True)
    routed = jnp.take(spread[:, :halo_rows], source, axis=0, mode="clip")
    halo = lax.all_to_all(routed, "ctx", split_axis=0, concat_axis=0, tiled=True)
    halo = halo.reshape(tiles, tail_rows, LANES)

    base = jnp.pad(jnp.transpose(medium_taps[::-1]), ((0, 0), (1, rows - reach - 1)))
    medium_table = pl.pallas_call(
        medium_table_kernel,
        grid=(tiles,),
        in_specs=[pl.BlockSpec((1, tile_groups, rows), lambda i: (i, 0, 0))],
        out_specs=pl.BlockSpec((1, reach, tile_groups * rows), lambda i: (i, 0, 0)),
        out_shape=jax.ShapeDtypeStruct((tiles, reach, tile_groups * rows), jnp.bfloat16),
        compiler_params=params("arbitrary"),
        name="medium_table",
    )(base.astype(jnp.float32).reshape(tiles, tile_groups, rows))

    lags = min(ctx_count, 8)
    pieces = ctx_count // lags
    long_rows = jnp.transpose(
        spread[:, halo_rows:].reshape(ctx_count, shard_groups, rows), (1, 0, 2)
    ).reshape(shard_groups, ctx_count * rows)
    long_rows = jnp.pad(long_rows.astype(jnp.float32), ((0, 0), (rows, 0)))
    windows = jnp.stack(
        [long_rows[:, p * lags * rows : (p * lags + lags + 1) * rows] for p in range(pieces)], axis=1
    ).reshape(shard_groups * pieces, 1, (lags + 1) * rows)
    long_table = pl.pallas_call(
        long_table_kernel,
        grid=(shard_groups * pieces,),
        in_specs=[pl.BlockSpec((1, 1, (lags + 1) * rows), lambda i: (i, 0, 0))],
        out_specs=pl.BlockSpec((1, lags, rows, rows), lambda i: (i, 0, 0, 0)),
        out_shape=jax.ShapeDtypeStruct((shard_groups * pieces, lags, rows, rows), jnp.bfloat16),
        compiler_params=params("arbitrary"),
        name="long_table",
    )(windows)

    gated, energy = pl.pallas_call(
        mix_kernel,
        grid=(tiles,),
        in_specs=[
            pl.BlockSpec(memory_space=pltpu.SMEM),
            column,
            column,
            column,
            column,
            tail_spec,
            taps_spec,
            pl.BlockSpec((1, reach, tile_groups * rows), lambda i: (i, 0, 0)),
        ],
        out_specs=[turned_spec, pl.BlockSpec((1, rows), lambda i: (0, 0))],
        out_shape=[
            jax.ShapeDtypeStruct((tiles, LANES, rows), jnp.float32),
            jax.ShapeDtypeStruct((1, rows), jnp.float32),
        ],
        scratch_shapes=[pltpu.VMEM((rows, LANES), jnp.float32)],
        compiler_params=params("arbitrary"),
        name="mix",
    )(is_first, q_one, k_one, v_one, k_two, halo, short_lanes, medium_table)

    total = energy
    for step in range(1, tp_count):
        total = total + lax.ppermute(
            energy, "tp", [(i, (i + step) % tp_count) for i in range(tp_count)]
        )
    scale = lax.rsqrt(total / full_width + EPSILON)
    values = (gated * scale[None]).astype(jnp.bfloat16).reshape(ctx_count, shard, rows)
    values = lax.all_to_all(values, "ctx", split_axis=0, concat_axis=0, tiled=True)

    gain = lax.dynamic_slice_in_dim(skip_gain, me * shard, shard).reshape(shard_groups, 1, size, 1)
    gain = jnp.broadcast_to(gain, (shard_groups, ctx_count, size, 1))
    gain = gain.reshape(shard_groups, ctx_count * size, 1)
    group_spec = pl.BlockSpec((ctx_count, size, rows), lambda g, p, order: (0, g, 0))
    long_out = pl.pallas_call(
        long_kernel,
        grid_spec=pltpu.PrefetchScalarGridSpec(
            num_scalar_prefetch=1,
            grid=(shard_groups, pieces),
            in_specs=[
                group_spec,
                pl.BlockSpec(
                    (1, lags, rows, rows), lambda g, p, order: (g * pieces + p, 0, 0, 0)
                ),
                pl.BlockSpec((1, ctx_count * size, 1), lambda g, p, order: (g, 0, 0)),
            ],
            out_specs=group_spec,
            scratch_shapes=[
                pltpu.VMEM((2 * ctx_count * size, rows), jnp.bfloat16),
                pltpu.VMEM((ctx_count * size, rows), jnp.float32),
            ],
        ),
        out_shape=jax.ShapeDtypeStruct((ctx_count, shard, rows), jnp.bfloat16),
        compiler_params=params("arbitrary", "arbitrary"),
        name="long",
    )(holder, values, long_table, gain)
    returned = lax.all_to_all(long_out, "ctx", split_axis=0, concat_axis=0, tiled=True)

    return pl.pallas_call(
        gate_kernel,
        grid=(tiles,),
        in_specs=[turned_spec, column],
        out_specs=column,
        out_shape=jax.ShapeDtypeStruct((rows, width), jnp.bfloat16),
        compiler_params=params("arbitrary"),
        name="gate",
    )(returned.reshape(tiles, LANES, rows), q_two)


def solution(mesh):
    in_specs = (
        P("ctx", "tp"),
        P("ctx", "tp"),
        P("ctx", "tp"),
        P("ctx", "tp"),
        P("ctx", "tp"),
        P(None, None, "tp"),
        P(None, "tp"),
        P("tp", "ctx"),
        P("tp"),
        P(),
        P(),
    )
    out_specs = P("ctx", "tp")
    return jax.shard_map(
        per_device, mesh=mesh, in_specs=in_specs, out_specs=out_specs, check_vma=False
    )
```

time: 277 us -> 113 us (0.41)
  matrix products: 120 us -> 0 us
  blocking collectives: 58.7 us -> 17.5 us
  Pallas kernels: 0 us -> 40.4 us
  waiting for transfers between devices: 39 us -> 16.9 us
  local copies, waits for them, and re-layouts: 25.2 us -> 11 us
  starting transfers between devices: 22.3 us -> 17.7 us
    dot_general x18 -> x0, matrix products: 104 us -> none  [the longest x2 15.3 us: forward_spectrum(): jnp.einsum('bkm,mj->bkj', real_b, inner_cos, precision=HIGHEST)]
    psum x1 -> x0, blocking collectives: 40.9 us -> none  [per_device(): energy = lax.psum(jnp.sum(mixed * mixed, axis=0), ('ctx', 'tp'))]
    pallas_call x0 -> x6, Pallas kernels: none -> 40.4 us  [the longest x1 9.28 us: per_device(): pl.pallas_call(mix_kernel, grid=(tiles,), in_specs=[pl.BlockSpec(memory_s...]
    all_to_all x5 -> x3, waiting for transfers between devices: 39 us -> 13.9 us  [the longest x1 9.69 us: per_device(): lax.all_to_all(payload, 'ctx', split_axis=0, concat_axis=0, tiled=True)]
    conv_general_dilated x4 -> x0, matrix products: 15.4 us -> none  [lanes_filter(): lax.conv_general_dilated(signal[None], flipped, (1,), 'VALID', dimension_...]
    all_to_all x5 -> x3, starting transfers between devices: 22.3 us -> 16 us  [the longest x1 7.25 us: per_device(): lax.all_to_all(payload, 'ctx', split_axis=0, concat_axis=0, tiled=True)]
    transpose x4 -> x0, local copies, waits for them, and re-layouts: 5.13 us -> none  [the longest x1 2.1 us: per_device(): jnp.transpose(k_two)]
    convert_element_type x5 -> x1, other arithmetic: 5.29 us -> 2.11 us  [per_device(): (gated * scale[None]).astype(jnp.bfloat16).reshape(ctx_count, shard, rows)]
  transfers between devices with their start and end apart: 5 -> 6, of which waited for: 4 -> 5; matrix products, arithmetic and copies ran while one was open for 11% -> 7% of each run, Pallas kernels for 0% -> 11%
where the time goes in v1:
time: 113 us; the launch traced here: 111 us
  Pallas kernels  40.4 us (36%)
  starting transfers between devices  17.7 us (16%)
  blocking collectives  17.5 us (15%)
  waiting for transfers between devices  16.9 us (15%)
  local copies, waits for them, and re-layouts  11 us (10%)
  other arithmetic  6.55 us (6%)
    all_to_all x1, blocking collectives, per_device(): lax.all_to_all(long_out, 'ctx', split_axis=0, concat_axis=0, tiled=True)  17.5 us
    all_to_all x1, waiting for transfers between devices, per_device(): lax.all_to_all(payload, 'ctx', split_axis=0, concat_axis=0, tiled=True)  9.69 us
    pallas_call x1, Pallas kernels, per_device(): pl.pallas_call(mix_kernel, grid=(tiles,), in_specs=[pl.BlockSpec(memory_s...  9.28 us
    pallas_call x1, Pallas kernels, per_device(): pl.pallas_call(long_kernel, grid_spec=pltpu.PrefetchScalarGridSpec(num_sc...  8.54 us
    all_to_all x1, starting transfers between devices, per_device(): lax.all_to_all(payload, 'ctx', split_axis=0, concat_axis=0, tiled=True)  7.25 us
    pallas_call x1, Pallas kernels, per_device(): pl.pallas_call(long_table_kernel, grid=(shard_groups * pieces,), in_specs...  6.36 us
    pallas_call x1, Pallas kernels, per_device(): pl.pallas_call(tail_kernel, grid=(tiles,), in_specs=[column, column, colu...  5.46 us
    pallas_call x1, Pallas kernels, per_device(): pl.pallas_call(medium_table_kernel, grid=(tiles,), in_specs=[pl.BlockSpec...  5.45 us
  transfers between devices with their start and end apart: 6, of which 5 were waited for; matrix products, arithmetic and copies ran while one was open for 7% of the time, Pallas kernels for 11%

profile of v1, /device:TPU:0, one launch (start us, length us, event | category | flops | bytes accessed | tf_op | source)
XLA Modules:
  0.0 110.7 jit_solution(11619090222746404640)
XLA Ops:
  0.0 0.0 copy-start
  0.0 0.8 reshape.26
  0.8 0.9 broadcast_in_dim.38
  1.7 1.0 convert_element_type.28.taps_ref
  2.7 5.5 %tails.1 = bf16[8,160,128]{2,1,0:T(8,128)(2,1)} custom-call(bf16[256,1024]{1,0:T(8,128)(2,1)} %q_ref.3, bf16[256,1024]{1,0:T(8,128)(2,1)} %k_ref.3, bf16[256,1024]{1,0:T(8,128)(2,1)} %v_ref.3, f32[3,7,1024]{2,1,0:T(8,128)} %convert_element_type.28.taps_ref), custom_call_target="tpu_custom_call" | custom-call | tf_op jit(solution)/shard_map/tails/pallas_call | solution.py:178
  8.2 1.7 %pad_maximum_fusion = bf16[8,176,128]{2,1,0:T(8,128)(2,1)} fusion(bf16[8,16,128]{2,1,0:T(8,128)(2,1)S(1)} %reshape.26, bf16[8,160,128]{2,1,0:T(8,128)(2,1)} %tails.1), kind=kLoop, calls=%fused_computation.3 | loop fusion | flops 720896 | bytes 720896 | tf_op jit(solution)/shard_map/concatenate | solution.py:189
  9.9 7.3 %all-to-all-start = ((bf16[8,176,128]{2,1,0:T(8,128)(2,1)}), bf16[8,176,128]{2,1,0:T(8,128)(2,1)S(1)}, u32[]{:S(2)}, u32[]{:S(2)}) async-start(bf16[8,176,128]{2,1,0:T(8,128)(2,1)} %pad_maximum_fusion), calls=%async_computation | async-start | bytes 720896 | tf_op jit(solution)/shard_map/all_to_all | solution.py:196
  17.2 0.7 pad_clamp_fusion.1
  17.8 0.0 copy-done
  17.8 0.0 copy-start.3
  17.8 0.6 gather_fusion
  18.5 9.7 %all-to-all-done = bf16[8,176,128]{2,1,0:T(8,128)(2,1)S(1)} async-done(((bf16[8,176,128]{2,1,0:T(8,128)(2,1)}), bf16[8,176,128]{2,1,0:T(8,128)(2,1)S(1)}, u32[]{:S(2)}, u32[]{:S(2)}) %all-to-all-start) | async-done | bytes 360480 | tf_op jit(solution)/shard_map/all_to_all | solution.py:196
  28.2 1.3 %gather_fusion.1 = bf16[8,160,128]{2,1,0:T(8,128)(2,1)} fusion(bf16[8,160,128]{2,1,0:T(8,128)(2,1)S(1)} %slice.12, s32[1024]{0:T(1024)S(1)} %pad_clamp_fusion), kind=kCustom, calls=%fused_computation.1 | custom fusion | bytes 655392 | tf_op jit(solution)/shard_map/jit(_take)/gather | solution.py:197
  29.5 3.6 %all-to-all-start.1 = ((bf16[8,160,128]{2,1,0:T(8,128)(2,1)}), bf16[8,160,128]{2,1,0:T(8,128)(2,1)S(1)}, u32[]{:S(2)}, u32[]{:S(2)}) async-start(bf16[8,160,128]{2,1,0:T(8,128)(2,1)} %gather_fusion.1), calls=%async_computation.1 | async-start | bytes 655360 | tf_op jit(solution)/shard_map/all_to_all | solution.py:198
  33.1 1.3 %dynamic_slice.6 = s32[1]{0:T(128)} dynamic-slice(s32[8]{0:T(128)} %param.20, s32[]{:T(128)S(6)} %select_n.11), dynamic_slice_sizes={1} | dynamic-slice | bytes 12 | tf_op jit(solution)/shard_map/dynamic_slice | solution.py:169
  35.0 0.8 rev.3
  35.8 0.7 bitcast_convert_fusion.base_ref
  36.5 5.4 %medium_table.1.table_ref = bf16[8,128,2048]{2,1,0:T(8,128)(2,1)} custom-call(f32[8,8,256]{2,1,0:T(8,128)} %bitcast_convert_fusion.base_ref), custom_call_target="tpu_custom_call" | custom-call | tf_op jit(solution)/shard_map/medium_table/pallas_call | solution.py:202
  42.0 0.9 all-to-all-done.1.halo_ref
  42.9 0.0 copy-start.2
  42.9 0.7 copy-done.2
  43.6 9.3 %mix.1 = (f32[8,128,256]{2,1,0:T(8,128)}, f32[1,256]{1,0:T(1,128)}) custom-call(s32[1]{0:T(128)S(6)} %convert_element_type.26.first_ref, bf16[256,1024]{1,0:T(8,128)(2,1)} %q_ref.3, bf16[256,1024]{1,0:T(8,128)(2,1)} %k_ref.3, bf16[256,1024]{1,0:T(8,128)(2,1)} %v_ref.3, bf16[256,1024]{1,0:T(8,128)(2,1)} %gate_ref.2, bf16[8,160,128]{2,1,0:T(8,128)(2,1)} %copy-done.2, ...), custom_call_target="tpu_custom_call" | custom-call | tf_op jit(solution)/shard_map/mix/pallas_call | solution.py:231
  52.9 0.0 collective-permute-start.2
  52.9 1.6 %collective-permute-start.1 = (f32[1,256]{1,0:T(1,128)}, f32[1,256]{1,0:T(1,128)S(1)}, u32[]{:S(2)}, u32[]{:S(2)}) collective-permute-start(f32[1,256]{1,0:T(1,128)} %get-tuple-element.8), channel_id=1, source_target_pairs={{0,2},{1,3},{2,0},{3,1},{4,6},{5,7},{6,4},{7,5},{8,10},{9,11},{10,... | collective-permute-start | bytes 3080 | tf_op jit(solution)/shard_map/ppermute | solution.py:256
  54.5 0.2 collective-permute-start
  54.7 0.0 collective-permute-done.2
  54.7 2.1 %collective-permute-done.1 = f32[1,256]{1,0:T(1,128)S(1)} collective-permute-done((f32[1,256]{1,0:T(1,128)}, f32[1,256]{1,0:T(1,128)S(1)}, u32[]{:S(2)}, u32[]{:S(2)}) %collective-permute-start.1) | collective-permute-done | bytes 1056 | tf_op jit(solution)/shard_map/ppermute | solution.py:256
  56.8 0.9 collective-permute-done
  57.7 0.6 add_rsqrt_fusion
  58.3 2.1 %multiply_convert_fusion = bf16[8,128,256]{2,1,0:T(8,128)(2,1)} fusion(f32[8,128,256]{2,1,0:T(8,128)} %get-tuple-element.7, f32[256]{0:T(256)S(1)} %bitcast.12), kind=kLoop, calls=%fused_computation.2 | loop fusion | flops 524288 | bytes 1573888 | tf_op jit(solution)/shard_map/convert_element_type | solution.py:260
  60.5 5.1 %all-to-all-start.2 = ((bf16[8,128,256]{2,1,0:T(8,128)(2,1)}), bf16[8,128,256]{2,1,0:T(8,128)(2,1)S(1)}, u32[]{:S(2)}, u32[]{:S(2)}) async-start(bf16[8,128,256]{2,1,0:T(8,128)(2,1)} %multiply_convert_fusion), calls=%async_computation.2 | async-start | bytes 1048576 | tf_op jit(solution)/shard_map/all_to_all | solution.py:261
  65.6 0.8 dynamic_slice.7
  66.3 0.1 broadcast_in_dim.41
  66.4 1.1 %broadcast_in_dim.44.gain_ref = f32[8,128,1]{2,1,0:T(8,128)} reshape(f32[8,8,16]{2,1,0:T(8,128)S(1)} %broadcast_in_dim.42) | data formatting | bytes 8192 | tf_op jit(solution)/shard_map/broadcast_in_dim | solution.py:264
  67.5 0.0 copy-done.3
  67.5 0.7 select_reduce_fusion.holder_ref
  68.3 0.7 reshape.31.base_ref
  68.9 6.4 %long_table.1.table_ref = bf16[8,8,256,256]{3,2,1,0:T(8,128)(2,1)} custom-call(f32[8,1,2304]{2,1,0:T(1,128)} %reshape.31.base_ref), custom_call_target="tpu_custom_call" | custom-call | tf_op jit(solution)/shard_map/long_table/pallas_call | solution.py:221
  75.3 3.3 %all-to-all-done.2.value_ref = bf16[8,128,256]{2,1,0:T(8,128)(2,1)S(1)} async-done(((bf16[8,128,256]{2,1,0:T(8,128)(2,1)}), bf16[8,128,256]{2,1,0:T(8,128)(2,1)S(1)}, u32[]{:S(2)}, u32[]{:S(2)}) %all-to-all-start.2) | async-done | bytes 524320 | tf_op jit(solution)/shard_map/all_to_all | solution.py:261
  78.6 0.0 copy-start.1
  78.6 0.8 copy-done.1
  79.3 8.5 %long.1 = bf16[8,128,256]{2,1,0:T(8,128)(2,1)} custom-call(s32[8]{0:T(128)} %select_reduce_fusion.holder_ref, bf16[8,128,256]{2,1,0:T(8,128)(2,1)} %copy-done.1, bf16[8,8,256,256]{3,2,1,0:T(8,128)(2,1)} %long_table.1.table_ref, f32[8,128,1]{2,1,0:T(8,128)} %broadcast_in_dim.44.gain_ref), custom_call_target="tpu_custom_call" | custom-call | tf_op jit(solution)/shard_map/long/pallas_call | solution.py:267
  87.9 17.5 %all_to_all.20.mixed_ref = bf16[8,128,256]{2,1,0:T(8,128)(2,1)} all-to-all(bf16[8,128,256]{2,1,0:T(8,128)(2,1)} %long.1), channel_id=1, replica_groups=mesh['ctx'=8,'tp'=4] {'ctx'}, dimensions={0} | all-to-all | bytes 1048576 | tf_op jit(solution)/shard_map/all_to_all | solution.py:289
  105.4 5.3 %gate.1 = bf16[256,1024]{1,0:T(8,128)(2,1)} custom-call(bf16[8,128,256]{2,1,0:T(8,128)(2,1)} %all_to_all.20.mixed_ref, bf16[256,1024]{1,0:T(8,128)(2,1)} %gate_ref.3), custom_call_target="tpu_custom_call" | custom-call | tf_op jit(solution)/shard_map/gate/pallas_call | solution.py:291
  (6 shorter events, 0.1 us)
Async XLA Ops:
  0.0 17.8 %copy-start = (s32[8]{0:T(128)S(1)}, s32[8]{0:T(128)}, u32[]{:S(2)}) copy-start(s32[8]{0:T(128)} %param.21) | copy-start | bytes 100
  9.9 18.3 %all-to-all-start = ((bf16[8,176,128]{2,1,0:T(8,128)(2,1)}), bf16[8,176,128]{2,1,0:T(8,128)(2,1)S(1)}, u32[]{:S(2)}, u32[]{:S(2)}) async-start(bf16[8,176,128]{2,1,0:T(8,128)(2,1)} %pad_maximum_fusion), calls=%async_computation | async-start | bytes 720896 | tf_op jit(solution)/shard_map/all_to_all | solution.py:196
  17.8 49.7 %copy-start.3 = (s32[8]{0:T(128)S(1)}, s32[8]{0:T(128)}, u32[]{:S(2)}) copy-start(s32[8]{0:T(128)} %param.20) | copy-start | bytes 100
  29.5 13.4 %all-to-all-start.1 = ((bf16[8,160,128]{2,1,0:T(8,128)(2,1)}), bf16[8,160,128]{2,1,0:T(8,128)(2,1)S(1)}, u32[]{:S(2)}, u32[]{:S(2)}) async-start(bf16[8,160,128]{2,1,0:T(8,128)(2,1)} %gather_fusion.1), calls=%async_computation.1 | async-start | bytes 655360 | tf_op jit(solution)/shard_map/all_to_all | solution.py:198
  42.9 0.7 copy-start.2
  52.9 1.7 %collective-permute-start.2 = (f32[1,256]{1,0:T(1,128)}, f32[1,256]{1,0:T(1,128)S(1)}, u32[]{:S(2)}, u32[]{:S(2)}) collective-permute-start(f32[1,256]{1,0:T(1,128)} %get-tuple-element.8), channel_id=1, source_target_pairs={{0,3},{1,0},{2,1},{3,2},{4,7},{5,4},{6,5},{7,6},{8,11},{9,8},{10,9... | collective-permute-start | bytes 3080 | tf_op jit(solution)/shard_map/ppermute | solution.py:256
  52.9 3.8 %collective-permute-start.1 = (f32[1,256]{1,0:T(1,128)}, f32[1,256]{1,0:T(1,128)S(1)}, u32[]{:S(2)}, u32[]{:S(2)}) collective-permute-start(f32[1,256]{1,0:T(1,128)} %get-tuple-element.8), channel_id=1, source_target_pairs={{0,2},{1,3},{2,0},{3,1},{4,6},{5,7},{6,4},{7,5},{8,10},{9,11},{10,... | collective-permute-start | bytes 3080 | tf_op jit(solution)/shard_map/ppermute | solution.py:256
  54.5 3.2 %collective-permute-start = (f32[1,256]{1,0:T(1,128)}, f32[1,256]{1,0:T(1,128)S(1)}, u32[]{:S(2)}, u32[]{:S(2)}) collective-permute-start(f32[1,256]{1,0:T(1,128)} %get-tuple-element.8), channel_id=1, source_target_pairs={{0,1},{1,2},{2,3},{3,0},{4,5},{5,6},{6,7},{7,4},{8,9},{9,10},{10,1... | collective-permute-start | bytes 3080 | tf_op jit(solution)/shard_map/ppermute | solution.py:256
  60.5 18.1 %all-to-all-start.2 = ((bf16[8,128,256]{2,1,0:T(8,128)(2,1)}), bf16[8,128,256]{2,1,0:T(8,128)(2,1)S(1)}, u32[]{:S(2)}, u32[]{:S(2)}) async-start(bf16[8,128,256]{2,1,0:T(8,128)(2,1)} %multiply_convert_fusion), calls=%async_computation.2 | async-start | bytes 1048576 | tf_op jit(solution)/shard_map/all_to_all | solution.py:261
  78.6 0.8 copy-start.1

commit v2 on v1

v2 whole, which is shorter than its diff:
```python
import jax
import jax.numpy as jnp
from jax import lax
from jax.experimental import pallas as pl
from jax.experimental.pallas import tpu as pltpu
from jax.sharding import PartitionSpec as P

EPSILON = 1e-06
LANES = 128
EDGE = 8
VMEM_BYTES = 24 * 1024 * 1024
TAIL_TILES = 4
MIX_TILES = 2
GATE_TILES = 4
F32 = jnp.float32
BF16 = jnp.bfloat16


def params(*semantics):
    return pltpu.CompilerParams(dimension_semantics=semantics, vmem_limit_bytes=VMEM_BYTES)


def lane_taps(taps_ref, which, size, width):
    groups = taps_ref.shape[2]
    group = lax.broadcasted_iota(jnp.int32, (groups, width), 0)
    lane = lax.broadcasted_iota(jnp.int32, (groups, width), 1) + pl.program_id(0) * width
    spread = (group == lane // size).astype(BF16)
    return jnp.dot(taps_ref[which], spread, preferred_element_type=F32)


def short_filter(extended, taps, start, rows):
    total = extended[start : start + rows] * taps[0:1]
    for j in range(1, taps.shape[0]):
        total = total + extended[start - j : start - j + rows] * taps[j : j + 1]
    return total


def tail_kernel(size, reach, q_ref, k_ref, v_ref, taps_ref, *rest):
    out_ref = rest[-1]
    rows, width = q_ref.shape
    first = rows - reach - 16
    k_part = k_ref[first:, :].astype(F32)
    v_part = v_ref[first:, :].astype(F32)
    q_part = q_ref[rows - 16 :, :].astype(F32)
    k_feat = short_filter(k_part, lane_taps(taps_ref, 1, size, width), 16, reach)
    v_feat = short_filter(v_part, lane_taps(taps_ref, 2, size, width), 16, reach)
    z_tail = (k_feat * v_feat).astype(BF16)
    edges = jnp.concatenate(
        [q_part[16 - EDGE :], k_part[-EDGE:], v_part[-EDGE:], jnp.zeros((EDGE, width), F32)], axis=0
    ).astype(BF16)
    for t in range(width // LANES):
        lanes = slice(t * LANES, (t + 1) * LANES)
        out_ref[t, :reach, :] = z_tail[:, lanes]
        out_ref[t, reach : reach + 4 * EDGE, :] = edges[:, lanes]
        if len(rest) == 2:
            out_ref[t, reach + 4 * EDGE :, :] = rest[0][t]


def call_tails(q_one, k_one, v_one, short_taps, reach, extra):
    rows, width = q_one.shape
    tiles = width // LANES
    size = width // short_taps.shape[2]
    wide = TAIL_TILES * LANES
    column = pl.BlockSpec((rows, wide), lambda i: (0, i))
    inputs = [q_one, k_one, v_one, short_taps]
    in_specs = [column, column, column, pl.BlockSpec(short_taps.shape, lambda i: (0, 0, 0))]
    out_rows = reach + 4 * EDGE
    if extra is not None:
        inputs.append(extra)
        in_specs.append(pl.BlockSpec((TAIL_TILES,) + extra.shape[1:], lambda i: (i, 0, 0)))
        out_rows += extra.shape[1]

    def kernel(*refs):
        tail_kernel(size, reach, *refs)

    return pl.pallas_call(
        kernel,
        grid=(tiles // TAIL_TILES,),
        in_specs=in_specs,
        out_specs=pl.BlockSpec((TAIL_TILES, out_rows, LANES), lambda i: (i, 0, 0)),
        out_shape=jax.ShapeDtypeStruct((tiles, out_rows, LANES), BF16),
        compiler_params=params("arbitrary"),
        name="tails",
    )(*inputs)


def route_kernel(order_ref, owner_ref, spread_ref, out_ref):
    kept = out_ref.shape[1]
    for d in range(out_ref.shape[0]):
        out_ref[d] = spread_ref[owner_ref[order_ref[d]], :kept, :]


def call_route(block_order, prev_owner, spread, kept):
    count, _, lanes = spread.shape
    return pl.pallas_call(
        route_kernel,
        in_specs=[
            pl.BlockSpec(memory_space=pltpu.SMEM),
            pl.BlockSpec(memory_space=pltpu.SMEM),
            pl.BlockSpec(memory_space=pltpu.VMEM),
        ],
        out_specs=pl.BlockSpec(memory_space=pltpu.VMEM),
        out_shape=jax.ShapeDtypeStruct((count, kept, lanes), BF16),
        compiler_params=params(),
        name="route",
    )(block_order, prev_owner, spread)


def medium_table_kernel(base_ref, out_ref):
    reach, wide = out_ref.shape[2], base_ref.shape[2]
    for g in range(base_ref.shape[1]):
        row = jnp.broadcast_to(base_ref[0, g : g + 1, :], (reach, wide))
        out_ref[0, g] = pltpu.roll(row, 0, 1, stride=1, stride_axis=0).astype(BF16)


def call_medium_table(medium_taps, tile_groups, rows):
    reach, groups = medium_taps.shape
    tiles = groups // tile_groups
    base = jnp.pad(jnp.transpose(medium_taps[::-1]), ((0, 0), (1, rows - reach - 1)))
    return pl.pallas_call(
        medium_table_kernel,
        grid=(tiles,),
        in_specs=[pl.BlockSpec((1, tile_groups, rows), lambda i: (i, 0, 0))],
        out_specs=pl.BlockSpec((1, tile_groups, reach, rows), lambda i: (i, 0, 0, 0)),
        out_shape=jax.ShapeDtypeStruct((tiles, tile_groups, reach, rows), BF16),
        compiler_params=params("arbitrary"),
        name="medium_table",
    )(base.astype(F32).reshape(tiles, tile_groups, rows))


def long_table_kernel(base_ref, out_ref):
    lags, rows, _ = out_ref.shape[1:]
    strip = jnp.broadcast_to(base_ref[0], (rows, base_ref.shape[2]))
    strip = pltpu.roll(strip, 0, 1, stride=1, stride_axis=0)
    for lag in range(lags):
        out_ref[0, lag] = strip[:, (lag + 1) * rows : (lag + 2) * rows].astype(BF16)


def call_long_table(long_rows, rows, lags):
    groups, length = long_rows.shape
    pieces = length // (lags * rows)
    padded = jnp.pad(long_rows.astype(F32), ((0, 0), (rows, 0)))
    windows = jnp.stack(
        [padded[:, p * lags * rows : (p * lags + lags + 1) * rows] for p in range(pieces)], axis=1
    ).reshape(groups * pieces, 1, (lags + 1) * rows)
    return pl.pallas_call(
        long_table_kernel,
        grid=(groups * pieces,),
        in_specs=[pl.BlockSpec((1, 1, (lags + 1) * rows), lambda i: (i, 0, 0))],
        out_specs=pl.BlockSpec((1, lags, rows, rows), lambda i: (i, 0, 0, 0)),
        out_shape=jax.ShapeDtypeStruct((groups * pieces, lags, rows, rows), BF16),
        compiler_params=params("arbitrary"),
        name="long_table",
    )(windows)


def mix_kernel(
    size, first_ref, q_ref, k_ref, v_ref, gate_ref, halo_ref, taps_ref, table_ref, out_ref, energy_ref, squares_ref
):
    rows, width = q_ref.shape
    tiles, groups, reach, wide = table_ref.shape
    step = pl.program_id(0)
    keep = jnp.where(first_ref[0] != 0, 0.0, 1.0)
    taps = [lane_taps(taps_ref, which, size, width) for which in range(3)]
    lane_group = lax.broadcasted_iota(jnp.int32, (1, 2 * LANES), 1) % LANES // size
    squares = jnp.zeros((rows, LANES), F32)
    for t in range(tiles):
        lanes = slice(t * LANES, (t + 1) * LANES)
        edges = halo_ref[t, reach:, :].astype(F32) * keep

        def feature(ref, which):
            extended = jnp.concatenate(
                [edges[which * EDGE : (which + 1) * EDGE], ref[:, lanes].astype(F32)], axis=0
            )
            return short_filter(extended, taps[which][:, lanes], EDGE, rows)

        q_feat = feature(q_ref, 0)
        z_own = (feature(k_ref, 1) * feature(v_ref, 2)).astype(BF16)
        z_halo = (halo_ref[t, :reach, :].astype(F32) * keep).astype(BF16)
        window = jnp.concatenate([jnp.concatenate([z_halo, z_own[:reach]], axis=0), z_own], axis=1)
        every = jnp.dot(
            table_ref[t].reshape(groups * reach, wide), window, preferred_element_type=F32
        )
        medium = every[:reach]
        for g in range(1, groups):
            medium = jnp.where(lane_group == g, every[g * reach : (g + 1) * reach], medium)
        mixed = q_feat * jnp.concatenate([medium[:, :LANES], medium[:, LANES:]], axis=0)
        out_ref[t] = jnp.transpose(mixed * gate_ref[:, lanes].astype(F32))
        squares = squares + mixed * mixed

    @pl.when(step == 0)
    def _():
        squares_ref[...] = squares

    @pl.when(step != 0)
    def _():
        squares_ref[...] += squares

    @pl.when(step == pl.num_programs(0) - 1)
    def _():
        energy_ref[...] = jnp.sum(jnp.transpose(squares_ref[...]), axis=0, keepdims=True)


def call_mix(is_first, q_one, k_one, v_one, k_two, halo, short_taps, medium_table):
    rows, width = q_one.shape
    size = width // short_taps.shape[2]
    wide = MIX_TILES * LANES
    column = pl.BlockSpec((rows, wide), lambda i: (0, i))

    def kernel(*refs):
        mix_kernel(size, *refs)

    return pl.pallas_call(
        kernel,
        grid=(width // wide,),
        in_specs=[
            pl.BlockSpec(memory_space=pltpu.SMEM),
            column,
            column,
            column,
            column,
            pl.BlockSpec((MIX_TILES,) + halo.shape[1:], lambda i: (i, 0, 0)),
            pl.BlockSpec(short_taps.shape, lambda i: (0, 0, 0)),
            pl.BlockSpec((MIX_TILES,) + medium_table.shape[1:], lambda i: (i, 0, 0, 0)),
        ],
        out_specs=[
            pl.BlockSpec((MIX_TILES, LANES, rows), lambda i: (i, 0, 0)),
            pl.BlockSpec((1, rows), lambda i: (0, 0)),
        ],
        out_shape=[
            jax.ShapeDtypeStruct((width // LANES, LANES, rows), F32),
            jax.ShapeDtypeStruct((1, rows), F32),
        ],
        scratch_shapes=[pltpu.VMEM((rows, LANES), F32)],
        compiler_params=params("arbitrary"),
        name="mix",
    )(is_first, q_one, k_one, v_one, k_two, halo, short_taps, medium_table)


def long_kernel(holder_ref, value_ref, table_ref, gain_ref, out_ref, ordered_ref, total_ref):
    blocks, size, rows = value_ref.shape
    lags = table_ref.shape[1]
    piece = pl.program_id(1)
    reach = blocks * size

    @pl.when(piece == 0)
    def _():
        ordered_ref[:reach] = jnp.zeros((reach, rows), BF16)
        for b in range(blocks):
            ordered_ref[reach + b * size : reach + (b + 1) * size] = value_ref[holder_ref[b]]
        total_ref[...] = ordered_ref[reach:].astype(F32) * gain_ref[0]

    def lagged(lag):
        if lags == blocks:
            return ordered_ref[(blocks - lag) * size : (2 * blocks - lag) * size]
        start = pl.multiple_of((blocks - piece * lags - lag) * size, size)
        return ordered_ref[pl.ds(start, reach)]

    left = jnp.concatenate([lagged(lag) for lag in range(lags)], axis=1)
    right = table_ref[0].reshape(lags * rows, rows)
    total_ref[...] += jnp.dot(left, right, preferred_element_type=F32)

    @pl.when(piece == pl.num_programs(1) - 1)
    def _():
        for b in range(blocks):
            out_ref[holder_ref[b]] = total_ref[b * size : (b + 1) * size].astype(BF16)


def call_long(holder, values, long_table, gain, size):
    blocks, channels, rows = values.shape
    lags = long_table.shape[1]
    groups = channels // size
    pieces = blocks // lags
    group_spec = pl.BlockSpec((blocks, size, rows), lambda g, p, order: (0, g, 0))
    return pl.pallas_call(
        long_kernel,
        grid_spec=pltpu.PrefetchScalarGridSpec(
            num_scalar_prefetch=1,
            grid=(groups, pieces),
            in_specs=[
                group_spec,
                pl.BlockSpec(
                    (1, lags, rows, rows), lambda g, p, order: (g * pieces + p, 0, 0, 0)
                ),
                pl.BlockSpec((1, blocks * size, 1), lambda g, p, order: (g, 0, 0)),
            ],
            out_specs=group_spec,
            scratch_shapes=[
                pltpu.VMEM((2 * blocks * size, rows), BF16),
                pltpu.VMEM((blocks * size, rows), F32),
            ],
        ),
        out_shape=jax.ShapeDtypeStruct((blocks, channels, rows), BF16),
        compiler_params=params("arbitrary", "arbitrary"),
        name="long",
    )(holder, values, long_table, gain)


def gate_kernel(mixed_ref, gate_ref, out_ref):
    for t in range(mixed_ref.shape[0]):
        lanes = slice(t * LANES, (t + 1) * LANES)
        mixed = jnp.transpose(mixed_ref[t]).astype(F32)
        out_ref[:, lanes] = (gate_ref[:, lanes].astype(F32) * mixed).astype(BF16)


def call_gate(mixed, q_two):
    rows, width = q_two.shape
    wide = GATE_TILES * LANES
    column = pl.BlockSpec((rows, wide), lambda i: (0, i))
    return pl.pallas_call(
        gate_kernel,
        grid=(width // wide,),
        in_specs=[pl.BlockSpec((GATE_TILES, LANES, rows), lambda i: (i, 0, 0)), column],
        out_specs=column,
        out_shape=jax.ShapeDtypeStruct((rows, width), BF16),
        compiler_params=params("arbitrary"),
        name="gate",
    )(mixed, q_two)


def exchange(array):
    return lax.all_to_all(array, "ctx", split_axis=0, concat_axis=0, tiled=True)


def per_device(
    q_one,
    k_one,
    v_one,
    q_two,
    k_two,
    short_taps,
    medium_taps,
    long_taps,
    skip_gain,
    block_order,
    prev_owner,
):
    rows, width = q_one.shape
    ctx_count = lax.axis_size("ctx")
    tp_count = lax.axis_size("tp")
    me = lax.axis_index("ctx")
    size = width // short_taps.shape[2]
    reach = medium_taps.shape[0]
    assert rows == 2 * reach and short_taps.shape[1] <= EDGE + 1
    tiles = width // LANES
    shard = width // ctx_count
    shard_groups = shard // size
    full_width = width * tp_count

    slots = jnp.arange(ctx_count, dtype=jnp.int32)
    holder = jnp.sum(jnp.where(block_order[None, :] == slots[:, None], slots[None, :], 0), axis=1)
    is_first = (lax.dynamic_slice_in_dim(block_order, me, 1) == 0).astype(jnp.int32)

    tail_rows = reach + 4 * EDGE
    halo_rows = tiles * tail_rows // ctx_count
    taps_sent = long_taps.reshape(ctx_count, shard_groups * rows // LANES, LANES)
    if ctx_count == tiles:
        payload = call_tails(q_one, k_one, v_one, short_taps, reach, taps_sent)
    else:
        tails = call_tails(q_one, k_one, v_one, short_taps, reach, None)
        payload = jnp.concatenate([tails.reshape(ctx_count, halo_rows, LANES), taps_sent], axis=1)
    spread = exchange(payload)
    halo = exchange(call_route(block_order, prev_owner, spread, halo_rows))
    halo = halo.reshape(tiles, tail_rows, LANES)

    medium_table = call_medium_table(medium_taps, LANES // size, rows)
    long_rows = jnp.transpose(
        spread[:, halo_rows:].reshape(ctx_count, shard_groups, rows), (1, 0, 2)
    ).reshape(shard_groups, ctx_count * rows)
    long_table = call_long_table(long_rows, rows, min(ctx_count, 8))

    gated, energy = call_mix(is_first, q_one, k_one, v_one, k_two, halo, short_taps, medium_table)
    total = energy
    for step in range(1, tp_count):
        total = total + lax.ppermute(
            energy, "tp", [(i, (i + step) % tp_count) for i in range(tp_count)]
        )
    scale = lax.rsqrt(total / full_width + EPSILON)
    values = (gated * scale[None]).astype(BF16).reshape(ctx_count, shard, rows)
    values = exchange(values)

    gain = lax.dynamic_slice_in_dim(skip_gain, me * shard, shard).reshape(shard_groups, 1, size, 1)
    gain = jnp.broadcast_to(gain, (shard_groups, ctx_count, size, 1))
    gain = gain.reshape(shard_groups, ctx_count * size, 1)
    returned = exchange(call_long(holder, values, long_table, gain, size))
    return call_gate(returned.reshape(tiles, LANES, rows), q_two)


def solution(mesh):
    in_specs = (
        P("ctx", "tp"),
        P("ctx", "tp"),
        P("ctx", "tp"),
        P("ctx", "tp"),
        P("ctx", "tp"),
        P(None, None, "tp"),
        P(None, "tp"),
        P("tp", "ctx"),
        P("tp"),
        P(),
        P(),
    )
    out_specs = P("ctx", "tp")
    return jax.shard_map(
        per_device, mesh=mesh, in_specs=in_specs, out_specs=out_specs, check_vma=False
    )
```

time: 113 us -> 97 us (0.86); the launches traced: 111 us -> 96.2 us
  Pallas kernels: 40.4 us -> 16.8 us
  blocking collectives: 17.5 us -> 35.8 us
  local copies, waits for them, and re-layouts: 11 us -> 20 us
  starting transfers between devices: 17.7 us -> 8.88 us
  other arithmetic: 6.55 us -> 1.09 us
  waiting for transfers between devices: 16.9 us -> 12.9 us
    pallas_call x6 -> x7, Pallas kernels: 40.4 us -> 16.8 us  [the longest x1 5.41 us: call_mix(): pl.pallas_call(kernel, grid=(width // wide,), in_specs=[pl.BlockSpec(memo...]
    all_to_all x1 -> x2, blocking collectives: 17.5 us -> 35.8 us  [exchange(): return lax.all_to_all(array, 'ctx', split_axis=0, concat_axis=0, tiled=True)]
    unnamed x8 -> x34, local copies, waits for them, and re-layouts: 1.52 us -> 15.9 us
    all_to_all x3 -> x2, starting transfers between devices: 16 us -> 7.07 us  [exchange(): return lax.all_to_all(array, 'ctx', split_axis=0, concat_axis=0, tiled=True)]
    all_to_all x3 -> x2, waiting for transfers between devices: 13.9 us -> 10.1 us  [exchange(): return lax.all_to_all(array, 'ctx', split_axis=0, concat_axis=0, tiled=True)]
    gather x2 -> x0, local copies, waits for them, and re-layouts: 1.96 us -> none  [the longest x1 1.31 us: per_device(): routed = jnp.take(spread[:, :halo_rows], source, axis=0, mode='clip')]
    concatenate x1 -> x0, other arithmetic: 1.73 us -> none  [per_device(): jnp.concatenate([tails.reshape(ctx_count, halo_rows, LANES), long_taps.re...]
    convert_element_type x1, other arithmetic: 2.11 us -> 0.88 us  [per_device(): values = (gated * scale[None]).astype(BF16).reshape(ctx_count, shard, rows)]
  transfers between devices with their start and end apart: 6 -> 5, of which waited for: 5 -> 4; matrix products, arithmetic and copies ran while one was open for 7% -> 4% of each run, Pallas kernels for 11% -> 4%
where the time goes in v2:
time: 97 us; the launch traced here: 96.2 us
  blocking collectives  35.8 us (37%)
  local copies, waits for them, and re-layouts  20 us (21%)
  Pallas kernels  16.8 us (17%)
  waiting for transfers between devices  12.9 us (13%)
  starting transfers between devices  8.88 us (9%)
  other arithmetic  1.09 us (1%)
    all_to_all x2, blocking collectives, exchange(): return lax.all_to_all(array, 'ctx', split_axis=0, concat_axis=0, tiled=True)  35.8 us
    unnamed x34, local copies, waits for them, and re-layouts  15.9 us
    all_to_all x2, waiting for transfers between devices, exchange(): return lax.all_to_all(array, 'ctx', split_axis=0, concat_axis=0, tiled=True)  10.1 us
    all_to_all x2, starting transfers between devices, exchange(): return lax.all_to_all(array, 'ctx', split_axis=0, concat_axis=0, tiled=True)  7.07 us
    pallas_call x1, Pallas kernels, call_mix(): pl.pallas_call(kernel, grid=(width // wide,), in_specs=[pl.BlockSpec(memo...  5.41 us
    pallas_call x1, Pallas kernels, call_long(): pl.pallas_call(long_kernel, grid_spec=pltpu.PrefetchScalarGridSpec(num_sc...  3.3 us
    ppermute x3, waiting for transfers between devices, per_device(): lax.ppermute(energy, 'tp', [(i, (i + step) % tp_count) for i in range(tp_...  2.83 us
    pallas_call x1, Pallas kernels, call_tails(): pl.pallas_call(kernel, grid=(tiles // TAIL_TILES,), in_specs=in_specs, ou...  2.02 us
  transfers between devices with their start and end apart: 5, of which 4 were waited for; matrix products, arithmetic and copies ran while one was open for 4% of the time, Pallas kernels for 4%

profile of v2, /device:TPU:0, one launch (start us, length us, event | category | flops | bytes accessed | tf_op | source)
XLA Modules:
  0.0 96.2 jit_solution(17246350492887169958)
XLA Ops:
  0.0 0.0 copy-start.13
  0.0 0.8 reshape.24.refs_4_
  0.8 0.0 copy-start.4
  0.8 1.0 %copy-done.4 = bf16[256,1024]{1,0:T(8,128)(2,1)S(1)} copy-done((bf16[256,1024]{1,0:T(8,128)(2,1)S(1)}, bf16[256,1024]{1,0:T(8,128)(2,1)}, u32[]{:S(2)}) %copy-start.4) | copy-done | bytes 524312
  1.8 0.0 copy-start.6
  1.8 1.0 %copy-done.6 = bf16[256,1024]{1,0:T(8,128)(2,1)S(1)} copy-done((bf16[256,1024]{1,0:T(8,128)(2,1)S(1)}, bf16[256,1024]{1,0:T(8,128)(2,1)}, u32[]{:S(2)}) %copy-start.6) | copy-done | bytes 524312
  2.9 0.0 copy-start.8
  2.9 1.0 %copy-done.8 = bf16[256,1024]{1,0:T(8,128)(2,1)S(1)} copy-done((bf16[256,1024]{1,0:T(8,128)(2,1)S(1)}, bf16[256,1024]{1,0:T(8,128)(2,1)}, u32[]{:S(2)}) %copy-start.8) | copy-done | bytes 524312
  3.9 0.0 copy-start.12
  3.9 0.7 copy-done.12
  4.6 0.0 copy-start.5
  4.6 0.0 copy-start.7
  4.6 0.0 copy-start.9
  4.6 0.0 copy-start.11
  4.6 2.0 %tails.1 = bf16[8,176,128]{2,1,0:T(8,128)(2,1)S(1)} custom-call(bf16[256,1024]{1,0:T(8,128)(2,1)S(1)} %copy-done.4, bf16[256,1024]{1,0:T(8,128)(2,1)S(1)} %copy-done.6, bf16[256,1024]{1,0:T(8,128)(2,1)S(1)} %copy-done.8, bf16[3,7,64]{2,1,0:T(8,128)(2,1)S(1)} %copy-done.12, bf16[8,16,128]{2,1,0:T(8,128)(2,1)S(1)} %reshape.24.refs_4_), custom_call_target="tpu_custom_call" | custom-call | tf_op jit(solution)/shard_map/tails/pallas_call | solution.py:76
  6.7 0.0 copy-start.16
  6.7 18.6 %all_to_all.20.spread_ref = bf16[8,176,128]{2,1,0:T(8,128)(2,1)S(1)} all-to-all(bf16[8,176,128]{2,1,0:T(8,128)(2,1)S(1)} %tails.1), channel_id=1, replica_groups=mesh['ctx'=8,'tp'=4] {'ctx'}, dimensions={0} | all-to-all | bytes 720896 | tf_op jit(solution)/shard_map/all_to_all | solution.py:322
  25.2 0.0 copy-start.14
  25.2 0.7 copy-done.14
  25.9 0.0 copy-start.15
  25.9 0.7 copy-done.15
  26.5 1.3 %route.1 = bf16[8,160,128]{2,1,0:T(8,128)(2,1)} custom-call(s32[8]{0:T(128)S(1)} %copy-done.15, s32[8]{0:T(128)S(1)} %copy-done.14, bf16[8,176,128]{2,1,0:T(8,128)(2,1)S(1)} %all_to_all.20.spread_ref), custom_call_target="tpu_custom_call" | custom-call | tf_op jit(solution)/shard_map/route/pallas_call | solution.py:95
  27.8 3.4 %all-to-all-start.1 = ((bf16[8,160,128]{2,1,0:T(8,128)(2,1)}), bf16[8,160,128]{2,1,0:T(8,128)(2,1)S(1)}, u32[]{:S(2)}, u32[]{:S(2)}) async-start(bf16[8,160,128]{2,1,0:T(8,128)(2,1)} %route.1), calls=%async_computation.1 | async-start | bytes 655360 | tf_op jit(solution)/shard_map/all_to_all | solution.py:322
  31.3 1.3 %dynamic_slice.6 = s32[1]{0:T(128)} dynamic-slice(s32[8]{0:T(128)} %order_ref.1, s32[]{:T(128)S(6)} %select_n.11), dynamic_slice_sizes={1} | dynamic-slice | bytes 12 | tf_op jit(solution)/shard_map/dynamic_slice | solution.py:352
  33.2 0.8 rev.3
  34.0 0.1 bitcast_convert_fusion.base_ref
  34.1 1.7 %medium_table.1.refs_7_ = bf16[8,8,128,256]{3,2,1,0:T(8,128)(2,1)S(1)} custom-call(f32[8,8,256]{2,1,0:T(8,128)S(1)} %bitcast_convert_fusion.base_ref), custom_call_target="tpu_custom_call" | custom-call | tf_op jit(solution)/shard_map/medium_table/pallas_call | solution.py:120
  35.8 0.0 copy-start.2
  35.8 1.9 %copy-done.2 = bf16[8,8,128,256]{3,2,1,0:T(8,128)(2,1)} copy-done((bf16[8,8,128,256]{3,2,1,0:T(8,128)(2,1)}, bf16[8,8,128,256]{3,2,1,0:T(8,128)(2,1)S(1)}, u32[]{:S(2)}) %copy-start.2) | copy-done | bytes 4194328
  37.7 3.3 %all-to-all-done.1.refs_5_ = bf16[8,160,128]{2,1,0:T(8,128)(2,1)S(1)} async-done(((bf16[8,160,128]{2,1,0:T(8,128)(2,1)}), bf16[8,160,128]{2,1,0:T(8,128)(2,1)S(1)}, u32[]{:S(2)}, u32[]{:S(2)}) %all-to-all-start.1) | async-done | bytes 327712 | tf_op jit(solution)/shard_map/all_to_all | solution.py:322
  41.0 0.0 copy-done.13
  41.0 0.0 copy-done.5
  41.0 0.0 copy-done.7
  41.0 0.0 copy-done.9
  41.1 0.0 copy-done.11
  41.1 0.0 copy-start.3
  41.1 2.2 %copy-done.3 = bf16[8,8,128,256]{3,2,1,0:T(8,128)(2,1)S(1)} copy-done((bf16[8,8,128,256]{3,2,1,0:T(8,128)(2,1)S(1)}, bf16[8,8,128,256]{3,2,1,0:T(8,128)(2,1)}, u32[]{:S(2)}) %copy-start.3) | copy-done | bytes 4194328
  43.3 5.4 %mix.1 = (f32[8,128,256]{2,1,0:T(8,128)S(1)}, f32[1,256]{1,0:T(1,128)S(1)}) custom-call(s32[1]{0:T(128)S(6)} %convert_element_type.21.refs_0_, bf16[256,1024]{1,0:T(8,128)(2,1)S(1)} %copy-done.5, bf16[256,1024]{1,0:T(8,128)(2,1)S(1)} %copy-done.7, bf16[256,1024]{1,0:T(8,128)(2,1)S(1)} %copy-done.9, bf16[256,1024]{1,0:T(8,128)(2,1)S(1)} %copy-done.11, ...), custom_call_target="tpu_custom_call" | custom-call | tf_op jit(solution)/shard_map/mix/pallas_call | solution.py:213
  48.7 0.1 collective-permute-start.2
  48.7 1.6 %collective-permute-start.1 = (f32[1,256]{1,0:T(1,128)S(1)}, f32[1,256]{1,0:T(1,128)S(1)}, u32[]{:S(2)}, u32[]{:S(2)}) collective-permute-start(f32[1,256]{1,0:T(1,128)S(1)} %get-tuple-element.8), channel_id=1, source_target_pairs={{0,2},{1,3},{2,0},{3,1},{4,6},{5,7},{6,4},{7,5},{8,10},{9,11},{10,... | collective-permute-start | bytes 3080 | tf_op jit(solution)/shard_map/ppermute | solution.py:375
  50.3 0.2 collective-permute-start
  50.5 0.0 collective-permute-done.2
  50.5 1.9 %collective-permute-done.1 = f32[1,256]{1,0:T(1,128)S(1)} collective-permute-done((f32[1,256]{1,0:T(1,128)S(1)}, f32[1,256]{1,0:T(1,128)S(1)}, u32[]{:S(2)}, u32[]{:S(2)}) %collective-permute-start.1) | collective-permute-done | bytes 1056 | tf_op jit(solution)/shard_map/ppermute | solution.py:375
  52.4 0.9 collective-permute-done
  53.3 0.9 multiply_convert_fusion
  54.2 3.6 %all-to-all-start.2 = ((bf16[8,128,256]{2,1,0:T(8,128)(2,1)}), bf16[8,128,256]{2,1,0:T(8,128)(2,1)S(1)}, u32[]{:S(2)}, u32[]{:S(2)}) async-start(bf16[8,128,256]{2,1,0:T(8,128)(2,1)} %multiply_convert_fusion), calls=%async_computation.2 | async-start | bytes 1048576 | tf_op jit(solution)/shard_map/all_to_all | solution.py:322
  57.8 0.8 dynamic_slice.7
  58.6 0.1 broadcast_in_dim.27
  58.7 0.3 broadcast_in_dim.30.gain_ref
  59.0 0.0 copy-done.16
  59.0 0.1 select_reduce_fusion.holder_ref
  59.2 0.1 reshape.29.base_ref
  59.2 0.0 copy-start.10
  59.2 2.0 %long_table.1.table_ref = bf16[8,8,256,256]{3,2,1,0:T(8,128)(2,1)S(1)} custom-call(f32[8,1,2304]{2,1,0:T(1,128)S(1)} %reshape.29.base_ref), custom_call_target="tpu_custom_call" | custom-call | tf_op jit(solution)/shard_map/long_table/pallas_call | solution.py:146
  61.3 0.0 copy-start
  61.3 3.2 %copy-done = bf16[8,8,256,256]{3,2,1,0:T(8,128)(2,1)} copy-done((bf16[8,8,256,256]{3,2,1,0:T(8,128)(2,1)}, bf16[8,8,256,256]{3,2,1,0:T(8,128)(2,1)S(1)}, u32[]{:S(2)}) %copy-start) | copy-done | bytes 8388632
  64.5 6.8 %all-to-all-done.2.value_ref = bf16[8,128,256]{2,1,0:T(8,128)(2,1)S(1)} async-done(((bf16[8,128,256]{2,1,0:T(8,128)(2,1)}), bf16[8,128,256]{2,1,0:T(8,128)(2,1)S(1)}, u32[]{:S(2)}, u32[]{:S(2)}) %all-to-all-start.2) | async-done | bytes 524320 | tf_op jit(solution)/shard_map/all_to_all | solution.py:322
  71.3 0.0 copy-start.1
  71.3 3.4 %copy-done.1 = bf16[8,8,256,256]{3,2,1,0:T(8,128)(2,1)S(1)} copy-done((bf16[8,8,256,256]{3,2,1,0:T(8,128)(2,1)S(1)}, bf16[8,8,256,256]{3,2,1,0:T(8,128)(2,1)}, u32[]{:S(2)}) %copy-start.1) | copy-done | bytes 8388632
  74.7 3.3 %long.1 = bf16[8,128,256]{2,1,0:T(8,128)(2,1)S(1)} custom-call(s32[8]{0:T(128)S(1)} %select_reduce_fusion.holder_ref, bf16[8,128,256]{2,1,0:T(8,128)(2,1)S(1)} %all-to-all-done.2.value_ref, bf16[8,8,256,256]{3,2,1,0:T(8,128)(2,1)S(1)} %copy-done.1, f32[8,128,1]{2,1,0:T(8,128)S(1)} %broadcast_in_dim.30.gain_ref), custom_call_target="tpu_custom_call" | custom-call | tf_op jit(solution)/shard_map/long/pallas_call | solution.py:275
  78.0 17.2 %all_to_all.21.mixed_ref = bf16[8,128,256]{2,1,0:T(8,128)(2,1)S(1)} all-to-all(bf16[8,128,256]{2,1,0:T(8,128)(2,1)S(1)} %long.1), channel_id=1, replica_groups=mesh['ctx'=8,'tp'=4] {'ctx'}, dimensions={0} | all-to-all | bytes 1048576 | tf_op jit(solution)/shard_map/all_to_all | solution.py:322
  95.2 0.0 copy-done.10
  95.2 1.0 %gate.1 = bf16[256,1024]{1,0:T(8,128)(2,1)} custom-call(bf16[8,128,256]{2,1,0:T(8,128)(2,1)S(1)} %all_to_all.21.mixed_ref, bf16[256,1024]{1,0:T(8,128)(2,1)S(1)} %copy-done.10), custom_call_target="tpu_custom_call" | custom-call | tf_op jit(solution)/shard_map/gate/pallas_call | solution.py:310
  (5 shorter events, 0.0 us)
Async XLA Ops:
  0.0 41.0 %copy-start.13 = (bf16[3,7,64]{2,1,0:T(8,128)(2,1)S(1)}, bf16[3,7,64]{2,1,0:T(8,128)(2,1)}, u32[]{:S(2)}) copy-start(bf16[3,7,64]{2,1,0:T(8,128)(2,1)} %refs_6_.1) | copy-start | bytes 8068
  0.8 1.0 %copy-start.4 = (bf16[256,1024]{1,0:T(8,128)(2,1)S(1)}, bf16[256,1024]{1,0:T(8,128)(2,1)}, u32[]{:S(2)}) copy-start(bf16[256,1024]{1,0:T(8,128)(2,1)} %refs_1_.3) | copy-start | bytes 1572868
  1.8 1.0 %copy-start.6 = (bf16[256,1024]{1,0:T(8,128)(2,1)S(1)}, bf16[256,1024]{1,0:T(8,128)(2,1)}, u32[]{:S(2)}) copy-start(bf16[256,1024]{1,0:T(8,128)(2,1)} %refs_2_.3) | copy-start | bytes 1572868
  2.9 1.0 %copy-start.8 = (bf16[256,1024]{1,0:T(8,128)(2,1)S(1)}, bf16[256,1024]{1,0:T(8,128)(2,1)}, u32[]{:S(2)}) copy-start(bf16[256,1024]{1,0:T(8,128)(2,1)} %refs_3_.3) | copy-start | bytes 1572868
  3.9 0.7 copy-start.12
  4.6 36.4 %copy-start.5 = (bf16[256,1024]{1,0:T(8,128)(2,1)S(1)}, bf16[256,1024]{1,0:T(8,128)(2,1)}, u32[]{:S(2)}) copy-start(bf16[256,1024]{1,0:T(8,128)(2,1)} %refs_1_.3) | copy-start | bytes 1572868
  4.6 36.4 %copy-start.7 = (bf16[256,1024]{1,0:T(8,128)(2,1)S(1)}, bf16[256,1024]{1,0:T(8,128)(2,1)}, u32[]{:S(2)}) copy-start(bf16[256,1024]{1,0:T(8,128)(2,1)} %refs_2_.3) | copy-start | bytes 1572868
  4.6 36.4 %copy-start.9 = (bf16[256,1024]{1,0:T(8,128)(2,1)S(1)}, bf16[256,1024]{1,0:T(8,128)(2,1)}, u32[]{:S(2)}) copy-start(bf16[256,1024]{1,0:T(8,128)(2,1)} %refs_3_.3) | copy-start | bytes 1572868
  4.6 36.4 %copy-start.11 = (bf16[256,1024]{1,0:T(8,128)(2,1)S(1)}, bf16[256,1024]{1,0:T(8,128)(2,1)}, u32[]{:S(2)}) copy-start(bf16[256,1024]{1,0:T(8,128)(2,1)} %refs_4_.1) | copy-start | bytes 1572868
  6.7 52.3 %copy-start.16 = (s32[8]{0:T(128)S(1)}, s32[8]{0:T(128)}, u32[]{:S(2)}) copy-start(s32[8]{0:T(128)} %order_ref.1) | copy-start | bytes 100
  25.2 0.7 copy-start.14
  25.9 0.7 copy-start.15
  27.8 13.2 %all-to-all-start.1 = ((bf16[8,160,128]{2,1,0:T(8,128)(2,1)}), bf16[8,160,128]{2,1,0:T(8,128)(2,1)S(1)}, u32[]{:S(2)}, u32[]{:S(2)}) async-start(bf16[8,160,128]{2,1,0:T(8,128)(2,1)} %route.1), calls=%async_computation.1 | async-start | bytes 655360 | tf_op jit(solution)/shard_map/all_to_all | solution.py:322
  35.8 1.9 %copy-start.2 = (bf16[8,8,128,256]{3,2,1,0:T(8,128)(2,1)}, bf16[8,8,128,256]{3,2,1,0:T(8,128)(2,1)S(1)}, u32[]{:S(2)}) copy-start(bf16[8,8,128,256]{3,2,1,0:T(8,128)(2,1)S(1)} %medium_table.1.refs_7_) | copy-start | bytes 12582916
  41.1 2.2 %copy-start.3 = (bf16[8,8,128,256]{3,2,1,0:T(8,128)(2,1)S(1)}, bf16[8,8,128,256]{3,2,1,0:T(8,128)(2,1)}, u32[]{:S(2)}) copy-start(bf16[8,8,128,256]{3,2,1,0:T(8,128)(2,1)} %copy-done.2) | copy-start | bytes 12582916
  48.7 1.8 %collective-permute-start.2 = (f32[1,256]{1,0:T(1,128)S(1)}, f32[1,256]{1,0:T(1,128)S(1)}, u32[]{:S(2)}, u32[]{:S(2)}) collective-permute-start(f32[1,256]{1,0:T(1,128)S(1)} %get-tuple-element.8), channel_id=1, source_target_pairs={{0,3},{1,0},{2,1},{3,2},{4,7},{5,4},{6,5},{7,6},{8,11},{9,8},{10,9... | collective-permute-start | bytes 3080 | tf_op jit(solution)/shard_map/ppermute | solution.py:375
  48.7 3.6 %collective-permute-start.1 = (f32[1,256]{1,0:T(1,128)S(1)}, f32[1,256]{1,0:T(1,128)S(1)}, u32[]{:S(2)}, u32[]{:S(2)}) collective-permute-start(f32[1,256]{1,0:T(1,128)S(1)} %get-tuple-element.8), channel_id=1, source_target_pairs={{0,2},{1,3},{2,0},{3,1},{4,6},{5,7},{6,4},{7,5},{8,10},{9,11},{10,... | collective-permute-start | bytes 3080 | tf_op jit(solution)/shard_map/ppermute | solution.py:375
  50.3 3.0 %collective-permute-start = (f32[1,256]{1,0:T(1,128)S(1)}, f32[1,256]{1,0:T(1,128)S(1)}, u32[]{:S(2)}, u32[]{:S(2)}) collective-permute-start(f32[1,256]{1,0:T(1,128)S(1)} %get-tuple-element.8), channel_id=1, source_target_pairs={{0,1},{1,2},{2,3},{3,0},{4,5},{5,6},{6,7},{7,4},{8,9},{9,10},{10,1... | collective-permute-start | bytes 3080 | tf_op jit(solution)/shard_map/ppermute | solution.py:375
  54.2 17.1 %all-to-all-start.2 = ((bf16[8,128,256]{2,1,0:T(8,128)(2,1)}), bf16[8,128,256]{2,1,0:T(8,128)(2,1)S(1)}, u32[]{:S(2)}, u32[]{:S(2)}) async-start(bf16[8,128,256]{2,1,0:T(8,128)(2,1)} %multiply_convert_fusion), calls=%async_computation.2 | async-start | bytes 1048576 | tf_op jit(solution)/shard_map/all_to_all | solution.py:322
  59.2 36.0 %copy-start.10 = (bf16[256,1024]{1,0:T(8,128)(2,1)S(1)}, bf16[256,1024]{1,0:T(8,128)(2,1)}, u32[]{:S(2)}) copy-start(bf16[256,1024]{1,0:T(8,128)(2,1)} %gate_ref.1) | copy-start | bytes 1572868
  61.3 3.3 %copy-start = (bf16[8,8,256,256]{3,2,1,0:T(8,128)(2,1)}, bf16[8,8,256,256]{3,2,1,0:T(8,128)(2,1)S(1)}, u32[]{:S(2)}) copy-start(bf16[8,8,256,256]{3,2,1,0:T(8,128)(2,1)S(1)} %long_table.1.table_ref) | copy-start | bytes 25165828
  71.3 3.4 %copy-start.1 = (bf16[8,8,256,256]{3,2,1,0:T(8,128)(2,1)S(1)}, bf16[8,8,256,256]{3,2,1,0:T(8,128)(2,1)}, u32[]{:S(2)}) copy-start(bf16[8,8,256,256]{3,2,1,0:T(8,128)(2,1)} %copy-done) | copy-start | bytes 25165828

commit v3 on v2

v3 whole, which is shorter than its diff:
```python
import jax
import jax.numpy as jnp
from jax import lax
from jax.experimental import pallas as pl
from jax.experimental.pallas import tpu as pltpu
from jax.sharding import PartitionSpec as P

EPSILON = 1e-06
LANES = 128
EDGE = 8
VMEM_BYTES = 24 * 1024 * 1024
TAIL_TILES = 2
GATE_TILES = 4
F32 = jnp.float32
BF16 = jnp.bfloat16


def params(*semantics):
    return pltpu.CompilerParams(dimension_semantics=semantics, vmem_limit_bytes=VMEM_BYTES)


def in_vmem(array):
    return pltpu.with_memory_space_constraint(array, pltpu.VMEM)


def lane_taps(taps_ref, which, size, width, first=0):
    groups = taps_ref.shape[2]
    group = lax.broadcasted_iota(jnp.int32, (groups, width), 0)
    lane = lax.broadcasted_iota(jnp.int32, (groups, width), 1) + first
    spread = (group == lane // size).astype(BF16)
    return jnp.dot(taps_ref[which], spread, preferred_element_type=F32)


def short_filter(extended, taps, start, rows):
    total = extended[start : start + rows] * taps[0:1]
    for j in range(1, taps.shape[0]):
        total = total + extended[start - j : start - j + rows] * taps[j : j + 1]
    return total


def tail_kernel(size, reach, q_hbm, k_hbm, v_hbm, taps_ref, *rest):
    q_ref, k_ref, v_ref, sems = rest[-4:]
    out_ref = rest[-5]
    rows, width = q_hbm.shape
    first = rows - k_ref.shape[0]
    wide = TAIL_TILES * LANES
    parts = width // wide
    copies = []
    for p in range(parts):
        lanes = pl.ds(p * wide, wide)
        for which, (source, target, start) in enumerate(
            ((k_hbm, k_ref, first), (v_hbm, v_ref, first), (q_hbm, q_ref, rows - 16))
        ):
            copy = pltpu.make_async_copy(
                source.at[pl.ds(start, target.shape[0]), lanes], target.at[:, lanes], sems.at[p, which]
            )
            copy.start()
            copies.append(copy)
    k_taps = lane_taps(taps_ref, 1, size, width)
    v_taps = lane_taps(taps_ref, 2, size, width)
    for t in range(width // LANES):
        if t % TAIL_TILES == 0:
            for copy in copies[3 * (t // TAIL_TILES) : 3 * (t // TAIL_TILES) + 3]:
                copy.wait()
        lanes = slice(t * LANES, (t + 1) * LANES)
        k_part = k_ref[:, lanes].astype(F32)
        v_part = v_ref[:, lanes].astype(F32)
        q_part = q_ref[:, lanes].astype(F32)
        k_feat = short_filter(k_part, k_taps[:, lanes], 16, reach)
        v_feat = short_filter(v_part, v_taps[:, lanes], 16, reach)
        out_ref[t, :reach, :] = (k_feat * v_feat).astype(BF16)
        edges = [q_part[-EDGE:], k_part[-EDGE:], v_part[-EDGE:], jnp.zeros((EDGE, LANES), F32)]
        out_ref[t, reach : reach + 4 * EDGE, :] = jnp.concatenate(edges, axis=0).astype(BF16)
        if len(rest) == 6:
            out_ref[t, reach + 4 * EDGE :, :] = rest[0][t]


def call_tails(q_one, k_one, v_one, short_taps, reach, extra):
    rows, width = q_one.shape
    tiles = width // LANES
    size = width // short_taps.shape[2]
    inputs = [q_one, k_one, v_one, short_taps]
    out_rows = reach + 4 * EDGE
    if extra is not None:
        inputs.append(extra)
        out_rows += extra.shape[1]

    def kernel(*refs):
        tail_kernel(size, reach, *refs)

    return pl.pallas_call(
        kernel,
        in_specs=[pl.BlockSpec(memory_space=pltpu.HBM)] * 3
        + [pl.BlockSpec(memory_space=pltpu.VMEM)] * (len(inputs) - 3),
        out_specs=pl.BlockSpec(memory_space=pltpu.VMEM),
        out_shape=jax.ShapeDtypeStruct((tiles, out_rows, LANES), BF16),
        scratch_shapes=[
            pltpu.VMEM((16, width), BF16),
            pltpu.VMEM((reach + 16, width), BF16),
            pltpu.VMEM((reach + 16, width), BF16),
            pltpu.SemaphoreType.DMA((tiles // TAIL_TILES, 3)),
        ],
        compiler_params=params(),
        name="tails",
    )(*inputs)


def route_kernel(source_ref, spread_ref, out_ref):
    kept = out_ref.shape[1]
    for d in range(out_ref.shape[0]):
        out_ref[d] = spread_ref[source_ref[d], :kept, :]


def call_route(source, spread, kept):
    count, _, lanes = spread.shape
    return pl.pallas_call(
        route_kernel,
        in_specs=[
            pl.BlockSpec(memory_space=pltpu.SMEM),
            pl.BlockSpec(memory_space=pltpu.VMEM),
        ],
        out_specs=pl.BlockSpec(memory_space=pltpu.VMEM),
        out_shape=jax.ShapeDtypeStruct((count, kept, lanes), BF16),
        compiler_params=params(),
        name="route",
    )(source, spread)


def medium_table_kernel(base_ref, out_ref):
    reach, wide = out_ref.shape[2], base_ref.shape[2]
    for g in range(base_ref.shape[1]):
        row = jnp.broadcast_to(base_ref[0, g : g + 1, :], (reach, wide))
        out_ref[0, g] = pltpu.roll(row, 0, 1, stride=1, stride_axis=0).astype(BF16)


def call_medium_table(medium_taps, tile_groups, rows):
    reach, groups = medium_taps.shape
    tiles = groups // tile_groups
    base = jnp.pad(jnp.transpose(medium_taps[::-1]), ((0, 0), (1, rows - reach - 1)))
    return pl.pallas_call(
        medium_table_kernel,
        grid=(tiles,),
        in_specs=[pl.BlockSpec((1, tile_groups, rows), lambda i: (i, 0, 0))],
        out_specs=pl.BlockSpec((1, tile_groups, reach, rows), lambda i: (i, 0, 0, 0)),
        out_shape=pltpu.VMEM((tiles, tile_groups, reach, rows), BF16),
        compiler_params=params("arbitrary"),
        name="medium_table",
    )(base.astype(F32).reshape(tiles, tile_groups, rows))


def long_table_kernel(base_ref, out_ref):
    half, wide = out_ref.shape[1:]
    strip = jnp.broadcast_to(base_ref[0], (half, base_ref.shape[2]))
    strip = pltpu.roll(strip, 0, 1, stride=1, stride_axis=0)
    out_ref[0] = strip[:, half:].astype(BF16)


def call_long_table(long_rows, rows, lags):
    groups, length = long_rows.shape
    pieces = length // (lags * rows)
    half = rows // 2
    reach = lags * rows
    padded = jnp.pad(long_rows.astype(F32), ((0, 0), (rows, 0)))
    windows = jnp.stack(
        [padded[:, p * reach : p * reach + reach + rows] for p in range(pieces)], axis=1
    ).reshape(groups * pieces, 1, reach + rows)
    return pl.pallas_call(
        long_table_kernel,
        grid=(groups * pieces,),
        in_specs=[pl.BlockSpec((1, 1, reach + rows), lambda i: (i, 0, 0))],
        out_specs=pl.BlockSpec((1, half, reach + half), lambda i: (i, 0, 0)),
        out_shape=pltpu.VMEM((groups * pieces, half, reach + half), BF16),
        compiler_params=params("arbitrary"),
        name="long_table",
    )(windows)


def mix_kernel(
    size, keep_ref, q_ref, k_ref, v_ref, gate_ref, halo_ref, taps_ref, table_ref, out_ref, energy_ref
):
    rows, width = q_ref.shape
    tiles, groups, reach, wide = table_ref.shape
    keep = keep_ref[0:1, :]
    taps = [lane_taps(taps_ref, which, size, width) for which in range(3)]
    lane_group = lax.broadcasted_iota(jnp.int32, (1, 2 * LANES), 1) % LANES // size
    squares = jnp.zeros((rows, LANES), F32)
    for t in range(tiles):
        lanes = slice(t * LANES, (t + 1) * LANES)
        edges = halo_ref[t, reach:, :].astype(F32) * keep

        def feature(ref, which):
            extended = jnp.concatenate(
                [edges[which * EDGE : (which + 1) * EDGE], ref[:, lanes].astype(F32)], axis=0
            )
            return short_filter(extended, taps[which][:, lanes], EDGE, rows)

        q_feat = feature(q_ref, 0)
        z_own = (feature(k_ref, 1) * feature(v_ref, 2)).astype(BF16)
        z_halo = (halo_ref[t, :reach, :].astype(F32) * keep).astype(BF16)
        window = jnp.concatenate([jnp.concatenate([z_halo, z_own[:reach]], axis=0), z_own], axis=1)
        every = jnp.dot(
            table_ref[t].reshape(groups * reach, wide), window, preferred_element_type=F32
        )
        medium = every[:reach]
        for g in range(1, groups):
            medium = jnp.where(lane_group == g, every[g * reach : (g + 1) * reach], medium)
        mixed = q_feat * jnp.concatenate([medium[:, :LANES], medium[:, LANES:]], axis=0)
        out_ref[t] = jnp.transpose(mixed * gate_ref[:, lanes].astype(F32)).astype(BF16)
        squares = squares + mixed * mixed
    energy_ref[...] = jnp.sum(jnp.transpose(squares), axis=0, keepdims=True)


def call_mix(keep, q_one, k_one, v_one, k_two, halo, short_taps, medium_table):
    rows, width = q_one.shape
    size = width // short_taps.shape[2]

    def kernel(*refs):
        mix_kernel(size, *refs)

    return pl.pallas_call(
        kernel,
        in_specs=[pl.BlockSpec(memory_space=pltpu.VMEM)] * 8,
        out_specs=[pl.BlockSpec(memory_space=pltpu.VMEM)] * 2,
        out_shape=[
            jax.ShapeDtypeStruct((width // LANES, LANES, rows), BF16),
            jax.ShapeDtypeStruct((1, rows), F32),
        ],
        compiler_params=params(),
        name="mix",
    )(keep, q_one, k_one, v_one, k_two, halo, short_taps, in_vmem(medium_table))


def long_kernel(full_width, size, holder_ref, value_ref, energy_ref, table_ref, gain_ref, out_ref, ordered_ref):
    blocks, channels, rows = value_ref.shape
    slots, half, wide = table_ref.shape
    lags = wide // rows
    pieces = blocks // lags
    reach = blocks * size
    holders = [holder_ref[b] for b in range(blocks)]
    scales = [lax.rsqrt(energy_ref[holder] / full_width + EPSILON) for holder in holders]
    for g in range(channels // size):
        here = slice(g * size, (g + 1) * size)
        ordered_ref[g, :reach] = jnp.zeros((reach, rows), BF16)
        for b, holder in enumerate(holders):
            scaled = (value_ref[holder, here].astype(F32) * scales[b]).astype(BF16)
            ordered_ref[g, reach + b * size : reach + (b + 1) * size] = scaled
        total = ordered_ref[g, reach:].astype(F32) * gain_ref[g]
        for p in range(pieces):
            left = jnp.concatenate(
                [
                    ordered_ref[g, (blocks - lag) * size : (2 * blocks - lag) * size]
                    for lag in range(p * lags, (p + 1) * lags)
                ],
                axis=1,
            )
            right = jnp.concatenate(
                [
                    table_ref[g * pieces + p, :, lag * rows + shift : (lag + 1) * rows + shift]
                    for lag in range(lags)
                    for shift in (half, 0)
                ],
                axis=0,
            )
            total = total + jnp.dot(left, right, preferred_element_type=F32)
        for b, holder in enumerate(holders):
            out_ref[holder, here] = total[b * size : (b + 1) * size].astype(BF16)


def call_long(holder, values, energy, long_table, gain, size, full_width):
    blocks, channels, rows = values.shape

    def kernel(*refs):
        long_kernel(full_width, size, *refs)

    return pl.pallas_call(
        kernel,
        in_specs=[pl.BlockSpec(memory_space=pltpu.SMEM)]
        + [pl.BlockSpec(memory_space=pltpu.VMEM)] * 4,
        out_specs=pl.BlockSpec(memory_space=pltpu.VMEM),
        out_shape=jax.ShapeDtypeStruct((blocks, channels, rows), BF16),
        scratch_shapes=[pltpu.VMEM((channels // size, 2 * blocks * size, rows), BF16)],
        compiler_params=params(),
        name="long",
    )(holder, values, energy, in_vmem(long_table), gain)


def gate_kernel(mixed_ref, gate_ref, out_ref):
    for t in range(mixed_ref.shape[0]):
        lanes = slice(t * LANES, (t + 1) * LANES)
        mixed = jnp.transpose(mixed_ref[t]).astype(F32)
        out_ref[:, lanes] = (gate_ref[:, lanes].astype(F32) * mixed).astype(BF16)


def call_gate(mixed, q_two):
    rows, width = q_two.shape
    wide = GATE_TILES * LANES
    column = pl.BlockSpec((rows, wide), lambda i: (0, i))
    return pl.pallas_call(
        gate_kernel,
        grid=(width // wide,),
        in_specs=[pl.BlockSpec((GATE_TILES, LANES, rows), lambda i: (i, 0, 0)), column],
        out_specs=column,
        out_shape=jax.ShapeDtypeStruct((rows, width), BF16),
        compiler_params=params("arbitrary"),
        name="gate",
    )(mixed, q_two)


def exchange(array):
    return lax.all_to_all(array, "ctx", split_axis=0, concat_axis=0, tiled=True)


def sum_by_pairs(array, axis):
    count = lax.axis_size(axis)
    assert count & (count - 1) == 0
    bit = 1
    while bit < count:
        array = array + lax.ppermute(array, axis, [(i, i ^ bit) for i in range(count)])
        bit *= 2
    return array


def per_device(
    q_one,
    k_one,
    v_one,
    q_two,
    k_two,
    short_taps,
    medium_taps,
    long_taps,
    skip_gain,
    block_order,
    prev_owner,
):
    rows, width = q_one.shape
    ctx_count = lax.axis_size("ctx")
    tp_count = lax.axis_size("tp")
    me = lax.axis_index("ctx")
    size = width // short_taps.shape[2]
    reach = medium_taps.shape[0]
    assert rows == 2 * reach and short_taps.shape[1] <= EDGE + 1
    tiles = width // LANES
    shard = width // ctx_count
    shard_groups = shard // size
    full_width = width * tp_count

    slots = jnp.arange(ctx_count, dtype=jnp.int32)
    holder = jnp.sum(jnp.where(block_order[None, :] == slots[:, None], slots[None, :], 0), axis=1)
    source = jnp.take(prev_owner, block_order, mode="clip")
    is_first = jnp.sum(jnp.where(slots == me, block_order, 0)) == 0
    keep = jnp.broadcast_to(jnp.where(is_first, 0.0, 1.0), (EDGE, LANES)).astype(F32)

    tail_rows = reach + 4 * EDGE
    halo_rows = tiles * tail_rows // ctx_count
    taps_sent = long_taps.reshape(ctx_count, shard_groups * rows // LANES, LANES)
    if ctx_count == tiles:
        payload = call_tails(q_one, k_one, v_one, short_taps, reach, taps_sent)
    else:
        tails = call_tails(q_one, k_one, v_one, short_taps, reach, None)
        payload = jnp.concatenate([tails.reshape(ctx_count, halo_rows, LANES), taps_sent], axis=1)
    spread = exchange(payload)
    halo = exchange(call_route(source, spread, halo_rows))
    halo = halo.reshape(tiles, tail_rows, LANES)

    medium_table = call_medium_table(medium_taps, LANES // size, rows)
    long_rows = jnp.transpose(
        spread[:, halo_rows:].reshape(ctx_count, shard_groups, rows), (1, 0, 2)
    ).reshape(shard_groups, ctx_count * rows)
    long_table = call_long_table(long_rows, rows, min(ctx_count, 8))

    gated, energy = call_mix(keep, q_one, k_one, v_one, k_two, halo, short_taps, medium_table)
    values = exchange(gated.reshape(ctx_count, shard, rows))
    energy = sum_by_pairs(energy, "tp")
    energy = sum_by_pairs(jnp.where(slots[:, None] == me, energy, 0.0), "ctx")
    energy = energy.reshape(ctx_count, 1, rows)

    gain = lax.dynamic_slice_in_dim(skip_gain, me * shard, shard).reshape(shard_groups, 1, size, 1)
    gain = jnp.broadcast_to(gain, (shard_groups, ctx_count, size, 1))
    gain = gain.reshape(shard_groups, ctx_count * size, 1)
    returned = exchange(call_long(holder, values, energy, long_table, gain, size, full_width))
    return call_gate(returned.reshape(tiles, LANES, rows), q_two)


def solution(mesh):
    in_specs = (
        P("ctx", "tp"),
        P("ctx", "tp"),
        P("ctx", "tp"),
        P("ctx", "tp"),
        P("ctx", "tp"),
        P(None, None, "tp"),
        P(None, "tp"),
        P("tp", "ctx"),
        P("tp"),
        P(),
        P(),
    )
    out_specs = P("ctx", "tp")
    return jax.shard_map(
        per_device, mesh=mesh, in_specs=in_specs, out_specs=out_specs, check_vma=False
    )
```

time: 97 us -> 93 us (0.959)
  blocking collectives: 35.8 us -> 15.9 us
  starting transfers between devices: 8.88 us -> 22.6 us
  waiting for transfers between devices: 12.9 us -> 21.1 us
  local copies, waits for them, and re-layouts: 20 us -> 15 us
  Pallas kernels: 16.8 us -> 15.1 us
    all_to_all x2 -> x1, blocking collectives: 35.8 us -> 15.9 us  [exchange(): return lax.all_to_all(array, 'ctx', split_axis=0, concat_axis=0, tiled=True)]
    all_to_all x2 -> x3, starting transfers between devices: 7.07 us -> 14.5 us  [exchange(): return lax.all_to_all(array, 'ctx', split_axis=0, concat_axis=0, tiled=True)]
    ppermute x3 -> x5, starting transfers between devices: 1.81 us -> 8.11 us  [sum_by_pairs(): lax.ppermute(array, axis, [(i, i ^ bit) for i in range(count)])]
    all_to_all x2 -> x3, waiting for transfers between devices: 10.1 us -> 14.5 us  [exchange(): return lax.all_to_all(array, 'ctx', split_axis=0, concat_axis=0, tiled=True)]
    ppermute x3 -> x5, waiting for transfers between devices: 2.83 us -> 6.6 us  [sum_by_pairs(): lax.ppermute(array, axis, [(i, i ^ bit) for i in range(count)])]
    unnamed x34, local copies, waits for them, and re-layouts: 15.9 us -> 12.3 us
    pallas_call x3, Pallas kernels: 10.7 us -> 9.2 us  [the longest x1 5.24 us: call_mix(): pl.pallas_call(kernel, in_specs=[pl.BlockSpec(memory_space=pltpu.VMEM)] *...]
    dynamic_slice x1 -> x0, local copies, waits for them, and re-layouts: 1.28 us -> none  [per_device(): lax.dynamic_slice_in_dim(block_order, me, 1) == 0]
  transfers between devices with their start and end apart: 5 -> 8, of which waited for: 4 -> 5; matrix products, arithmetic and copies ran while one was open for 4% -> 4% of each run, Pallas kernels for 4% -> 4%
where the time goes in v3:
time: 93 us; the launch traced here: 92.2 us
  starting transfers between devices  22.6 us (24%)
  waiting for transfers between devices  21.1 us (23%)
  blocking collectives  15.9 us (17%)
  Pallas kernels  15.1 us (16%)
  local copies, waits for them, and re-layouts  15 us (16%)
  other arithmetic  1.72 us (2%)
    all_to_all x1, blocking collectives, exchange(): return lax.all_to_all(array, 'ctx', split_axis=0, concat_axis=0, tiled=True)  15.9 us
    all_to_all x3, starting transfers between devices, exchange(): return lax.all_to_all(array, 'ctx', split_axis=0, concat_axis=0, tiled=True)  14.5 us
    all_to_all x3, waiting for transfers between devices, exchange(): return lax.all_to_all(array, 'ctx', split_axis=0, concat_axis=0, tiled=True)  14.5 us
    unnamed x34, local copies, waits for them, and re-layouts  12.3 us
    ppermute x5, starting transfers between devices, sum_by_pairs(): lax.ppermute(array, axis, [(i, i ^ bit) for i in range(count)])  8.11 us
    ppermute x5, waiting for transfers between devices, sum_by_pairs(): lax.ppermute(array, axis, [(i, i ^ bit) for i in range(count)])  6.6 us
    pallas_call x1, Pallas kernels, call_mix(): pl.pallas_call(kernel, in_specs=[pl.BlockSpec(memory_space=pltpu.VMEM)] *...  5.24 us
    pallas_call x1, Pallas kernels, call_tails(): pl.pallas_call(kernel, in_specs=[pl.BlockSpec(memory_space=pltpu.HBM)] *...  2.13 us
  transfers between devices with their start and end apart: 8, of which 5 were waited for; matrix products, arithmetic and copies ran while one was open for 4% of the time, Pallas kernels for 4%

profile of v3, /device:TPU:0, one launch (start us, length us, event | category | flops | bytes accessed | tf_op | source)
XLA Modules:
  0.0 92.2 jit_solution(17184688566003895510)
XLA Ops:
  0.0 0.0 copy-start
  0.0 0.8 reshape.31.refs_4_
  0.8 0.0 copy-start.5
  0.8 1.0 %copy-done.5 = bf16[256,1024]{1,0:T(8,128)(2,1)S(1)} copy-done((bf16[256,1024]{1,0:T(8,128)(2,1)S(1)}, bf16[256,1024]{1,0:T(8,128)(2,1)}, u32[]{:S(2)}) %copy-start.5) | copy-done | bytes 524312
  1.9 1.0 %copy-done.7 = bf16[256,1024]{1,0:T(8,128)(2,1)S(1)} copy-done((bf16[256,1024]{1,0:T(8,128)(2,1)S(1)}, bf16[256,1024]{1,0:T(8,128)(2,1)}, u32[]{:S(2)}) %copy-start.7) | copy-done | bytes 524312
  2.9 1.0 %copy-done.9 = bf16[256,1024]{1,0:T(8,128)(2,1)S(1)} copy-done((bf16[256,1024]{1,0:T(8,128)(2,1)S(1)}, bf16[256,1024]{1,0:T(8,128)(2,1)}, u32[]{:S(2)}) %copy-start.9) | copy-done | bytes 524312
  3.9 0.7 copy-done.13
  4.6 0.0 copy-start.11
  4.6 0.0 copy-start.14
  4.7 2.1 %tails.1 = bf16[8,176,128]{2,1,0:T(8,128)(2,1)} custom-call(bf16[256,1024]{1,0:T(8,128)(2,1)S(1)} %copy-done.5, bf16[256,1024]{1,0:T(8,128)(2,1)S(1)} %copy-done.7, bf16[256,1024]{1,0:T(8,128)(2,1)S(1)} %copy-done.9, bf16[3,7,64]{2,1,0:T(8,128)(2,1)S(1)} %copy-done.13, bf16[8,16,128]{2,1,0:T(8,128)(2,1)S(1)} %reshape.31.refs_4_), custom_call_target="tpu_custom_call" | custom-call | tf_op jit(solution)/shard_map/tails/pallas_call | solution.py:91
  6.8 7.3 %all-to-all-start = ((bf16[8,176,128]{2,1,0:T(8,128)(2,1)}), bf16[8,176,128]{2,1,0:T(8,128)(2,1)S(1)}, u32[]{:S(2)}, u32[]{:S(2)}) async-start(bf16[8,176,128]{2,1,0:T(8,128)(2,1)} %tails.1), calls=%async_computation | async-start | bytes 720896 | tf_op jit(solution)/shard_map/all_to_all | solution.py:310
  14.1 0.7 pad_clamp_fusion
  14.7 0.0 copy-done
  14.7 0.6 gather_fusion
  15.4 9.7 %all-to-all-done.spread_ref = bf16[8,176,128]{2,1,0:T(8,128)(2,1)S(1)} async-done(((bf16[8,176,128]{2,1,0:T(8,128)(2,1)}), bf16[8,176,128]{2,1,0:T(8,128)(2,1)S(1)}, u32[]{:S(2)}, u32[]{:S(2)}) %all-to-all-start) | async-done | bytes 360480 | tf_op jit(solution)/shard_map/all_to_all | solution.py:310
  25.1 1.3 %route.1 = bf16[8,160,128]{2,1,0:T(8,128)(2,1)} custom-call(s32[8]{0:T(128)S(1)} %gather_fusion, bf16[8,176,128]{2,1,0:T(8,128)(2,1)S(1)} %all-to-all-done.spread_ref), custom_call_target="tpu_custom_call" | custom-call | tf_op jit(solution)/shard_map/route/pallas_call | solution.py:116
  26.4 3.6 %all-to-all-start.1 = ((bf16[8,160,128]{2,1,0:T(8,128)(2,1)}), bf16[8,160,128]{2,1,0:T(8,128)(2,1)S(1)}, u32[]{:S(2)}, u32[]{:S(2)}) async-start(bf16[8,160,128]{2,1,0:T(8,128)(2,1)} %route.1), calls=%async_computation.1 | async-start | bytes 655360 | tf_op jit(solution)/shard_map/all_to_all | solution.py:310
  30.0 0.0 copy-done.15
  30.0 0.1 rev.3
  30.1 0.1 bitcast_convert_fusion.base_ref
  30.1 1.7 %medium_table.1.refs_7_ = bf16[8,8,128,256]{3,2,1,0:T(8,128)(2,1)S(1)} custom-call(f32[8,8,256]{2,1,0:T(8,128)S(1)} %bitcast_convert_fusion.base_ref), custom_call_target="tpu_custom_call" | custom-call | tf_op jit(solution)/shard_map/medium_table/pallas_call | solution.py:140
  31.9 0.0 copy-start.3
  31.9 1.9 %copy-done.3 = bf16[8,8,128,256]{3,2,1,0:T(8,128)(2,1)} copy-done((bf16[8,8,128,256]{3,2,1,0:T(8,128)(2,1)}, bf16[8,8,128,256]{3,2,1,0:T(8,128)(2,1)S(1)}, u32[]{:S(2)}) %copy-start.3) | copy-done | bytes 4194328
  33.8 0.0 copy-done.16
  33.8 0.6 select_reduce_fusion.1
  35.0 4.8 %all-to-all-done.1.refs_5_ = bf16[8,160,128]{2,1,0:T(8,128)(2,1)S(1)} async-done(((bf16[8,160,128]{2,1,0:T(8,128)(2,1)}), bf16[8,160,128]{2,1,0:T(8,128)(2,1)S(1)}, u32[]{:S(2)}, u32[]{:S(2)}) %all-to-all-start.1) | async-done | bytes 327712 | tf_op jit(solution)/shard_map/all_to_all | solution.py:310
  39.8 0.0 copy-done.6
  39.8 0.0 copy-done.8
  39.8 0.0 copy-done.10
  39.8 0.0 copy-done.11
  39.8 0.0 copy-done.14
  39.8 0.0 copy-start.4
  39.8 2.2 %copy-done.4 = bf16[8,8,128,256]{3,2,1,0:T(8,128)(2,1)S(1)} copy-done((bf16[8,8,128,256]{3,2,1,0:T(8,128)(2,1)S(1)}, bf16[8,8,128,256]{3,2,1,0:T(8,128)(2,1)}, u32[]{:S(2)}) %copy-start.4) | copy-done | bytes 4194328
  42.0 5.2 %mix.1 = (bf16[8,128,256]{2,1,0:T(8,128)(2,1)}, f32[1,256]{1,0:T(1,128)S(1)}) custom-call(f32[8,128]{1,0:T(8,128)S(1)} %broadcast_in_dim.61.refs_0_, bf16[256,1024]{1,0:T(8,128)(2,1)S(1)} %copy-done.6, bf16[256,1024]{1,0:T(8,128)(2,1)S(1)} %copy-done.8, bf16[256,1024]{1,0:T(8,128)(2,1)S(1)} %copy-done.10, bf16[256,1024]{1,0:T(8,128)(2,1)S(1)} %copy-done.11, ...), custom_call_target="tpu_custom_call" | custom-call | tf_op jit(solution)/shard_map/mix/pallas_call | solution.py:220
  47.2 0.0 collective-permute-start
  47.2 1.1 %collective-permute-done = f32[1,256]{1,0:T(1,128)S(1)} collective-permute-done((f32[1,256]{1,0:T(1,128)S(1)}, f32[1,256]{1,0:T(1,128)S(1)}, u32[]{:S(2)}, u32[]{:S(2)}) %collective-permute-start) | collective-permute-done | bytes 1056 | tf_op jit(solution)/shard_map/ppermute | solution.py:318
  48.4 1.5 %collective-permute-start.1 = (f32[1,256]{1,0:T(1,128)S(1)}, f32[1,256]{1,0:T(1,128)S(1)}, u32[]{:S(2)}, u32[]{:S(2)}) collective-permute-start(f32[1,256]{1,0:T(1,128)S(1)} %add.22), channel_id=1, source_target_pairs={{0,2},{1,3},{2,0},{3,1},{4,6},{5,7},{6,4},{7,5},{8,10},{9,11},{10,... | collective-permute-start | bytes 3080 | tf_op jit(solution)/shard_map/ppermute | solution.py:318
  49.9 3.6 %all-to-all-start.2 = ((bf16[8,128,256]{2,1,0:T(8,128)(2,1)}), bf16[8,128,256]{2,1,0:T(8,128)(2,1)S(1)}, u32[]{:S(2)}, u32[]{:S(2)}) async-start(bf16[8,128,256]{2,1,0:T(8,128)(2,1)} %get-tuple-element.7), calls=%async_computation.2 | async-start | bytes 1048576 | tf_op jit(solution)/shard_map/all_to_all | solution.py:310
  53.5 0.0 collective-permute-done.1
  53.5 0.1 broadcast_select_fusion
  53.6 2.0 %collective-permute-start.2 = (f32[8,256]{1,0:T(8,128)S(1)}, f32[8,256]{1,0:T(8,128)S(1)}, u32[]{:S(2)}, u32[]{:S(2)}) collective-permute-start(f32[8,256]{1,0:T(8,128)S(1)} %broadcast_select_fusion), channel_id=1, source_target_pairs={{0,4},{4,0},{8,12},{12,8},{16,20},{20,16},{24,28},{28,24},{1,5},{5... | collective-permute-start | bytes 24584 | tf_op jit(solution)/shard_map/ppermute | solution.py:318
  55.6 3.9 %collective-permute-done.2 = f32[8,256]{1,0:T(8,128)S(1)} collective-permute-done((f32[8,256]{1,0:T(8,128)S(1)}, f32[8,256]{1,0:T(8,128)S(1)}, u32[]{:S(2)}, u32[]{:S(2)}) %collective-permute-start.2) | collective-permute-done | bytes 8224 | tf_op jit(solution)/shard_map/ppermute | solution.py:318
  59.5 0.1 fusion
  59.6 0.8 collective-permute-start.3
  60.3 0.1 select_reduce_fusion.refs_0_
  60.4 0.8 dynamic_slice.3
  61.2 0.1 broadcast_in_dim.67
  61.3 0.3 broadcast_in_dim.70.refs_4_
  61.6 1.6 %collective-permute-done.3 = f32[8,256]{1,0:T(8,128)S(1)} collective-permute-done((f32[8,256]{1,0:T(8,128)S(1)}, f32[8,256]{1,0:T(8,128)S(1)}, u32[]{:S(2)}, u32[]{:S(2)}) %collective-permute-start.3) | collective-permute-done | bytes 8224 | tf_op jit(solution)/shard_map/ppermute | solution.py:318
  63.2 0.1 fusion.1
  63.3 3.8 %collective-permute-start.4 = (f32[8,256]{1,0:T(8,128)S(1)}, f32[8,256]{1,0:T(8,128)S(1)}, u32[]{:S(2)}, u32[]{:S(2)}) collective-permute-start(f32[8,256]{1,0:T(8,128)S(1)} %fusion.1), channel_id=1, source_target_pairs={{0,16},{4,20},{8,24},{12,28},{16,0},{20,4},{24,8},{28,12},{1,17},{... | collective-permute-start | bytes 24584 | tf_op jit(solution)/shard_map/ppermute | solution.py:318
  67.1 0.1 reshape.37.base_ref
  67.2 0.0 copy-start.12
  67.2 1.9 %long_table.1.refs_3_ = bf16[8,128,2176]{2,1,0:T(8,128)(2,1)S(1)} custom-call(f32[8,1,2304]{2,1,0:T(1,128)S(1)} %reshape.37.base_ref), custom_call_target="tpu_custom_call" | custom-call | tf_op jit(solution)/shard_map/long_table/pallas_call | solution.py:167
  69.1 0.0 copy-start.1
  69.1 2.1 %copy-done.1 = bf16[8,128,2176]{2,1,0:T(8,128)(2,1)} copy-done((bf16[8,128,2176]{2,1,0:T(8,128)(2,1)}, bf16[8,128,2176]{2,1,0:T(8,128)(2,1)S(1)}, u32[]{:S(2)}) %copy-start.1) | copy-done | bytes 4456472
  71.1 0.0 collective-permute-done.4
  71.2 0.0 all-to-all-done.2.refs_1_
  71.2 0.0 copy-start.2
  71.2 2.3 %copy-done.2 = bf16[8,128,2176]{2,1,0:T(8,128)(2,1)S(1)} copy-done((bf16[8,128,2176]{2,1,0:T(8,128)(2,1)S(1)}, bf16[8,128,2176]{2,1,0:T(8,128)(2,1)}, u32[]{:S(2)}) %copy-start.2) | copy-done | bytes 4456472
  73.4 1.8 %long.1 = bf16[8,128,256]{2,1,0:T(8,128)(2,1)S(1)} custom-call(s32[8]{0:T(128)S(1)} %select_reduce_fusion.refs_0_, bf16[8,128,256]{2,1,0:T(8,128)(2,1)S(1)} %all-to-all-done.2.refs_1_, f32[8,1,256]{2,1,0:T(1,128)S(1)} %reshape.34.refs_2_, bf16[8,128,2176]{2,1,0:T(8,128)(2,1)S(1)} %copy-done.2, f32[8,128,1]{2,1,0:T(8,128)S(1)} %broadcast_in_dim.70.refs_4_), custom_call_target="tpu_custom_call" | custom-call | tf_op jit(solution)/shard_map/long/pallas_call | solution.py:275
  75.3 15.9 %all_to_all.20.mixed_ref = bf16[8,128,256]{2,1,0:T(8,128)(2,1)S(1)} all-to-all(bf16[8,128,256]{2,1,0:T(8,128)(2,1)S(1)} %long.1), channel_id=1, replica_groups=mesh['ctx'=8,'tp'=4] {'ctx'}, dimensions={0} | all-to-all | bytes 1048576 | tf_op jit(solution)/shard_map/all_to_all | solution.py:310
  91.1 0.0 copy-done.12
  91.2 1.0 %gate.1 = bf16[256,1024]{1,0:T(8,128)(2,1)} custom-call(bf16[8,128,256]{2,1,0:T(8,128)(2,1)S(1)} %all_to_all.20.mixed_ref, bf16[256,1024]{1,0:T(8,128)(2,1)S(1)} %copy-done.12), custom_call_target="tpu_custom_call" | custom-call | tf_op jit(solution)/shard_map/gate/pallas_call | solution.py:298
  (18 shorter events, 0.1 us)
Async XLA Ops:
  0.0 14.7 %copy-start = (s32[8]{0:T(128)S(1)}, s32[8]{0:T(128)}, u32[]{:S(2)}) copy-start(s32[8]{0:T(128)} %param.21) | copy-start | bytes 100
  0.0 30.0 %copy-start.15 = (bf16[128,64]{0,1:T(8,128)(2,1)S(1)}, bf16[128,64]{0,1:T(8,128)(2,1)}, u32[]{:S(2)}) copy-start(bf16[128,64]{0,1:T(8,128)(2,1)} %param.17) | copy-start | bytes 49156
  0.8 1.0 %copy-start.5 = (bf16[256,1024]{1,0:T(8,128)(2,1)S(1)}, bf16[256,1024]{1,0:T(8,128)(2,1)}, u32[]{:S(2)}) copy-start(bf16[256,1024]{1,0:T(8,128)(2,1)} %refs_1_.3) | copy-start | bytes 1572868
  1.8 1.0 %copy-start.7 = (bf16[256,1024]{1,0:T(8,128)(2,1)S(1)}, bf16[256,1024]{1,0:T(8,128)(2,1)}, u32[]{:S(2)}) copy-start(bf16[256,1024]{1,0:T(8,128)(2,1)} %refs_2_.3) | copy-start | bytes 1572868
  2.9 1.0 %copy-start.9 = (bf16[256,1024]{1,0:T(8,128)(2,1)S(1)}, bf16[256,1024]{1,0:T(8,128)(2,1)}, u32[]{:S(2)}) copy-start(bf16[256,1024]{1,0:T(8,128)(2,1)} %refs_3_.3) | copy-start | bytes 1572868
  3.9 0.7 copy-start.13
  4.6 29.2 %copy-start.16 = (s32[8]{0:T(128)S(1)}, s32[8]{0:T(128)}, u32[]{:S(2)}) copy-start(s32[8]{0:T(128)} %param.20) | copy-start | bytes 100
  4.6 35.1 %copy-start.6 = (bf16[256,1024]{1,0:T(8,128)(2,1)S(1)}, bf16[256,1024]{1,0:T(8,128)(2,1)}, u32[]{:S(2)}) copy-start(bf16[256,1024]{1,0:T(8,128)(2,1)} %refs_1_.3) | copy-start | bytes 1572868
  4.6 35.1 %copy-start.8 = (bf16[256,1024]{1,0:T(8,128)(2,1)S(1)}, bf16[256,1024]{1,0:T(8,128)(2,1)}, u32[]{:S(2)}) copy-start(bf16[256,1024]{1,0:T(8,128)(2,1)} %refs_2_.3) | copy-start | bytes 1572868
  4.6 35.1 %copy-start.10 = (bf16[256,1024]{1,0:T(8,128)(2,1)S(1)}, bf16[256,1024]{1,0:T(8,128)(2,1)}, u32[]{:S(2)}) copy-start(bf16[256,1024]{1,0:T(8,128)(2,1)} %refs_3_.3) | copy-start | bytes 1572868
  4.6 35.1 %copy-start.11 = (bf16[256,1024]{1,0:T(8,128)(2,1)S(1)}, bf16[256,1024]{1,0:T(8,128)(2,1)}, u32[]{:S(2)}) copy-start(bf16[256,1024]{1,0:T(8,128)(2,1)} %refs_4_.1) | copy-start | bytes 1572868
  4.6 35.1 %copy-start.14 = (bf16[3,7,64]{2,1,0:T(8,128)(2,1)S(1)}, bf16[3,7,64]{2,1,0:T(8,128)(2,1)}, u32[]{:S(2)}) copy-start(bf16[3,7,64]{2,1,0:T(8,128)(2,1)} %refs_6_.1) | copy-start | bytes 8068
  6.8 18.3 %all-to-all-start = ((bf16[8,176,128]{2,1,0:T(8,128)(2,1)}), bf16[8,176,128]{2,1,0:T(8,128)(2,1)S(1)}, u32[]{:S(2)}, u32[]{:S(2)}) async-start(bf16[8,176,128]{2,1,0:T(8,128)(2,1)} %tails.1), calls=%async_computation | async-start | bytes 720896 | tf_op jit(solution)/shard_map/all_to_all | solution.py:310
  26.4 13.4 %all-to-all-start.1 = ((bf16[8,160,128]{2,1,0:T(8,128)(2,1)}), bf16[8,160,128]{2,1,0:T(8,128)(2,1)S(1)}, u32[]{:S(2)}, u32[]{:S(2)}) async-start(bf16[8,160,128]{2,1,0:T(8,128)(2,1)} %route.1), calls=%async_computation.1 | async-start | bytes 655360 | tf_op jit(solution)/shard_map/all_to_all | solution.py:310
  31.9 1.9 %copy-start.3 = (bf16[8,8,128,256]{3,2,1,0:T(8,128)(2,1)}, bf16[8,8,128,256]{3,2,1,0:T(8,128)(2,1)S(1)}, u32[]{:S(2)}) copy-start(bf16[8,8,128,256]{3,2,1,0:T(8,128)(2,1)S(1)} %medium_table.1.refs_7_) | copy-start | bytes 12582916
  39.8 2.2 %copy-start.4 = (bf16[8,8,128,256]{3,2,1,0:T(8,128)(2,1)S(1)}, bf16[8,8,128,256]{3,2,1,0:T(8,128)(2,1)}, u32[]{:S(2)}) copy-start(bf16[8,8,128,256]{3,2,1,0:T(8,128)(2,1)} %copy-done.3) | copy-start | bytes 12582916
  47.2 1.1 %collective-permute-start = (f32[1,256]{1,0:T(1,128)S(1)}, f32[1,256]{1,0:T(1,128)S(1)}, u32[]{:S(2)}, u32[]{:S(2)}) collective-permute-start(f32[1,256]{1,0:T(1,128)S(1)} %get-tuple-element.8), channel_id=1, source_target_pairs={{0,1},{1,0},{2,3},{3,2},{4,5},{5,4},{6,7},{7,6},{8,9},{9,8},{10,11... | collective-permute-start | bytes 3080 | tf_op jit(solution)/shard_map/ppermute | solution.py:318
  48.4 5.2 %collective-permute-start.1 = (f32[1,256]{1,0:T(1,128)S(1)}, f32[1,256]{1,0:T(1,128)S(1)}, u32[]{:S(2)}, u32[]{:S(2)}) collective-permute-start(f32[1,256]{1,0:T(1,128)S(1)} %add.22), channel_id=1, source_target_pairs={{0,2},{1,3},{2,0},{3,1},{4,6},{5,7},{6,4},{7,5},{8,10},{9,11},{10,... | collective-permute-start | bytes 3080 | tf_op jit(solution)/shard_map/ppermute | solution.py:318
  49.9 21.3 %all-to-all-start.2 = ((bf16[8,128,256]{2,1,0:T(8,128)(2,1)}), bf16[8,128,256]{2,1,0:T(8,128)(2,1)S(1)}, u32[]{:S(2)}, u32[]{:S(2)}) async-start(bf16[8,128,256]{2,1,0:T(8,128)(2,1)} %get-tuple-element.7), calls=%async_computation.2 | async-start | bytes 1048576 | tf_op jit(solution)/shard_map/all_to_all | solution.py:310
  53.6 5.9 %collective-permute-start.2 = (f32[8,256]{1,0:T(8,128)S(1)}, f32[8,256]{1,0:T(8,128)S(1)}, u32[]{:S(2)}, u32[]{:S(2)}) collective-permute-start(f32[8,256]{1,0:T(8,128)S(1)} %broadcast_select_fusion), channel_id=1, source_target_pairs={{0,4},{4,0},{8,12},{12,8},{16,20},{20,16},{24,28},{28,24},{1,5},{5... | collective-permute-start | bytes 24584 | tf_op jit(solution)/shard_map/ppermute | solution.py:318
  59.6 3.7 %collective-permute-start.3 = (f32[8,256]{1,0:T(8,128)S(1)}, f32[8,256]{1,0:T(8,128)S(1)}, u32[]{:S(2)}, u32[]{:S(2)}) collective-permute-start(f32[8,256]{1,0:T(8,128)S(1)} %fusion), channel_id=1, source_target_pairs={{0,8},{4,12},{8,0},{12,4},{16,24},{20,28},{24,16},{28,20},{1,9},{5... | collective-permute-start | bytes 24584 | tf_op jit(solution)/shard_map/ppermute | solution.py:318
  63.3 7.8 %collective-permute-start.4 = (f32[8,256]{1,0:T(8,128)S(1)}, f32[8,256]{1,0:T(8,128)S(1)}, u32[]{:S(2)}, u32[]{:S(2)}) collective-permute-start(f32[8,256]{1,0:T(8,128)S(1)} %fusion.1), channel_id=1, source_target_pairs={{0,16},{4,20},{8,24},{12,28},{16,0},{20,4},{24,8},{28,12},{1,17},{... | collective-permute-start | bytes 24584 | tf_op jit(solution)/shard_map/ppermute | solution.py:318
  67.2 24.0 %copy-start.12 = (bf16[256,1024]{1,0:T(8,128)(2,1)S(1)}, bf16[256,1024]{1,0:T(8,128)(2,1)}, u32[]{:S(2)}) copy-start(bf16[256,1024]{1,0:T(8,128)(2,1)} %gate_ref.1) | copy-start | bytes 1572868
  69.1 2.1 %copy-start.1 = (bf16[8,128,2176]{2,1,0:T(8,128)(2,1)}, bf16[8,128,2176]{2,1,0:T(8,128)(2,1)S(1)}, u32[]{:S(2)}) copy-start(bf16[8,128,2176]{2,1,0:T(8,128)(2,1)S(1)} %long_table.1.refs_3_) | copy-start | bytes 13369348
  71.2 2.3 %copy-start.2 = (bf16[8,128,2176]{2,1,0:T(8,128)(2,1)S(1)}, bf16[8,128,2176]{2,1,0:T(8,128)(2,1)}, u32[]{:S(2)}) copy-start(bf16[8,128,2176]{2,1,0:T(8,128)(2,1)} %copy-done.1) | copy-start | bytes 13369348

commit v4 on v3

v4 whole, which is shorter than its diff:
```python
import jax
import jax.numpy as jnp
from jax import lax
from jax.experimental import pallas as pl
from jax.experimental.pallas import tpu as pltpu
from jax.sharding import PartitionSpec as P

EPSILON = 1e-06
LANES = 128
EDGE = 8
VMEM_BYTES = 24 * 1024 * 1024
TAIL_TILES = 2
MIX_AHEAD = 1
GATE_TILES = 4
F32 = jnp.float32
BF16 = jnp.bfloat16


def params(*semantics):
    return pltpu.CompilerParams(dimension_semantics=semantics, vmem_limit_bytes=VMEM_BYTES)


def in_hbm(array):
    return pltpu.with_memory_space_constraint(array, pltpu.HBM)


def lane_taps(taps_ref, which, size, width, first=0):
    groups = taps_ref.shape[2]
    group = lax.broadcasted_iota(jnp.int32, (groups, width), 0)
    lane = lax.broadcasted_iota(jnp.int32, (groups, width), 1) + first
    spread = (group == lane // size).astype(BF16)
    return jnp.dot(taps_ref[which], spread, preferred_element_type=F32)


def short_filter(extended, taps, start, rows):
    total = extended[start : start + rows] * taps[0:1]
    for j in range(1, taps.shape[0]):
        total = total + extended[start - j : start - j + rows] * taps[j : j + 1]
    return total


def tail_kernel(
    size,
    reach,
    carry,
    q_hbm,
    k_hbm,
    v_hbm,
    taps_hbm,
    long_hbm,
    out_ref,
    q_ref,
    k_ref,
    v_ref,
    taps_ref,
    long_ref,
    wide_ref,
    sems,
):
    rows, width = q_hbm.shape
    first = rows - k_ref.shape[0]
    wide = TAIL_TILES * LANES
    taps_copy = pltpu.make_async_copy(taps_hbm, taps_ref, sems.at[0, 3])
    taps_copy.start()
    parts = []
    for p in range(width // wide):
        lanes = pl.ds(p * wide, wide)
        copies = []
        for which, (source, target, start) in enumerate(
            ((k_hbm, k_ref, first), (v_hbm, v_ref, first), (q_hbm, q_ref, rows - 16))
        ):
            copy = pltpu.make_async_copy(
                source.at[pl.ds(start, target.shape[0]), lanes], target.at[:, lanes], sems.at[p, which]
            )
            copy.start()
            copies.append(copy)
        parts.append(copies)
    long_copy = pltpu.make_async_copy(long_hbm, long_ref, sems.at[1, 3])
    long_copy.start()
    taps_copy.wait()
    k_taps = lane_taps(taps_ref, 1, size, width)
    v_taps = lane_taps(taps_ref, 2, size, width)
    for t in range(width // LANES):
        if t % TAIL_TILES == 0:
            for copy in parts[t // TAIL_TILES]:
                copy.wait()
        lanes = slice(t * LANES, (t + 1) * LANES)
        wide_ref[t, 0] = k_ref[:, lanes].astype(F32)
        wide_ref[t, 1] = v_ref[:, lanes].astype(F32)
        q_part = q_ref[:, lanes].astype(F32)
        k_feat = short_filter(wide_ref.at[t, 0], k_taps[:, lanes], 16, reach)
        v_feat = short_filter(wide_ref.at[t, 1], v_taps[:, lanes], 16, reach)
        out_ref[t, :reach, :] = (k_feat * v_feat).astype(BF16)
        last = slice(reach + 16 - EDGE, reach + 16)
        edges = [q_part[-EDGE:], wide_ref[t, 0, last], wide_ref[t, 1, last], jnp.zeros((EDGE, LANES), F32)]
        out_ref[t, reach : reach + 4 * EDGE, :] = jnp.concatenate(edges, axis=0).astype(BF16)
    long_copy.wait()
    if carry:
        groups = LANES // size
        for t in range(width // LANES):
            taps = long_ref[t * groups : (t + 1) * groups, :].astype(F32)
            pieces = [taps[:, a : a + LANES] for a in range(0, rows, LANES)]
            out_ref[t, reach + 4 * EDGE :, :] = jnp.concatenate(pieces, axis=0).astype(BF16)


def call_tails(q_one, k_one, v_one, short_taps, long_taps, reach, carry):
    rows, width = q_one.shape
    tiles = width // LANES
    size = width // short_taps.shape[2]
    out_rows = reach + 4 * EDGE + (long_taps.size // width if carry else 0)

    def kernel(*refs):
        tail_kernel(size, reach, carry, *refs)

    inputs = [in_hbm(array) for array in (q_one, k_one, v_one, short_taps, long_taps)]
    return pl.pallas_call(
        kernel,
        in_specs=[pl.BlockSpec(memory_space=pltpu.HBM)] * 5,
        out_specs=pl.BlockSpec(memory_space=pltpu.VMEM),
        out_shape=jax.ShapeDtypeStruct((tiles, out_rows, LANES), BF16),
        scratch_shapes=[
            pltpu.VMEM((16, width), BF16),
            pltpu.VMEM((reach + 16, width), BF16),
            pltpu.VMEM((reach + 16, width), BF16),
            pltpu.VMEM(short_taps.shape, BF16),
            pltpu.VMEM(long_taps.shape, BF16),
            pltpu.VMEM((tiles, 2, reach + 16, LANES), F32),
            pltpu.SemaphoreType.DMA((tiles // TAIL_TILES, 4)),
        ],
        compiler_params=params(),
        name="tails",
    )(*inputs)


def route_kernel(source_ref, spread_ref, out_ref):
    kept = out_ref.shape[1]
    for d in range(out_ref.shape[0]):
        out_ref[d] = spread_ref[source_ref[d], :kept, :]


def call_route(source, spread, kept):
    count, _, lanes = spread.shape
    return pl.pallas_call(
        route_kernel,
        in_specs=[
            pl.BlockSpec(memory_space=pltpu.SMEM),
            pl.BlockSpec(memory_space=pltpu.VMEM),
        ],
        out_specs=pl.BlockSpec(memory_space=pltpu.VMEM),
        out_shape=jax.ShapeDtypeStruct((count, kept, lanes), BF16),
        compiler_params=params(),
        name="route",
    )(source, spread)


def shifted_rows(row, count):
    return pltpu.roll(jnp.broadcast_to(row, (count, row.shape[1])), 0, 1, stride=1, stride_axis=0)


def medium_rows(medium_taps, rows):
    reach = medium_taps.shape[0]
    base = jnp.pad(jnp.transpose(medium_taps[::-1]), ((0, 0), (1, rows - reach - 1)))
    return base.astype(F32)


def long_windows(long_rows, rows, lags):
    groups, length = long_rows.shape
    reach = lags * rows
    padded = jnp.pad(long_rows.astype(F32), ((0, 0), (rows, 0)))
    pieces = [padded[:, p : p + reach + rows] for p in range(0, length, reach)]
    return jnp.stack(pieces, axis=1).reshape(-1, reach + rows)


def mix_kernel(
    size,
    keep_ref,
    q_ref,
    k_ref,
    v_ref,
    gate_ref,
    halo_ref,
    taps_ref,
    base_ref,
    out_ref,
    energy_ref,
    extended_ref,
):
    rows, width = q_ref.shape
    tiles = width // LANES
    groups = LANES // size
    reach = rows // 2
    keep = keep_ref[0:1, :]
    taps = [lane_taps(taps_ref, which, size, width) for which in range(3)]
    lane_group = lax.broadcasted_iota(jnp.int32, (1, 2 * LANES), 1) % LANES // size

    def short(t):
        lanes = slice(t * LANES, (t + 1) * LANES)
        edges = halo_ref[t, reach:, :].astype(F32) * keep

        def feature(ref, which):
            extended_ref[t, which, :EDGE] = edges[which * EDGE : (which + 1) * EDGE]
            extended_ref[t, which, EDGE:] = ref[:, lanes].astype(F32)
            return short_filter(extended_ref.at[t, which], taps[which][:, lanes], EDGE, rows)

        z_own = (feature(k_ref, 1) * feature(v_ref, 2)).astype(BF16)
        z_halo = (halo_ref[t, :reach, :].astype(F32) * keep).astype(BF16)
        window = jnp.concatenate([jnp.concatenate([z_halo, z_own[:reach]], axis=0), z_own], axis=1)
        return feature(q_ref, 0), window

    squares = jnp.zeros((rows, LANES), F32)
    ready = [short(t) for t in range(MIX_AHEAD)]
    for t in range(tiles):
        if t + MIX_AHEAD < tiles:
            ready.append(short(t + MIX_AHEAD))
        q_feat, window = ready[t]
        table = jnp.concatenate(
            [
                shifted_rows(base_ref[g : g + 1, :], reach).astype(BF16)
                for g in range(t * groups, (t + 1) * groups)
            ],
            axis=0,
        )
        every = jnp.dot(table, window, preferred_element_type=F32)
        medium = every[:reach]
        for g in range(1, groups):
            medium = jnp.where(lane_group == g, every[g * reach : (g + 1) * reach], medium)
        mixed = q_feat * jnp.concatenate([medium[:, :LANES], medium[:, LANES:]], axis=0)
        gate = gate_ref[:, t * LANES : (t + 1) * LANES].astype(F32)
        out_ref[t] = jnp.transpose(mixed * gate)
        squares = squares + mixed * mixed
    energy_ref[...] = jnp.sum(jnp.transpose(squares), axis=0, keepdims=True)


def call_mix(keep, q_one, k_one, v_one, k_two, halo, short_taps, medium_base):
    rows, width = q_one.shape
    size = width // short_taps.shape[2]

    def kernel(*refs):
        mix_kernel(size, *refs)

    return pl.pallas_call(
        kernel,
        in_specs=[pl.BlockSpec(memory_space=pltpu.VMEM)] * 8,
        out_specs=[pl.BlockSpec(memory_space=pltpu.VMEM)] * 2,
        out_shape=[
            jax.ShapeDtypeStruct((width // LANES, LANES, rows), F32),
            jax.ShapeDtypeStruct((1, rows), F32),
        ],
        scratch_shapes=[pltpu.VMEM((width // LANES, 3, EDGE + rows, LANES), F32)],
        compiler_params=params(),
        name="mix",
    )(keep, q_one, k_one, v_one, k_two, halo, short_taps, medium_base)


def long_kernel(size, holder_ref, value_ref, window_ref, gain_ref, out_ref, ordered_ref):
    blocks, channels, rows = value_ref.shape
    half = rows // 2
    lags = window_ref.shape[1] // rows - 1
    pieces = blocks // lags
    reach = blocks * size
    holders = [holder_ref[b] for b in range(blocks)]
    for g in range(channels // size):
        here = slice(g * size, (g + 1) * size)
        ordered_ref[g, :reach] = jnp.zeros((reach, rows), BF16)
        for b, holder in enumerate(holders):
            ordered_ref[g, reach + b * size : reach + (b + 1) * size] = value_ref[holder, here]
    for g in range(channels // size):
        here = slice(g * size, (g + 1) * size)
        total = ordered_ref[g, reach:].astype(F32) * jnp.concatenate([gain_ref[here]] * blocks, axis=0)
        for p in range(pieces):
            slot = g * pieces + p
            left = jnp.concatenate(
                [
                    ordered_ref[g, (blocks - lag) * size : (2 * blocks - lag) * size]
                    for lag in range(p * lags, (p + 1) * lags)
                ],
                axis=1,
            )
            strip = shifted_rows(window_ref[slot : slot + 1, :], half).astype(BF16)
            right = jnp.concatenate(
                [
                    strip[:, shift : shift + rows]
                    for lag in range(1, lags + 1)
                    for shift in (lag * rows, lag * rows - half)
                ],
                axis=0,
            )
            total = total + jnp.dot(left, right, preferred_element_type=F32)
        for b, holder in enumerate(holders):
            out_ref[holder, here] = total[b * size : (b + 1) * size].astype(BF16)


def call_long(holder, values, windows, gain, size):
    blocks, channels, rows = values.shape

    def kernel(*refs):
        long_kernel(size, *refs)

    return pl.pallas_call(
        kernel,
        in_specs=[
            pl.BlockSpec(memory_space=pltpu.SMEM),
            pl.BlockSpec(memory_space=pltpu.VMEM),
            pl.BlockSpec(memory_space=pltpu.VMEM),
            pl.BlockSpec(memory_space=pltpu.VMEM),
        ],
        out_specs=pl.BlockSpec(memory_space=pltpu.VMEM),
        out_shape=jax.ShapeDtypeStruct((blocks, channels, rows), BF16),
        scratch_shapes=[
            pltpu.VMEM((channels // size, 2 * blocks * size, rows), BF16),
        ],
        compiler_params=params(),
        name="long",
    )(holder, values, windows, gain)


def gate_kernel(mixed_ref, gate_ref, out_ref):
    for t in range(mixed_ref.shape[0]):
        lanes = slice(t * LANES, (t + 1) * LANES)
        mixed = jnp.transpose(mixed_ref[t]).astype(F32)
        out_ref[:, lanes] = (gate_ref[:, lanes].astype(F32) * mixed).astype(BF16)


def call_gate(mixed, q_two):
    rows, width = q_two.shape
    wide = GATE_TILES * LANES
    column = pl.BlockSpec((rows, wide), lambda i: (0, i))
    return pl.pallas_call(
        gate_kernel,
        grid=(width // wide,),
        in_specs=[pl.BlockSpec((GATE_TILES, LANES, rows), lambda i: (i, 0, 0)), column],
        out_specs=column,
        out_shape=jax.ShapeDtypeStruct((rows, width), BF16),
        compiler_params=params("arbitrary"),
        name="gate",
    )(mixed, q_two)


def exchange(array):
    return lax.all_to_all(array, "ctx", split_axis=0, concat_axis=0, tiled=True)


def sum_by_pairs(array, axis):
    count = lax.axis_size(axis)
    assert count & (count - 1) == 0
    bit = 1
    while bit < count:
        array = array + lax.ppermute(array, axis, [(i, i ^ bit) for i in range(count)])
        bit *= 2
    return array


def per_device(
    q_one,
    k_one,
    v_one,
    q_two,
    k_two,
    short_taps,
    medium_taps,
    long_taps,
    skip_gain,
    block_order,
    prev_owner,
):
    rows, width = q_one.shape
    ctx_count = lax.axis_size("ctx")
    tp_count = lax.axis_size("tp")
    me = lax.axis_index("ctx")
    size = width // short_taps.shape[2]
    reach = medium_taps.shape[0]
    assert rows == 2 * reach and short_taps.shape[1] <= EDGE + 1
    tiles = width // LANES
    shard = width // ctx_count
    shard_groups = shard // size
    full_width = width * tp_count

    slots = jnp.arange(ctx_count, dtype=jnp.int32)
    holder = jnp.sum(jnp.where(block_order[None, :] == slots[:, None], slots[None, :], 0), axis=1)
    source = jnp.take(prev_owner, block_order, mode="clip")
    is_first = jnp.sum(jnp.where(slots == me, block_order, 0)) == 0
    keep = jnp.broadcast_to(jnp.where(is_first, 0.0, 1.0), (EDGE, LANES)).astype(F32)

    tail_rows = reach + 4 * EDGE
    halo_rows = tiles * tail_rows // ctx_count
    carry = ctx_count == tiles
    payload = call_tails(q_one, k_one, v_one, short_taps, long_taps, reach, carry)
    if not carry:
        taps_sent = long_taps.reshape(ctx_count, shard_groups, rows // LANES, LANES)
        taps_sent = jnp.transpose(taps_sent, (0, 2, 1, 3)).reshape(ctx_count, -1, LANES)
        payload = jnp.concatenate([payload.reshape(ctx_count, halo_rows, LANES), taps_sent], axis=1)
    spread = exchange(payload)
    halo = exchange(call_route(source, spread, halo_rows))
    halo = halo.reshape(tiles, tail_rows, LANES)

    medium_base = medium_rows(medium_taps, rows)
    long_rows = spread[:, halo_rows:].reshape(ctx_count, rows // LANES, shard_groups, LANES)
    long_rows = jnp.transpose(long_rows, (2, 0, 1, 3)).reshape(shard_groups, ctx_count * rows)
    windows = long_windows(long_rows, rows, min(ctx_count, 8))

    gated, energy = call_mix(keep, q_one, k_one, v_one, k_two, halo, short_taps, medium_base)
    energy = sum_by_pairs(energy, "tp")
    scale = lax.rsqrt(energy / full_width + EPSILON)
    values = (gated * scale[None]).astype(BF16).reshape(ctx_count, shard, rows)
    values = exchange(values)

    gain = lax.dynamic_slice_in_dim(skip_gain, me * shard, shard).reshape(shard, 1)
    returned = exchange(call_long(holder, values, windows, gain, size))
    return call_gate(returned.reshape(tiles, LANES, rows), q_two)


def solution(mesh):
    in_specs = (
        P("ctx", "tp"),
        P("ctx", "tp"),
        P("ctx", "tp"),
        P("ctx", "tp"),
        P("ctx", "tp"),
        P(None, None, "tp"),
        P(None, "tp"),
        P("tp", "ctx"),
        P("tp"),
        P(),
        P(),
    )
    out_specs = P("ctx", "tp")
    return jax.shard_map(
        per_device, mesh=mesh, in_specs=in_specs, out_specs=out_specs, check_vma=False
    )
```

time: 93 us -> 84.6 us (0.910)
  waiting for transfers between devices: 21.1 us -> 35.4 us
  local copies, waits for them, and re-layouts: 15 us -> 0.98 us
  starting transfers between devices: 22.6 us -> 16.4 us
  Pallas kernels: 15.1 us -> 11.6 us
  blocking collectives: 15.9 us -> 17.3 us
    all_to_all x3, waiting for transfers between devices: 14.5 us -> 32.2 us  [exchange(): return lax.all_to_all(array, 'ctx', split_axis=0, concat_axis=0, tiled=True)]
    unnamed x34 -> x20, local copies, waits for them, and re-layouts: 12.3 us -> 0.05 us
    ppermute x5 -> x2, starting transfers between devices: 8.11 us -> 1.59 us  [sum_by_pairs(): lax.ppermute(array, axis, [(i, i ^ bit) for i in range(count)])]
    ppermute x5 -> x2, waiting for transfers between devices: 6.6 us -> 3.17 us  [sum_by_pairs(): lax.ppermute(array, axis, [(i, i ^ bit) for i in range(count)])]
    pallas_call x3 -> x1, Pallas kernels: 5.43 us -> 2.46 us  [call_long(): pl.pallas_call(kernel, in_specs=[pl.BlockSpec(memory_space=pltpu.SMEM), p...]
    all_to_all x1, blocking collectives: 15.9 us -> 17.3 us  [exchange(): return lax.all_to_all(array, 'ctx', split_axis=0, concat_axis=0, tiled=True)]
    convert_element_type x0 -> x2, other arithmetic: none -> 0.97 us  [the longest x1 0.89 us: per_device(): values = (gated * scale[None]).astype(BF16).reshape(ctx_count, shard, rows)]
  transfers between devices with their start and end apart: 8 -> 5, of which waited for: 5 -> 5; matrix products, arithmetic and copies ran while one was open for 4% -> 2% of each run, Pallas kernels for 4% -> 0%
where the time goes in v4:
time: 84.6 us; the launch traced here: 84.1 us
  waiting for transfers between devices  35.4 us (42%)
  blocking collectives  17.3 us (20%)
  starting transfers between devices  16.4 us (19%)
  Pallas kernels  11.6 us (14%)
  other arithmetic  1.75 us (2%)
  local copies, waits for them, and re-layouts  0.98 us (1%)
    all_to_all x3, waiting for transfers between devices, exchange(): return lax.all_to_all(array, 'ctx', split_axis=0, concat_axis=0, tiled=True)  32.2 us
    all_to_all x1, blocking collectives, exchange(): return lax.all_to_all(array, 'ctx', split_axis=0, concat_axis=0, tiled=True)  17.3 us
    all_to_all x3, starting transfers between devices, exchange(): return lax.all_to_all(array, 'ctx', split_axis=0, concat_axis=0, tiled=True)  14.8 us
    pallas_call x1, Pallas kernels, call_mix(): pl.pallas_call(kernel, in_specs=[pl.BlockSpec(memory_space=pltpu.VMEM)] *...  4.31 us
    ppermute x2, waiting for transfers between devices, sum_by_pairs(): lax.ppermute(array, axis, [(i, i ^ bit) for i in range(count)])  3.17 us
    pallas_call x1, Pallas kernels, call_tails(): pl.pallas_call(kernel, in_specs=[pl.BlockSpec(memory_space=pltpu.HBM)] *...  2.47 us
    pallas_call x1, Pallas kernels, call_long(): pl.pallas_call(kernel, in_specs=[pl.BlockSpec(memory_space=pltpu.SMEM), p...  2.46 us
  transfers between devices with their start and end apart: 5, of which 5 were waited for; matrix products, arithmetic and copies ran while one was open for 2% of the time, Pallas kernels for 0%

profile of v4, /device:TPU:0, one launch (start us, length us, event | category | flops | bytes accessed | tf_op | source)
XLA Modules:
  0.0 84.1 jit_solution(2961997631547096743)
XLA Ops:
  0.0 0.0 copy-start
  0.0 2.5 %tails.1 = bf16[8,176,128]{2,1,0:T(8,128)(2,1)} custom-call(bf16[256,1024]{1,0:T(8,128)(2,1)} %refs_1_.3, bf16[256,1024]{1,0:T(8,128)(2,1)} %refs_2_.3, bf16[256,1024]{1,0:T(8,128)(2,1)} %refs_3_.3, bf16[3,7,64]{2,1,0:T(8,128)(2,1)} %refs_6_.1, bf16[64,256]{1,0:T(8,128)(2,1)} %refs_4_.2), custom_call_target="tpu_custom_call" | custom-call | tf_op jit(solution)/shard_map/tails/pallas_call | solution.py:116
  2.5 0.0 copy-start.9
  2.5 0.0 copy-start.7
  2.5 0.0 copy-start.5
  2.5 7.4 %all-to-all-start = ((bf16[8,176,128]{2,1,0:T(8,128)(2,1)}), bf16[8,176,128]{2,1,0:T(8,128)(2,1)S(1)}, u32[]{:S(2)}, u32[]{:S(2)}) async-start(bf16[8,176,128]{2,1,0:T(8,128)(2,1)} %tails.1), calls=%async_computation | async-start | bytes 720896 | tf_op jit(solution)/shard_map/all_to_all | solution.py:340
  9.9 0.0 copy-done.9
  9.9 0.0 copy-done.7
  9.9 0.0 copy-start.3
  10.0 0.6 gather_fusion
  10.6 10.3 %all-to-all-done.spread_ref = bf16[8,176,128]{2,1,0:T(8,128)(2,1)S(1)} async-done(((bf16[8,176,128]{2,1,0:T(8,128)(2,1)}), bf16[8,176,128]{2,1,0:T(8,128)(2,1)S(1)}, u32[]{:S(2)}, u32[]{:S(2)}) %all-to-all-start) | async-done | bytes 360480 | tf_op jit(solution)/shard_map/all_to_all | solution.py:340
  20.9 0.0 copy-start.2
  20.9 1.3 %route.1 = bf16[8,160,128]{2,1,0:T(8,128)(2,1)} custom-call(s32[8]{0:T(128)S(1)} %gather_fusion, bf16[8,176,128]{2,1,0:T(8,128)(2,1)S(1)} %all-to-all-done.spread_ref), custom_call_target="tpu_custom_call" | custom-call | tf_op jit(solution)/shard_map/route/pallas_call | solution.py:143
  22.2 0.0 copy-start.8
  22.2 0.0 copy-start.1
  22.2 3.7 %all-to-all-start.1 = ((bf16[8,160,128]{2,1,0:T(8,128)(2,1)}), bf16[8,160,128]{2,1,0:T(8,128)(2,1)S(1)}, u32[]{:S(2)}, u32[]{:S(2)}) async-start(bf16[8,160,128]{2,1,0:T(8,128)(2,1)} %route.1), calls=%async_computation.1 | async-start | bytes 655360 | tf_op jit(solution)/shard_map/all_to_all | solution.py:340
  26.0 0.0 copy-done.8
  26.0 0.1 rev.3
  26.0 0.6 fusion
  27.3 0.0 copy-start.6
  27.3 0.1 pad_convert_fusion.1.refs_7_
  27.3 8.4 %all-to-all-done.1.refs_5_ = bf16[8,160,128]{2,1,0:T(8,128)(2,1)S(1)} async-done(((bf16[8,160,128]{2,1,0:T(8,128)(2,1)}), bf16[8,160,128]{2,1,0:T(8,128)(2,1)S(1)}, u32[]{:S(2)}, u32[]{:S(2)}) %all-to-all-start.1) | async-done | bytes 327712 | tf_op jit(solution)/shard_map/all_to_all | solution.py:340
  35.7 0.0 copy-done.5
  35.8 0.0 copy-done.3
  35.8 0.0 copy-done.2
  35.8 0.0 copy-done.1
  35.8 0.0 copy-done.6
  35.8 4.3 %mix.1 = (f32[8,128,256]{2,1,0:T(8,128)S(1)}, f32[1,256]{1,0:T(1,128)S(1)}) custom-call(f32[8,128]{1,0:T(8,128)S(1)} %broadcast_in_dim.30.refs_0_, bf16[256,1024]{1,0:T(8,128)(2,1)S(1)} %copy-done.1, bf16[256,1024]{1,0:T(8,128)(2,1)S(1)} %copy-done.2, bf16[256,1024]{1,0:T(8,128)(2,1)S(1)} %copy-done.3, bf16[256,1024]{1,0:T(8,128)(2,1)S(1)} %copy-done.5, ...), custom_call_target="tpu_custom_call" | custom-call | tf_op jit(solution)/shard_map/mix/pallas_call | solution.py:241
  40.1 0.1 collective-permute-start
  40.2 1.1 %collective-permute-done = f32[1,256]{1,0:T(1,128)S(1)} collective-permute-done((f32[1,256]{1,0:T(1,128)S(1)}, f32[1,256]{1,0:T(1,128)S(1)}, u32[]{:S(2)}, u32[]{:S(2)}) %collective-permute-start) | collective-permute-done | bytes 1056 | tf_op jit(solution)/shard_map/ppermute | solution.py:348
  41.3 1.5 %collective-permute-start.1 = (f32[1,256]{1,0:T(1,128)S(1)}, f32[1,256]{1,0:T(1,128)S(1)}, u32[]{:S(2)}, u32[]{:S(2)}) collective-permute-start(f32[1,256]{1,0:T(1,128)S(1)} %add.19), channel_id=1, source_target_pairs={{0,2},{1,3},{2,0},{3,1},{4,6},{5,7},{6,4},{7,5},{8,10},{9,11},{10,... | collective-permute-start | bytes 3080 | tf_op jit(solution)/shard_map/ppermute | solution.py:348
  42.8 2.0 %collective-permute-done.1 = f32[1,256]{1,0:T(1,128)S(1)} collective-permute-done((f32[1,256]{1,0:T(1,128)S(1)}, f32[1,256]{1,0:T(1,128)S(1)}, u32[]{:S(2)}, u32[]{:S(2)}) %collective-permute-start.1) | collective-permute-done | bytes 1056 | tf_op jit(solution)/shard_map/ppermute | solution.py:348
  44.9 0.9 %multiply_convert_fusion = bf16[8,128,256]{2,1,0:T(8,128)(2,1)} fusion(f32[8,128,256]{2,1,0:T(8,128)S(1)} %get-tuple-element.7, f32[256]{0:T(256)S(1)} %bitcast.11), kind=kLoop, calls=%fused_computation.1 | loop fusion | flops 524288 | bytes 1573888 | tf_op jit(solution)/shard_map/convert_element_type | solution.py:404
  45.8 3.6 %all-to-all-start.2 = ((bf16[8,128,256]{2,1,0:T(8,128)(2,1)}), bf16[8,128,256]{2,1,0:T(8,128)(2,1)S(1)}, u32[]{:S(2)}, u32[]{:S(2)}) async-start(bf16[8,128,256]{2,1,0:T(8,128)(2,1)} %multiply_convert_fusion), calls=%async_computation.2 | async-start | bytes 1048576 | tf_op jit(solution)/shard_map/all_to_all | solution.py:340
  49.4 0.0 copy-done
  49.4 0.1 dynamic-slice_bitcast_fusion
  49.5 0.1 copy.14.refs_3_
  49.6 0.1 select_reduce_fusion.refs_0_
  49.7 13.5 %all-to-all-done.2.refs_1_ = bf16[8,128,256]{2,1,0:T(8,128)(2,1)S(1)} async-done(((bf16[8,128,256]{2,1,0:T(8,128)(2,1)}), bf16[8,128,256]{2,1,0:T(8,128)(2,1)S(1)}, u32[]{:S(2)}, u32[]{:S(2)}) %all-to-all-start.2) | async-done | bytes 524320 | tf_op jit(solution)/shard_map/all_to_all | solution.py:340
  63.2 2.5 %long.1 = bf16[8,128,256]{2,1,0:T(8,128)(2,1)S(1)} custom-call(s32[8]{0:T(128)S(1)} %select_reduce_fusion.refs_0_, bf16[8,128,256]{2,1,0:T(8,128)(2,1)S(1)} %all-to-all-done.2.refs_1_, f32[8,2304]{1,0:T(8,128)S(1)} %pad_convert_fusion.refs_2_, f32[128,1]{1,0:T(8,128)S(1)} %copy.14.refs_3_), custom_call_target="tpu_custom_call" | custom-call | tf_op jit(solution)/shard_map/long/pallas_call | solution.py:299
  65.7 0.0 copy-start.4
  65.7 17.3 %all_to_all.20.mixed_ref = bf16[8,128,256]{2,1,0:T(8,128)(2,1)S(1)} all-to-all(bf16[8,128,256]{2,1,0:T(8,128)(2,1)S(1)} %long.1), channel_id=1, replica_groups=mesh['ctx'=8,'tp'=4] {'ctx'}, dimensions={0} | all-to-all | bytes 1048576 | tf_op jit(solution)/shard_map/all_to_all | solution.py:340
  83.0 0.0 copy-done.4
  83.0 1.0 %gate.1 = bf16[256,1024]{1,0:T(8,128)(2,1)} custom-call(bf16[8,128,256]{2,1,0:T(8,128)(2,1)S(1)} %all_to_all.20.mixed_ref, bf16[256,1024]{1,0:T(8,128)(2,1)S(1)} %copy-done.4), custom_call_target="tpu_custom_call" | custom-call | tf_op jit(solution)/shard_map/gate/pallas_call | solution.py:328
  (6 shorter events, 0.0 us)
Async XLA Ops:
  0.0 49.4 %copy-start = (f32[1024]{0:T(1024)S(1)}, f32[1024]{0:T(1024)}, u32[]{:S(2)}) copy-start(f32[1024]{0:T(1024)} %param.19) | copy-start | bytes 12292
  2.5 7.4 %copy-start.9 = (s32[8]{0:T(128)S(1)}, s32[8]{0:T(128)}, u32[]{:S(2)}) copy-start(s32[8]{0:T(128)} %param.20) | copy-start | bytes 100
  2.5 7.4 %copy-start.7 = (s32[8]{0:T(128)S(1)}, s32[8]{0:T(128)}, u32[]{:S(2)}) copy-start(s32[8]{0:T(128)} %param.21) | copy-start | bytes 100
  2.5 33.2 %copy-start.5 = (bf16[256,1024]{1,0:T(8,128)(2,1)S(1)}, bf16[256,1024]{1,0:T(8,128)(2,1)}, u32[]{:S(2)}) copy-start(bf16[256,1024]{1,0:T(8,128)(2,1)} %refs_4_.3) | copy-start | bytes 1572868
  2.5 18.4 %all-to-all-start = ((bf16[8,176,128]{2,1,0:T(8,128)(2,1)}), bf16[8,176,128]{2,1,0:T(8,128)(2,1)S(1)}, u32[]{:S(2)}, u32[]{:S(2)}) async-start(bf16[8,176,128]{2,1,0:T(8,128)(2,1)} %tails.1), calls=%async_computation | async-start | bytes 720896 | tf_op jit(solution)/shard_map/all_to_all | solution.py:340
  9.9 25.8 %copy-start.3 = (bf16[256,1024]{1,0:T(8,128)(2,1)S(1)}, bf16[256,1024]{1,0:T(8,128)(2,1)}, u32[]{:S(2)}) copy-start(bf16[256,1024]{1,0:T(8,128)(2,1)} %refs_3_.3) | copy-start | bytes 1572868
  20.9 14.8 %copy-start.2 = (bf16[256,1024]{1,0:T(8,128)(2,1)S(1)}, bf16[256,1024]{1,0:T(8,128)(2,1)}, u32[]{:S(2)}) copy-start(bf16[256,1024]{1,0:T(8,128)(2,1)} %refs_2_.3) | copy-start | bytes 1572868
  22.2 3.7 %copy-start.8 = (bf16[128,64]{0,1:T(8,128)(2,1)S(1)}, bf16[128,64]{0,1:T(8,128)(2,1)}, u32[]{:S(2)}) copy-start(bf16[128,64]{0,1:T(8,128)(2,1)} %param.17) | copy-start | bytes 49156
  22.2 13.5 %copy-start.1 = (bf16[256,1024]{1,0:T(8,128)(2,1)S(1)}, bf16[256,1024]{1,0:T(8,128)(2,1)}, u32[]{:S(2)}) copy-start(bf16[256,1024]{1,0:T(8,128)(2,1)} %refs_1_.3) | copy-start | bytes 1572868
  22.2 13.5 %all-to-all-start.1 = ((bf16[8,160,128]{2,1,0:T(8,128)(2,1)}), bf16[8,160,128]{2,1,0:T(8,128)(2,1)S(1)}, u32[]{:S(2)}, u32[]{:S(2)}) async-start(bf16[8,160,128]{2,1,0:T(8,128)(2,1)} %route.1), calls=%async_computation.1 | async-start | bytes 655360 | tf_op jit(solution)/shard_map/all_to_all | solution.py:340
  27.3 8.5 %copy-start.6 = (bf16[3,7,64]{2,1,0:T(8,128)(2,1)S(1)}, bf16[3,7,64]{2,1,0:T(8,128)(2,1)}, u32[]{:S(2)}) copy-start(bf16[3,7,64]{2,1,0:T(8,128)(2,1)} %refs_6_.1) | copy-start | bytes 8068
  40.1 1.2 %collective-permute-start = (f32[1,256]{1,0:T(1,128)S(1)}, f32[1,256]{1,0:T(1,128)S(1)}, u32[]{:S(2)}, u32[]{:S(2)}) collective-permute-start(f32[1,256]{1,0:T(1,128)S(1)} %get-tuple-element.8), channel_id=1, source_target_pairs={{0,1},{1,0},{2,3},{3,2},{4,5},{5,4},{6,7},{7,6},{8,9},{9,8},{10,11... | collective-permute-start | bytes 3080 | tf_op jit(solution)/shard_map/ppermute | solution.py:348
  41.3 3.6 %collective-permute-start.1 = (f32[1,256]{1,0:T(1,128)S(1)}, f32[1,256]{1,0:T(1,128)S(1)}, u32[]{:S(2)}, u32[]{:S(2)}) collective-permute-start(f32[1,256]{1,0:T(1,128)S(1)} %add.19), channel_id=1, source_target_pairs={{0,2},{1,3},{2,0},{3,1},{4,6},{5,7},{6,4},{7,5},{8,10},{9,11},{10,... | collective-permute-start | bytes 3080 | tf_op jit(solution)/shard_map/ppermute | solution.py:348
  45.8 17.4 %all-to-all-start.2 = ((bf16[8,128,256]{2,1,0:T(8,128)(2,1)}), bf16[8,128,256]{2,1,0:T(8,128)(2,1)S(1)}, u32[]{:S(2)}, u32[]{:S(2)}) async-start(bf16[8,128,256]{2,1,0:T(8,128)(2,1)} %multiply_convert_fusion), calls=%async_computation.2 | async-start | bytes 1048576 | tf_op jit(solution)/shard_map/all_to_all | solution.py:340
  65.7 17.3 %copy-start.4 = (bf16[256,1024]{1,0:T(8,128)(2,1)S(1)}, bf16[256,1024]{1,0:T(8,128)(2,1)}, u32[]{:S(2)}) copy-start(bf16[256,1024]{1,0:T(8,128)(2,1)} %gate_ref.1) | copy-start | bytes 1572868

commit v5 on v4

v5 whole, which is shorter than its diff:
```python
import jax
import jax.numpy as jnp
from jax import lax
from jax.experimental import pallas as pl
from jax.experimental.pallas import tpu as pltpu
from jax.sharding import PartitionSpec as P

EPSILON = 1e-06
LANES = 128
EDGE = 8
VMEM_BYTES = 24 * 1024 * 1024
PACK_TILES = 2
GATE_TILES = 4
F32 = jnp.float32
BF16 = jnp.bfloat16


def params(*semantics):
    return pltpu.CompilerParams(dimension_semantics=semantics, vmem_limit_bytes=VMEM_BYTES)


def in_hbm(array):
    return pltpu.with_memory_space_constraint(array, pltpu.HBM)


def lane_taps(taps_ref, which, size, width, first=0):
    groups = taps_ref.shape[2]
    group = lax.broadcasted_iota(jnp.int32, (groups, width), 0)
    lane = lax.broadcasted_iota(jnp.int32, (groups, width), 1) + first
    spread = (group == lane // size).astype(BF16)
    return jnp.dot(taps_ref[which], spread, preferred_element_type=F32)


def short_filter(extended, taps, start, rows):
    total = extended[start : start + rows] * taps[0:1]
    for j in range(1, taps.shape[0]):
        total = total + extended[start - j : start - j + rows] * taps[j : j + 1]
    return total


def pack_kernel(
    size, q_hbm, k_hbm, v_hbm, taps_hbm, long_hbm, out_ref, q_ref, k_ref, v_ref, taps_ref, long_ref, wide_ref, sems
):
    rows, width = q_hbm.shape
    tiles = width // LANES
    wide = PACK_TILES * LANES
    groups = LANES // size
    taps_copy = pltpu.make_async_copy(taps_hbm, taps_ref, sems.at[0, 3])
    taps_copy.start()
    parts = []
    for p in range(width // wide):
        lanes = pl.ds(p * wide, wide)
        copies = [
            pltpu.make_async_copy(source.at[:, lanes], target.at[:, lanes], sems.at[p, which])
            for which, (source, target) in enumerate(((k_hbm, k_ref), (v_hbm, v_ref), (q_hbm, q_ref)))
        ]
        for copy in copies:
            copy.start()
        parts.append(copies)
    long_copy = pltpu.make_async_copy(long_hbm, long_ref, sems.at[1, 3])
    long_copy.start()
    taps_copy.wait()
    taps = [lane_taps(taps_ref, which, size, width) for which in (1, 2)]
    for t in range(tiles):
        if t % PACK_TILES == 0:
            for copy in parts[t // PACK_TILES]:
                copy.wait()
        lanes = slice(t * LANES, (t + 1) * LANES)
        out_ref[t, :LANES, :] = jnp.transpose(q_ref[:, lanes])
        features = []
        for which, ref in enumerate((k_ref, v_ref)):
            wide_ref[t, which, :EDGE] = jnp.zeros((EDGE, LANES), F32)
            wide_ref[t, which, EDGE:] = ref[:, lanes].astype(F32)
            features.append(short_filter(wide_ref.at[t, which], taps[which][:, lanes], EDGE, rows))
            ends = [wide_ref[t, which, EDGE : 2 * EDGE], wide_ref[t, which, rows : rows + EDGE]]
            out_ref[t, 2 * LANES : 2 * LANES + 2 * EDGE, which * LANES : (which + 1) * LANES] = (
                jnp.concatenate(ends, axis=0).astype(BF16)
            )
        out_ref[t, LANES : 2 * LANES, :] = jnp.transpose((features[0] * features[1]).astype(BF16))
    long_copy.wait()
    for t in range(tiles):
        here = long_ref[t * groups : (t + 1) * groups, :].astype(F32)
        filler = jnp.zeros((2 * EDGE - groups, rows), F32)
        out_ref[t, 2 * LANES + 2 * EDGE :, :] = jnp.concatenate([here, filler], axis=0).astype(BF16)


def call_pack(q_one, k_one, v_one, short_taps, long_taps):
    rows, width = q_one.shape
    tiles = width // LANES
    size = width // short_taps.shape[2]
    assert rows == 2 * LANES and LANES // size <= 2 * EDGE

    def kernel(*refs):
        pack_kernel(size, *refs)

    inputs = [in_hbm(array) for array in (q_one, k_one, v_one, short_taps, long_taps)]
    return pl.pallas_call(
        kernel,
        in_specs=[pl.BlockSpec(memory_space=pltpu.HBM)] * 5,
        out_specs=pl.BlockSpec(memory_space=pltpu.VMEM),
        out_shape=jax.ShapeDtypeStruct((tiles, 2 * LANES + 4 * EDGE, rows), BF16),
        scratch_shapes=[
            pltpu.VMEM((rows, width), BF16),
            pltpu.VMEM((rows, width), BF16),
            pltpu.VMEM((rows, width), BF16),
            pltpu.VMEM(short_taps.shape, BF16),
            pltpu.VMEM(long_taps.shape, BF16),
            pltpu.VMEM((tiles, 2, EDGE + rows, LANES), F32),
            pltpu.SemaphoreType.DMA((tiles // PACK_TILES, 4)),
        ],
        compiler_params=params(),
        name="pack",
    )(*inputs)


def turn_kernel(in_ref, out_ref):
    for t in range(out_ref.shape[0]):
        out_ref[t] = jnp.transpose(in_ref[:, t * LANES : (t + 1) * LANES])


def call_turn(array):
    rows, width = array.shape
    wide = GATE_TILES * LANES
    return pl.pallas_call(
        turn_kernel,
        grid=(width // wide,),
        in_specs=[pl.BlockSpec((rows, wide), lambda i: (0, i))],
        out_specs=pl.BlockSpec((GATE_TILES, LANES, rows), lambda i: (i, 0, 0)),
        out_shape=jax.ShapeDtypeStruct((width // LANES, LANES, rows), BF16),
        compiler_params=params("arbitrary"),
        name="turn",
    )(array)


def shifted_rows(row, count):
    return pltpu.roll(jnp.broadcast_to(row, (count, row.shape[1])), 0, 1, stride=1, stride_axis=0)


def long_windows(long_rows, rows, lags):
    groups, length = long_rows.shape
    reach = lags * rows
    padded = jnp.pad(long_rows.astype(F32), ((0, 0), (rows, 0)))
    pieces = [padded[:, p : p + reach + rows] for p in range(0, length, reach)]
    return jnp.stack(pieces, axis=1).reshape(-1, reach + rows)


def mix_kernel(
    size, holder_ref, moved_ref, ends_ref, taps_ref, column_ref, base_ref, out_ref, energy_ref, extended_ref, squares_ref
):
    blocks, shard, rows = out_ref.shape
    halves = rows // LANES
    span = 2 * EDGE
    holders = [holder_ref[b] for b in range(blocks)]
    ends = [ends_ref[holder, -span:, :].astype(F32) for holder in holders]

    features = []
    for which in range(2):
        lanes = slice(which * shard, (which + 1) * shard)
        extended_ref[which, :EDGE] = jnp.zeros((EDGE, shard), F32)
        for b in range(blocks):
            before = ends[b - 1][EDGE:, lanes] if b else jnp.zeros((EDGE, shard), F32)
            at = EDGE + b * span
            extended_ref[which, at : at + span] = jnp.concatenate([before, ends[b][:EDGE, lanes]], axis=0)
        features.append(
            short_filter(extended_ref.at[which], taps_ref[which + 1], EDGE, blocks * span)
        )
    starts = jnp.transpose((features[0] * features[1]).astype(BF16).astype(F32))
    wide = blocks * span
    lane = lax.broadcasted_iota(jnp.int32, (size, LANES), 1)

    squares_ref[...] = jnp.zeros(squares_ref.shape, F32)
    for g in range(shard // size):
        here = slice(g * size, (g + 1) * size)
        z_there = slice(shard + g * size, shard + (g + 1) * size)
        q_seq = [jnp.zeros((size, LANES), F32)]
        z_seq = [jnp.zeros((size, LANES), BF16)]
        for b, holder in enumerate(holders):
            q_seq.append(moved_ref[holder, here, :].astype(F32))
            z_block = moved_ref[holder, z_there, :]
            first = pltpu.roll(starts[here], (wide - b * span - EDGE) % wide, 1)[:, :LANES]
            z_first = jnp.where(lane < EDGE, first, z_block[:, :LANES].astype(F32)).astype(BF16)
            z_seq.append(jnp.concatenate([z_first, z_block[:, LANES:]], axis=1))
        q_seq = jnp.concatenate(q_seq, axis=1)
        z_seq = jnp.concatenate(z_seq, axis=1)
        q_feat = q_seq * column_ref[here, 0:1]
        for j in range(1, taps_ref.shape[1]):
            q_feat = q_feat + pltpu.roll(q_seq, j, 1) * column_ref[here, j : j + 1]
        table = shifted_rows(base_ref[g : g + 1, :], 2 * LANES)[:, :LANES].astype(BF16)
        windows = [z_seq[:, o * LANES : (o + 2) * LANES] for o in range(blocks * halves)]
        medium = jnp.dot(jnp.concatenate(windows, axis=0), table, preferred_element_type=F32)
        for o in range(blocks * halves):
            mixed = q_feat[:, (o + 1) * LANES : (o + 2) * LANES] * medium[o * size : (o + 1) * size]
            at = (o % halves) * LANES
            out_ref[o // halves, here, at : at + LANES] = mixed
            squares_ref[o] += mixed * mixed
    energy_ref[...] = jnp.sum(squares_ref[...], axis=1)


def call_mix(holder, moved, ends, short_local, medium_local, shard, rows):
    blocks = moved.shape[0]
    size = shard // medium_local.shape[1]
    reach = medium_local.shape[0]
    assert reach == LANES and short_local.shape[1] <= EDGE + 1
    lane_form = jnp.repeat(short_local, size, axis=2).astype(F32)
    base = jnp.pad(jnp.transpose(medium_local).astype(F32), ((0, 0), (LANES, 0)))

    def kernel(*refs):
        mix_kernel(size, *refs)

    return pl.pallas_call(
        kernel,
        in_specs=[pl.BlockSpec(memory_space=pltpu.SMEM)]
        + [pl.BlockSpec(memory_space=pltpu.VMEM)] * 5,
        out_specs=[pl.BlockSpec(memory_space=pltpu.VMEM)] * 2,
        out_shape=[
            jax.ShapeDtypeStruct((blocks, shard, rows), F32),
            jax.ShapeDtypeStruct((blocks * rows // LANES, LANES), F32),
        ],
        scratch_shapes=[
            pltpu.VMEM((2, EDGE + blocks * 2 * EDGE, shard), F32),
            pltpu.VMEM((blocks * rows // LANES, size, LANES), F32),
        ],
        compiler_params=params(),
        name="mix",
    )(holder, moved, ends, lane_form, jnp.transpose(lane_form[0]), base)


def long_kernel(
    full_width, size, holder_ref, mixed_ref, key_ref, energy_ref, window_ref, gain_ref, out_ref, ordered_ref
):
    blocks, shard, rows = mixed_ref.shape
    half = rows // 2
    halves = rows // LANES
    lags = window_ref.shape[1] // rows - 1
    pieces = blocks // lags
    reach = blocks * size
    holders = [holder_ref[b] for b in range(blocks)]
    scale = lax.rsqrt(energy_ref[...] / full_width + EPSILON)
    for b, holder in enumerate(holders):
        line = jnp.concatenate([scale[o : o + 1] for o in range(b * halves, (b + 1) * halves)], axis=1)
        for g in range(shard // size):
            here = slice(g * size, (g + 1) * size)
            value = key_ref[holder, here].astype(F32) * mixed_ref[b, here] * line
            ordered_ref[g, reach + b * size : reach + (b + 1) * size] = value.astype(BF16)
    for g in range(shard // size):
        here = slice(g * size, (g + 1) * size)
        ordered_ref[g, :reach] = jnp.zeros((reach, rows), BF16)
        total = ordered_ref[g, reach:].astype(F32) * jnp.concatenate([gain_ref[here]] * blocks, axis=0)
        for p in range(pieces):
            slot = g * pieces + p
            left = jnp.concatenate(
                [
                    ordered_ref[g, (blocks - lag) * size : (2 * blocks - lag) * size]
                    for lag in range(p * lags, (p + 1) * lags)
                ],
                axis=1,
            )
            strip = shifted_rows(window_ref[slot : slot + 1, :], half).astype(BF16)
            right = jnp.concatenate(
                [
                    strip[:, shift : shift + rows]
                    for lag in range(1, lags + 1)
                    for shift in (lag * rows, lag * rows - half)
                ],
                axis=0,
            )
            total = total + jnp.dot(left, right, preferred_element_type=F32)
        for b, holder in enumerate(holders):
            out_ref[holder, here] = total[b * size : (b + 1) * size].astype(BF16)


def call_long(holder, mixed, keys, energy, windows, gain, size, full_width):
    blocks, shard, rows = mixed.shape

    def kernel(*refs):
        long_kernel(full_width, size, *refs)

    return pl.pallas_call(
        kernel,
        in_specs=[pl.BlockSpec(memory_space=pltpu.SMEM)]
        + [pl.BlockSpec(memory_space=pltpu.VMEM)] * 5,
        out_specs=pl.BlockSpec(memory_space=pltpu.VMEM),
        out_shape=jax.ShapeDtypeStruct((blocks, shard, rows), BF16),
        scratch_shapes=[pltpu.VMEM((shard // size, 2 * blocks * size, rows), BF16)],
        compiler_params=params(),
        name="long",
    )(holder, mixed, keys, energy, windows, gain)


def gate_kernel(mixed_ref, gate_ref, out_ref):
    for t in range(mixed_ref.shape[0]):
        lanes = slice(t * LANES, (t + 1) * LANES)
        mixed = jnp.transpose(mixed_ref[t]).astype(F32)
        out_ref[:, lanes] = (gate_ref[:, lanes].astype(F32) * mixed).astype(BF16)


def call_gate(mixed, q_two):
    rows, width = q_two.shape
    wide = GATE_TILES * LANES
    column = pl.BlockSpec((rows, wide), lambda i: (0, i))
    return pl.pallas_call(
        gate_kernel,
        grid=(width // wide,),
        in_specs=[pl.BlockSpec((GATE_TILES, LANES, rows), lambda i: (i, 0, 0)), column],
        out_specs=column,
        out_shape=jax.ShapeDtypeStruct((rows, width), BF16),
        compiler_params=params("arbitrary"),
        name="gate",
    )(mixed, q_two)


def exchange(array):
    return lax.all_to_all(array, "ctx", split_axis=0, concat_axis=0, tiled=True)


def sum_by_pairs(array, axis):
    count = lax.axis_size(axis)
    assert count & (count - 1) == 0
    bit = 1
    while bit < count:
        array = array + lax.ppermute(array, axis, [(i, i ^ bit) for i in range(count)])
        bit *= 2
    return array


def per_device(
    q_one,
    k_one,
    v_one,
    q_two,
    k_two,
    short_taps,
    medium_taps,
    long_taps,
    skip_gain,
    block_order,
    prev_owner,
):
    rows, width = q_one.shape
    ctx_count = lax.axis_size("ctx")
    tp_count = lax.axis_size("tp")
    me = lax.axis_index("ctx")
    size = width // short_taps.shape[2]
    tiles = width // LANES
    tile_groups = LANES // size
    shard = width // ctx_count
    shard_groups = shard // size

    slots = jnp.arange(ctx_count, dtype=jnp.int32)
    holder = jnp.sum(jnp.where(block_order[None, :] == slots[:, None], slots[None, :], 0), axis=1)

    packed = call_pack(q_one, k_one, v_one, short_taps, long_taps)
    span = 2 * EDGE
    if ctx_count == tiles:
        moved = exchange(packed)
        taps_at = 2 * shard + span
        ends = lax.slice_in_dim(moved, 2 * shard, taps_at, axis=1)
    else:
        ends = packed[:, 2 * LANES : 2 * LANES + span].reshape(tiles, span, 2, -1, shard)
        parts = [
            packed[:, :LANES],
            packed[:, LANES : 2 * LANES],
            jnp.transpose(ends, (0, 3, 1, 2, 4)),
            packed[:, 2 * LANES + span : 2 * LANES + span + tile_groups],
        ]
        moved = exchange(
            jnp.concatenate([part.reshape(ctx_count, -1, rows) for part in parts], axis=1)
        )
        taps_at = 2 * shard + span * 2 * shard // rows
        ends = moved[:, 2 * shard : taps_at].reshape(ctx_count, span, 2 * shard)
    moved, k_two = lax.optimization_barrier((moved, k_two))
    keys = exchange(call_turn(k_two).reshape(ctx_count, shard, rows))

    short_local = lax.dynamic_slice_in_dim(short_taps, me * shard_groups, shard_groups, axis=2)
    medium_local = lax.dynamic_slice_in_dim(medium_taps, me * shard_groups, shard_groups, axis=1)
    mixed, energy = call_mix(holder, moved, ends, short_local, medium_local, shard, rows)
    energy = sum_by_pairs(sum_by_pairs(energy, "tp"), "ctx")

    long_rows = moved[:, taps_at : taps_at + shard_groups]
    long_rows = jnp.transpose(long_rows, (1, 0, 2)).reshape(shard_groups, ctx_count * rows)
    windows = long_windows(long_rows, rows, min(ctx_count, 8))
    gain = lax.dynamic_slice_in_dim(skip_gain, me * shard, shard).reshape(shard, 1)
    filtered = call_long(
        holder, mixed, keys, energy, windows, gain, size, width * tp_count
    )
    returned = exchange(filtered)
    return call_gate(returned.reshape(tiles, LANES, rows), q_two)


def solution(mesh):
    in_specs = (
        P("ctx", "tp"),
        P("ctx", "tp"),
        P("ctx", "tp"),
        P("ctx", "tp"),
        P("ctx", "tp"),
        P(None, None, "tp"),
        P(None, "tp"),
        P("tp", "ctx"),
        P("tp"),
        P(),
        P(),
    )
    out_specs = P("ctx", "tp")
    return jax.shard_map(
        per_device, mesh=mesh, in_specs=in_specs, out_specs=out_specs, check_vma=False
    )
```

time: 84.6 us -> 84.7 us (level)
  starting transfers between devices: 16.4 us -> 19.7 us
  other arithmetic: 1.75 us -> 0.22 us
  blocking collectives: 17.3 us -> 16.2 us
    ppermute x2 -> x5, starting transfers between devices: 1.59 us -> 8.71 us  [sum_by_pairs(): lax.ppermute(array, axis, [(i, i ^ bit) for i in range(count)])]
    ppermute x2 -> x5, waiting for transfers between devices: 3.17 us -> 7.3 us  [sum_by_pairs(): lax.ppermute(array, axis, [(i, i ^ bit) for i in range(count)])]
    all_to_all x3 -> x2, starting transfers between devices: 14.8 us -> 11 us  [exchange(): return lax.all_to_all(array, 'ctx', split_axis=0, concat_axis=0, tiled=True)]
    all_to_all x3 -> x2, waiting for transfers between devices: 32.2 us -> 28.5 us  [exchange(): return lax.all_to_all(array, 'ctx', split_axis=0, concat_axis=0, tiled=True)]
    all_to_all x1, blocking collectives: 17.3 us -> 16.2 us  [exchange(): return lax.all_to_all(array, 'ctx', split_axis=0, concat_axis=0, tiled=True)]
    convert_element_type x2 -> x1, other arithmetic: 0.97 us -> 0.08 us  [call_mix(): lane_form = jnp.repeat(short_local, size, axis=2).astype(F32)]
  transfers between devices with their start and end apart: 5 -> 7, of which waited for: 5 -> 6; matrix products, arithmetic and copies ran while one was open for 2% -> 2% of each run, Pallas kernels for 0% -> 3%
where the time goes in v5:
time: 84.7 us; the launch traced here: 84.4 us
  waiting for transfers between devices  35.8 us (42%)
  starting transfers between devices  19.7 us (23%)
  blocking collectives  16.2 us (19%)
  Pallas kernels  11.1 us (13%)
  local copies, waits for them, and re-layouts  1.17 us (1%)
    all_to_all x2, waiting for transfers between devices, exchange(): return lax.all_to_all(array, 'ctx', split_axis=0, concat_axis=0, tiled=True)  28.5 us
    all_to_all x1, blocking collectives, exchange(): return lax.all_to_all(array, 'ctx', split_axis=0, concat_axis=0, tiled=True)  16.2 us
    all_to_all x2, starting transfers between devices, exchange(): return lax.all_to_all(array, 'ctx', split_axis=0, concat_axis=0, tiled=True)  11 us
    ppermute x5, starting transfers between devices, sum_by_pairs(): lax.ppermute(array, axis, [(i, i ^ bit) for i in range(count)])  8.71 us
    ppermute x5, waiting for transfers between devices, sum_by_pairs(): lax.ppermute(array, axis, [(i, i ^ bit) for i in range(count)])  7.3 us
    pallas_call x1, Pallas kernels, call_pack(): pl.pallas_call(kernel, in_specs=[pl.BlockSpec(memory_space=pltpu.HBM)] *...  3.82 us
    pallas_call x1, Pallas kernels, call_mix(): pl.pallas_call(kernel, in_specs=[pl.BlockSpec(memory_space=pltpu.SMEM)] +...  2.73 us
    pallas_call x1, Pallas kernels, call_long(): pl.pallas_call(kernel, in_specs=[pl.BlockSpec(memory_space=pltpu.SMEM)] +...  2.51 us
  transfers between devices with their start and end apart: 7, of which 6 were waited for; matrix products, arithmetic and copies ran while one was open for 2% of the time, Pallas kernels for 3%

profile of v5, /device:TPU:0, one launch (start us, length us, event | category | flops | bytes accessed | tf_op | source)
XLA Modules:
  0.0 84.4 jit_solution(11009399429868562998)
XLA Ops:
  0.0 0.0 copy-start
  0.0 3.8 %pack.1 = bf16[8,288,256]{2,1,0:T(8,128)(2,1)} custom-call(bf16[256,1024]{1,0:T(8,128)(2,1)} %refs_0_.1, bf16[256,1024]{1,0:T(8,128)(2,1)} %refs_1_.1, bf16[256,1024]{1,0:T(8,128)(2,1)} %refs_2_.1, bf16[3,7,64]{2,1,0:T(8,128)(2,1)} %refs_3_.1, bf16[64,256]{1,0:T(8,128)(2,1)} %refs_4_.1), custom_call_target="tpu_custom_call" | custom-call | tf_op jit(solution)/shard_map/pack/pallas_call | solution.py:97
  3.8 0.0 copy-start.3
  3.8 0.0 copy-start.2
  3.9 7.4 %all-to-all-start = ((bf16[8,288,256]{2,1,0:T(8,128)(2,1)}), bf16[8,288,256]{2,1,0:T(8,128)(2,1)S(1)}, u32[]{:S(2)}, u32[]{:S(2)}) async-start(bf16[8,288,256]{2,1,0:T(8,128)(2,1)} %pack.1), calls=%async_computation | async-start | bytes 2359296 | tf_op jit(solution)/shard_map/all_to_all | solution.py:313
  11.2 0.0 copy-start.4
  11.3 0.0 copy-done.3
  11.3 0.1 dynamic-slice_convert_fusion
  11.3 28.5 %all-to-all-done.refs_1_ = bf16[8,288,256]{2,1,0:T(8,128)(2,1)S(1)} async-done(((bf16[8,288,256]{2,1,0:T(8,128)(2,1)}), bf16[8,288,256]{2,1,0:T(8,128)(2,1)S(1)}, u32[]{:S(2)}, u32[]{:S(2)}) %all-to-all-start) | async-done | bytes 1179680 | tf_op jit(solution)/shard_map/all_to_all | solution.py:313
  39.8 0.0 copy-done.2
  39.8 1.0 %turn.1 = bf16[8,128,256]{2,1,0:T(8,128)(2,1)} custom-call(bf16[256,1024]{1,0:T(8,128)(2,1)S(1)} %copy-done.2), custom_call_target="tpu_custom_call" | custom-call | tf_op jit(solution)/shard_map/turn/pallas_call | solution.py:124
  40.8 3.6 %all-to-all-start.1 = ((bf16[8,128,256]{2,1,0:T(8,128)(2,1)}), bf16[8,128,256]{2,1,0:T(8,128)(2,1)S(1)}, u32[]{:S(2)}, u32[]{:S(2)}) async-start(bf16[8,128,256]{2,1,0:T(8,128)(2,1)} %turn.1), calls=%async_computation.1 | async-start | bytes 1048576 | tf_op jit(solution)/shard_map/all_to_all | solution.py:313
  44.5 0.1 broadcast_in_dim.22
  44.6 0.1 convert_element_type.21.refs_3_
  44.7 0.1 copy.13
  44.8 0.0 copy-done
  44.8 0.0 copy-done.4
  44.8 0.1 select_reduce_fusion.refs_0_
  44.9 2.7 %mix.1 = (f32[8,128,256]{2,1,0:T(8,128)S(1)}, f32[16,128]{1,0:T(8,128)S(1)}) custom-call(s32[8]{0:T(128)S(1)} %select_reduce_fusion.refs_0_, bf16[8,288,256]{2,1,0:T(8,128)(2,1)S(1)} %all-to-all-done.refs_1_, bf16[8,16,256]{2,1,0:T(8,128)(2,1)S(1)} %slice.17.refs_2_, f32[3,7,128]{2,1,0:T(8,128)S(1)} %convert_element_type.21.refs_3_, f32[128,7]{1,0:T(8,128)S(1)} %bitcast.14, ...), custom_call_target="tpu_custom_call" | custom-call | tf_op jit(solution)/shard_map/mix/pallas_call | solution.py:210
  47.6 0.1 collective-permute-start
  47.7 1.2 %collective-permute-done = f32[16,128]{1,0:T(8,128)S(1)} collective-permute-done((f32[16,128]{1,0:T(8,128)S(1)}, f32[16,128]{1,0:T(8,128)S(1)}, u32[]{:S(2)}, u32[]{:S(2)}) %collective-permute-start) | collective-permute-done | bytes 8224 | tf_op jit(solution)/shard_map/ppermute | solution.py:321
  48.9 1.5 %collective-permute-start.1 = (f32[16,128]{1,0:T(8,128)S(1)}, f32[16,128]{1,0:T(8,128)S(1)}, u32[]{:S(2)}, u32[]{:S(2)}) collective-permute-start(f32[16,128]{1,0:T(8,128)S(1)} %add.27), channel_id=1, source_target_pairs={{0,2},{1,3},{2,0},{3,1},{4,6},{5,7},{6,4},{7,5},{8,10},{9,11},{10,... | collective-permute-start | bytes 24584 | tf_op jit(solution)/shard_map/ppermute | solution.py:321
  50.4 2.1 %collective-permute-done.1 = f32[16,128]{1,0:T(8,128)S(1)} collective-permute-done((f32[16,128]{1,0:T(8,128)S(1)}, f32[16,128]{1,0:T(8,128)S(1)}, u32[]{:S(2)}, u32[]{:S(2)}) %collective-permute-start.1) | collective-permute-done | bytes 8224 | tf_op jit(solution)/shard_map/ppermute | solution.py:321
  52.5 2.0 %collective-permute-start.2 = (f32[16,128]{1,0:T(8,128)S(1)}, f32[16,128]{1,0:T(8,128)S(1)}, u32[]{:S(2)}, u32[]{:S(2)}) collective-permute-start(f32[16,128]{1,0:T(8,128)S(1)} %add.28), channel_id=1, source_target_pairs={{0,4},{4,0},{8,12},{12,8},{16,20},{20,16},{24,28},{28,24},{1,5},{5... | collective-permute-start | bytes 24584 | tf_op jit(solution)/shard_map/ppermute | solution.py:321
  54.6 1.6 %collective-permute-done.2 = f32[16,128]{1,0:T(8,128)S(1)} collective-permute-done((f32[16,128]{1,0:T(8,128)S(1)}, f32[16,128]{1,0:T(8,128)S(1)}, u32[]{:S(2)}, u32[]{:S(2)}) %collective-permute-start.2) | collective-permute-done | bytes 8224 | tf_op jit(solution)/shard_map/ppermute | solution.py:321
  56.2 2.0 %collective-permute-start.3 = (f32[16,128]{1,0:T(8,128)S(1)}, f32[16,128]{1,0:T(8,128)S(1)}, u32[]{:S(2)}, u32[]{:S(2)}) collective-permute-start(f32[16,128]{1,0:T(8,128)S(1)} %add.29), channel_id=1, source_target_pairs={{0,8},{4,12},{8,0},{12,4},{16,24},{20,28},{24,16},{28,20},{1,9},{5... | collective-permute-start | bytes 24584 | tf_op jit(solution)/shard_map/ppermute | solution.py:321
  58.2 0.8 dynamic-slice_bitcast_fusion.1
  59.0 0.1 copy.14.refs_5_
  59.1 0.8 collective-permute-done.3
  59.9 3.1 %collective-permute-start.4 = (f32[16,128]{1,0:T(8,128)S(1)}, f32[16,128]{1,0:T(8,128)S(1)}, u32[]{:S(2)}, u32[]{:S(2)}) collective-permute-start(f32[16,128]{1,0:T(8,128)S(1)} %add.30), channel_id=1, source_target_pairs={{0,16},{4,20},{8,24},{12,28},{16,0},{20,4},{24,8},{28,12},{1,17},{... | collective-permute-start | bytes 24584 | tf_op jit(solution)/shard_map/ppermute | solution.py:321
  62.9 1.6 %collective-permute-done.4 = f32[16,128]{1,0:T(8,128)S(1)} collective-permute-done((f32[16,128]{1,0:T(8,128)S(1)}, f32[16,128]{1,0:T(8,128)S(1)}, u32[]{:S(2)}, u32[]{:S(2)}) %collective-permute-start.4) | collective-permute-done | bytes 8224 | tf_op jit(solution)/shard_map/ppermute | solution.py:321
  64.6 0.0 all-to-all-done.1.refs_2_
  64.6 0.0 copy-start.1
  64.6 2.5 %long.1 = bf16[8,128,256]{2,1,0:T(8,128)(2,1)S(1)} custom-call(s32[8]{0:T(128)S(1)} %select_reduce_fusion.refs_0_, f32[8,128,256]{2,1,0:T(8,128)S(1)} %get-tuple-element.10.refs_1_, bf16[8,128,256]{2,1,0:T(8,128)(2,1)S(1)} %all-to-all-done.1.refs_2_, f32[16,128]{1,0:T(8,128)S(1)} %add.31.refs_3_, f32[8,2304]{1,0:T(8,128)S(1)} %pad_convert_fusion.refs_4_, ...), custom_call_target="tpu_custom_call" | custom-call | tf_op jit(solution)/shard_map/long/pallas_call | solution.py:278
  67.1 16.2 %all_to_all.15.mixed_ref = bf16[8,128,256]{2,1,0:T(8,128)(2,1)S(1)} all-to-all(bf16[8,128,256]{2,1,0:T(8,128)(2,1)S(1)} %long.1), channel_id=1, replica_groups=mesh['ctx'=8,'tp'=4] {'ctx'}, dimensions={0} | all-to-all | bytes 1048576 | tf_op jit(solution)/shard_map/all_to_all | solution.py:313
  83.3 0.0 copy-done.1
  83.3 1.0 %gate.1 = bf16[256,1024]{1,0:T(8,128)(2,1)} custom-call(bf16[8,128,256]{2,1,0:T(8,128)(2,1)S(1)} %all_to_all.15.mixed_ref, bf16[256,1024]{1,0:T(8,128)(2,1)S(1)} %copy-done.1), custom_call_target="tpu_custom_call" | custom-call | tf_op jit(solution)/shard_map/gate/pallas_call | solution.py:301
  (12 shorter events, 0.0 us)
Async XLA Ops:
  0.0 44.8 %copy-start = (bf16[128,64]{0,1:T(8,128)(2,1)S(1)}, bf16[128,64]{0,1:T(8,128)(2,1)}, u32[]{:S(2)}) copy-start(bf16[128,64]{0,1:T(8,128)(2,1)} %param.17) | copy-start | bytes 49156
  3.8 7.4 %copy-start.3 = (bf16[3,7,64]{2,1,0:T(8,128)(2,1)S(1)}, bf16[3,7,64]{2,1,0:T(8,128)(2,1)}, u32[]{:S(2)}) copy-start(bf16[3,7,64]{2,1,0:T(8,128)(2,1)} %refs_3_.1) | copy-start | bytes 8068
  3.8 36.0 %copy-start.2 = (bf16[256,1024]{1,0:T(8,128)(2,1)S(1)}, bf16[256,1024]{1,0:T(8,128)(2,1)}, u32[]{:S(2)}) copy-start(bf16[256,1024]{1,0:T(8,128)(2,1)} %in_ref) | copy-start | bytes 1572868
  3.9 36.0 %all-to-all-start = ((bf16[8,288,256]{2,1,0:T(8,128)(2,1)}), bf16[8,288,256]{2,1,0:T(8,128)(2,1)S(1)}, u32[]{:S(2)}, u32[]{:S(2)}) async-start(bf16[8,288,256]{2,1,0:T(8,128)(2,1)} %pack.1), calls=%async_computation | async-start | bytes 2359296 | tf_op jit(solution)/shard_map/all_to_all | solution.py:313
  11.2 33.5 %copy-start.4 = (s32[8]{0:T(128)S(1)}, s32[8]{0:T(128)}, u32[]{:S(2)}) copy-start(s32[8]{0:T(128)} %param.20) | copy-start | bytes 100
  40.8 23.7 %all-to-all-start.1 = ((bf16[8,128,256]{2,1,0:T(8,128)(2,1)}), bf16[8,128,256]{2,1,0:T(8,128)(2,1)S(1)}, u32[]{:S(2)}, u32[]{:S(2)}) async-start(bf16[8,128,256]{2,1,0:T(8,128)(2,1)} %turn.1), calls=%async_computation.1 | async-start | bytes 1048576 | tf_op jit(solution)/shard_map/all_to_all | solution.py:313
  47.6 1.2 %collective-permute-start = (f32[16,128]{1,0:T(8,128)S(1)}, f32[16,128]{1,0:T(8,128)S(1)}, u32[]{:S(2)}, u32[]{:S(2)}) collective-permute-start(f32[16,128]{1,0:T(8,128)S(1)} %get-tuple-element.12), channel_id=1, source_target_pairs={{0,1},{1,0},{2,3},{3,2},{4,5},{5,4},{6,7},{7,6},{8,9},{9,8},{10,11... | collective-permute-start | bytes 24584 | tf_op jit(solution)/shard_map/ppermute | solution.py:321
  48.9 3.7 %collective-permute-start.1 = (f32[16,128]{1,0:T(8,128)S(1)}, f32[16,128]{1,0:T(8,128)S(1)}, u32[]{:S(2)}, u32[]{:S(2)}) collective-permute-start(f32[16,128]{1,0:T(8,128)S(1)} %add.27), channel_id=1, source_target_pairs={{0,2},{1,3},{2,0},{3,1},{4,6},{5,7},{6,4},{7,5},{8,10},{9,11},{10,... | collective-permute-start | bytes 24584 | tf_op jit(solution)/shard_map/ppermute | solution.py:321
  52.5 3.7 %collective-permute-start.2 = (f32[16,128]{1,0:T(8,128)S(1)}, f32[16,128]{1,0:T(8,128)S(1)}, u32[]{:S(2)}, u32[]{:S(2)}) collective-permute-start(f32[16,128]{1,0:T(8,128)S(1)} %add.28), channel_id=1, source_target_pairs={{0,4},{4,0},{8,12},{12,8},{16,20},{20,16},{24,28},{28,24},{1,5},{5... | collective-permute-start | bytes 24584 | tf_op jit(solution)/shard_map/ppermute | solution.py:321
  56.2 3.7 %collective-permute-start.3 = (f32[16,128]{1,0:T(8,128)S(1)}, f32[16,128]{1,0:T(8,128)S(1)}, u32[]{:S(2)}, u32[]{:S(2)}) collective-permute-start(f32[16,128]{1,0:T(8,128)S(1)} %add.29), channel_id=1, source_target_pairs={{0,8},{4,12},{8,0},{12,4},{16,24},{20,28},{24,16},{28,20},{1,9},{5... | collective-permute-start | bytes 24584 | tf_op jit(solution)/shard_map/ppermute | solution.py:321
  59.9 4.7 %collective-permute-start.4 = (f32[16,128]{1,0:T(8,128)S(1)}, f32[16,128]{1,0:T(8,128)S(1)}, u32[]{:S(2)}, u32[]{:S(2)}) collective-permute-start(f32[16,128]{1,0:T(8,128)S(1)} %add.30), channel_id=1, source_target_pairs={{0,16},{4,20},{8,24},{12,28},{16,0},{20,4},{24,8},{28,12},{1,17},{... | collective-permute-start | bytes 24584 | tf_op jit(solution)/shard_map/ppermute | solution.py:321
  64.6 18.7 %copy-start.1 = (bf16[256,1024]{1,0:T(8,128)(2,1)S(1)}, bf16[256,1024]{1,0:T(8,128)(2,1)}, u32[]{:S(2)}) copy-start(bf16[256,1024]{1,0:T(8,128)(2,1)} %gate_ref.1) | copy-start | bytes 1572868

commit v6 on v5

--- a/solution.py
+++ b/solution.py
@@ -66,29 +66,35 @@
             for copy in parts[t // PACK_TILES]:
                 copy.wait()
         lanes = slice(t * LANES, (t + 1) * LANES)
-        out_ref[t, :LANES, :] = jnp.transpose(q_ref[:, lanes])
+        turned = jnp.transpose(q_ref[:LANES, lanes])
+        at = LANES + LANES // 2
+        out_ref[t, LANES:at, :] = jnp.concatenate([turned[: LANES // 2], turned[LANES // 2 :]], axis=1)
         features = []
         for which, ref in enumerate((k_ref, v_ref)):
             wide_ref[t, which, :EDGE] = jnp.zeros((EDGE, LANES), F32)
             wide_ref[t, which, EDGE:] = ref[:, lanes].astype(F32)
             features.append(short_filter(wide_ref.at[t, which], taps[which][:, lanes], EDGE, rows))
             ends = [wide_ref[t, which, EDGE : 2 * EDGE], wide_ref[t, which, rows : rows + EDGE]]
-            out_ref[t, 2 * LANES : 2 * LANES + 2 * EDGE, which * LANES : (which + 1) * LANES] = (
+            out_ref[t, at : at + 2 * EDGE, which * LANES : (which + 1) * LANES] = (
                 jnp.concatenate(ends, axis=0).astype(BF16)
             )
-        out_ref[t, LANES : 2 * LANES, :] = jnp.transpose((features[0] * features[1]).astype(BF16))
+        out_ref[t, :LANES, :] = jnp.transpose((features[0] * features[1]).astype(BF16))
     long_copy.wait()
     for t in range(tiles):
+        lanes = slice(t * LANES, (t + 1) * LANES)
+        middle = q_ref[LANES : LANES + 2 * EDGE, lanes].astype(F32)[:EDGE]
+        last = q_ref[rows - 2 * EDGE :, lanes].astype(F32)[EDGE:]
         here = long_ref[t * groups : (t + 1) * groups, :].astype(F32)
-        filler = jnp.zeros((2 * EDGE - groups, rows), F32)
-        out_ref[t, 2 * LANES + 2 * EDGE :, :] = jnp.concatenate([here, filler], axis=0).astype(BF16)
+        lines = jnp.concatenate([jnp.concatenate([middle, last], axis=1), here], axis=0)
+        out_ref[t, LANES + LANES // 2 + 2 * EDGE :, :] = lines.astype(BF16)
 
 
 def call_pack(q_one, k_one, v_one, short_taps, long_taps):
     rows, width = q_one.shape
     tiles = width // LANES
     size = width // short_taps.shape[2]
-    assert rows == 2 * LANES and LANES // size <= 2 * EDGE
+    groups = LANES // size
+    assert rows == 2 * LANES
 
     def kernel(*refs):
         pack_kernel(size, *refs)
@@ -98,7 +104,7 @@
         kernel,
         in_specs=[pl.BlockSpec(memory_space=pltpu.HBM)] * 5,
         out_specs=pl.BlockSpec(memory_space=pltpu.VMEM),
-        out_shape=jax.ShapeDtypeStruct((tiles, 2 * LANES + 4 * EDGE, rows), BF16),
+        out_shape=jax.ShapeDtypeStruct((tiles, LANES + LANES // 2 + 3 * EDGE + groups, rows), BF16),
         scratch_shapes=[
             pltpu.VMEM((rows, width), BF16),
             pltpu.VMEM((rows, width), BF16),
@@ -113,25 +119,6 @@
     )(*inputs)
 
 
-def turn_kernel(in_ref, out_ref):
-    for t in range(out_ref.shape[0]):
-        out_ref[t] = jnp.transpose(in_ref[:, t * LANES : (t + 1) * LANES])
-
-
-def call_turn(array):
-    rows, width = array.shape
-    wide = GATE_TILES * LANES
-    return pl.pallas_call(
-        turn_kernel,
-        grid=(width // wide,),
-        in_specs=[pl.BlockSpec((rows, wide), lambda i: (0, i))],
-        out_specs=pl.BlockSpec((GATE_TILES, LANES, rows), lambda i: (i, 0, 0)),
-        out_shape=jax.ShapeDtypeStruct((width // LANES, LANES, rows), BF16),
-        compiler_params=params("arbitrary"),
-        name="turn",
-    )(array)
-
-
 def shifted_rows(row, count):
     return pltpu.roll(jnp.broadcast_to(row, (count, row.shape[1])), 0, 1, stride=1, stride_axis=0)
 
@@ -144,14 +131,112 @@
     return jnp.stack(pieces, axis=1).reshape(-1, reach + rows)
 
 
+def early_kernel(
+    size, q_ref, k_ref, v_ref, gate_ref, taps_ref, base_ref, out_ref, energy_ref, extended_ref
+):
+    rows, width = q_ref.shape
+    groups = LANES // size
+    taps = [lane_taps(taps_ref, which, size, width) for which in range(3)]
+    lane_group = lax.broadcasted_iota(jnp.int32, (1, LANES), 1) // size
+    own = lax.broadcasted_iota(jnp.int32, (LANES, LANES), 0) >= EDGE
+    squares = jnp.zeros((LANES, LANES), F32)
+    for t in range(width // LANES):
+        lanes = slice(t * LANES, (t + 1) * LANES)
+        for which, ref in enumerate((q_ref, k_ref, v_ref)):
+            extended_ref[t, which, :EDGE] = jnp.zeros((EDGE, LANES), F32)
+            extended_ref[t, which, EDGE:] = ref[:, lanes].astype(F32)
+        q_feat = short_filter(extended_ref.at[t, 0], taps[0][:, lanes], EDGE + LANES, LANES)
+        k_feat = short_filter(extended_ref.at[t, 1], taps[1][:, lanes], EDGE, rows)
+        v_feat = short_filter(extended_ref.at[t, 2], taps[2][:, lanes], EDGE, rows)
+        table = jnp.concatenate(
+            [
+                shifted_rows(base_ref[g : g + 1, :], LANES).astype(BF16)
+                for g in range(t * groups, (t + 1) * groups)
+            ],
+            axis=0,
+        )
+        every = jnp.dot(table, (k_feat * v_feat).astype(BF16), preferred_element_type=F32)
+        medium = every[:LANES]
+        for g in range(1, groups):
+            medium = jnp.where(lane_group == g, every[g * LANES : (g + 1) * LANES], medium)
+        mixed = jnp.where(own, q_feat * medium, 0.0)
+        out_ref[t] = jnp.transpose(mixed * gate_ref[LANES:, lanes].astype(F32))
+        squares = squares + mixed * mixed
+    energy_ref[...] = jnp.sum(jnp.transpose(squares), axis=0, keepdims=True)
+
+
+def call_early(q_one, k_one, v_one, k_two, short_taps, medium_taps):
+    rows, width = q_one.shape
+    tiles = width // LANES
+    size = width // short_taps.shape[2]
+    base = jnp.transpose(medium_taps[::-1])
+    base = jnp.pad(base, ((0, 0), (1, rows - medium_taps.shape[0] - 1))).astype(F32)
+
+    def kernel(*refs):
+        early_kernel(size, *refs)
+
+    return pl.pallas_call(
+        kernel,
+        in_specs=[pl.BlockSpec(memory_space=pltpu.VMEM)] * 6,
+        out_specs=[pl.BlockSpec(memory_space=pltpu.VMEM)] * 2,
+        out_shape=[
+            jax.ShapeDtypeStruct((tiles, LANES, LANES), F32),
+            jax.ShapeDtypeStruct((1, LANES), F32),
+        ],
+        scratch_shapes=[pltpu.VMEM((tiles, 3, EDGE + rows, LANES), F32)],
+        compiler_params=params(),
+        name="early",
+    )(q_one, k_one, v_one, k_two, short_taps, base)
+
+
+def join_kernel(full_width, gate_ref, early_ref, energy_ref, out_ref):
+    scale = lax.rsqrt(energy_ref[...] / full_width + EPSILON)
+    lane = lax.broadcasted_iota(jnp.int32, (LANES, LANES), 1)
+    for t in range(out_ref.shape[0]):
+        lanes = slice(t * LANES, (t + 1) * LANES)
+        turned = jnp.transpose(gate_ref[:, lanes])
+        values = jnp.where(lane < EDGE, turned[:, LANES:].astype(F32), early_ref[t] * scale)
+        out_ref[t, :, :LANES] = turned[:, :LANES]
+        out_ref[t, :, LANES:] = values.astype(BF16)
+
+
+def call_join(k_two, early, energy, full_width):
+    rows, width = k_two.shape
+
+    def kernel(*refs):
+        join_kernel(full_width, *refs)
+
+    return pl.pallas_call(
+        kernel,
+        in_specs=[pl.BlockSpec(memory_space=pltpu.VMEM)] * 3,
+        out_specs=pl.BlockSpec(memory_space=pltpu.VMEM),
+        out_shape=jax.ShapeDtypeStruct((width // LANES, LANES, rows), BF16),
+        compiler_params=params(),
+        name="join",
+    )(k_two, early, energy)
+
+
 def mix_kernel(
-    size, holder_ref, moved_ref, ends_ref, taps_ref, column_ref, base_ref, out_ref, energy_ref, extended_ref, squares_ref
+    size,
+    holder_ref,
+    moved_ref,
+    ends_ref,
+    more_ref,
+    taps_ref,
+    column_ref,
+    base_ref,
+    out_ref,
+    energy_ref,
+    extended_ref,
+    q_ends_ref,
+    squares_ref,
 ):
     blocks, shard, rows = out_ref.shape
     halves = rows // LANES
     span = 2 * EDGE
     holders = [holder_ref[b] for b in range(blocks)]
-    ends = [ends_ref[holder, -span:, :].astype(F32) for holder in holders]
+    ends = [ends_ref[holder].astype(F32) for holder in holders]
+    more = [more_ref[holder].astype(F32) for holder in holders]
 
     features = []
     for which in range(2):
@@ -166,37 +251,55 @@
         )
     starts = jnp.transpose((features[0] * features[1]).astype(BF16).astype(F32))
     wide = blocks * span
+    for b in range(blocks):
+        before = more[b - 1][:, shard:] if b else jnp.zeros((EDGE, shard), F32)
+        q_ends_ref[b * span : (b + 1) * span] = jnp.concatenate([before, more[b][:, :shard]], axis=0)
+    q_ends = jnp.transpose(q_ends_ref[...])
+    half = shard // 2
+
+    def q_first(holder, g):
+        if half % size == 0:
+            at = shard + g * size % half
+            beside = g * size // half * LANES
+            return moved_ref[holder, at : at + size, beside : beside + LANES].astype(F32)
+        both = moved_ref[holder, shard : shard + half, :].astype(F32)
+        both = jnp.concatenate([both[:, :LANES], both[:, LANES:]], axis=0)
+        return both[g * size : (g + 1) * size]
+
     lane = lax.broadcasted_iota(jnp.int32, (size, LANES), 1)
 
     squares_ref[...] = jnp.zeros(squares_ref.shape, F32)
     for g in range(shard // size):
         here = slice(g * size, (g + 1) * size)
-        z_there = slice(shard + g * size, shard + (g + 1) * size)
-        q_seq = [jnp.zeros((size, LANES), F32)]
         z_seq = [jnp.zeros((size, LANES), BF16)]
+        q_feats = []
         for b, holder in enumerate(holders):
-            q_seq.append(moved_ref[holder, here, :].astype(F32))
-            z_block = moved_ref[holder, z_there, :]
+            z_block = moved_ref[holder, here, :]
             first = pltpu.roll(starts[here], (wide - b * span - EDGE) % wide, 1)[:, :LANES]
             z_first = jnp.where(lane < EDGE, first, z_block[:, :LANES].astype(F32)).astype(BF16)
             z_seq.append(jnp.concatenate([z_first, z_block[:, LANES:]], axis=1))
-        q_seq = jnp.concatenate(q_seq, axis=1)
+            before = pltpu.roll(q_ends[here], (wide + LANES - EDGE - b * span) % wide, 1)[:, :LANES]
+            after = pltpu.roll(q_ends[here], (wide - b * span - EDGE) % wide, 1)[:, :LANES]
+            q_block = jnp.concatenate([before, q_first(holder, g), after], axis=1)
+            q_feat = q_block * column_ref[here, 0:1]
+            for j in range(1, taps_ref.shape[1]):
+                q_feat = q_feat + pltpu.roll(q_block, j, 1) * column_ref[here, j : j + 1]
+            q_feats.append(q_feat)
         z_seq = jnp.concatenate(z_seq, axis=1)
-        q_feat = q_seq * column_ref[here, 0:1]
-        for j in range(1, taps_ref.shape[1]):
-            q_feat = q_feat + pltpu.roll(q_seq, j, 1) * column_ref[here, j : j + 1]
         table = shifted_rows(base_ref[g : g + 1, :], 2 * LANES)[:, :LANES].astype(BF16)
         windows = [z_seq[:, o * LANES : (o + 2) * LANES] for o in range(blocks * halves)]
         medium = jnp.dot(jnp.concatenate(windows, axis=0), table, preferred_element_type=F32)
         for o in range(blocks * halves):
-            mixed = q_feat[:, (o + 1) * LANES : (o + 2) * LANES] * medium[o * size : (o + 1) * size]
-            at = (o % halves) * LANES
-            out_ref[o // halves, here, at : at + LANES] = mixed
+            b, at = o // halves, (o % halves) * LANES
+            mixed = q_feats[b][:, LANES + at : 2 * LANES + at] * medium[o * size : (o + 1) * size]
+            if at:
+                mixed = jnp.where(lane < EDGE, mixed, 0.0)
+            out_ref[b, here, at : at + LANES] = mixed
             squares_ref[o] += mixed * mixed
     energy_ref[...] = jnp.sum(squares_ref[...], axis=1)
 
 
-def call_mix(holder, moved, ends, short_local, medium_local, shard, rows):
+def call_mix(holder, moved, ends, more, short_local, medium_local, shard, rows):
     blocks = moved.shape[0]
     size = shard // medium_local.shape[1]
     reach = medium_local.shape[0]
@@ -210,7 +313,7 @@
     return pl.pallas_call(
         kernel,
         in_specs=[pl.BlockSpec(memory_space=pltpu.SMEM)]
-        + [pl.BlockSpec(memory_space=pltpu.VMEM)] * 5,
+        + [pl.BlockSpec(memory_space=pltpu.VMEM)] * 6,
         out_specs=[pl.BlockSpec(memory_space=pltpu.VMEM)] * 2,
         out_shape=[
             jax.ShapeDtypeStruct((blocks, shard, rows), F32),
@@ -218,11 +321,12 @@
         ],
         scratch_shapes=[
             pltpu.VMEM((2, EDGE + blocks * 2 * EDGE, shard), F32),
+            pltpu.VMEM((blocks * 2 * EDGE, shard), F32),
             pltpu.VMEM((blocks * rows // LANES, size, LANES), F32),
         ],
         compiler_params=params(),
         name="mix",
-    )(holder, moved, ends, lane_form, jnp.transpose(lane_form[0]), base)
+    )(holder, moved, ends, more, lane_form, jnp.transpose(lane_form[0]), base)
 
 
 def long_kernel(
@@ -236,11 +340,13 @@
     reach = blocks * size
     holders = [holder_ref[b] for b in range(blocks)]
     scale = lax.rsqrt(energy_ref[...] / full_width + EPSILON)
+    own = lax.broadcasted_iota(jnp.int32, (size, rows), 1) >= LANES + EDGE
     for b, holder in enumerate(holders):
         line = jnp.concatenate([scale[o : o + 1] for o in range(b * halves, (b + 1) * halves)], axis=1)
         for g in range(shard // size):
             here = slice(g * size, (g + 1) * size)
-            value = key_ref[holder, here].astype(F32) * mixed_ref[b, here] * line
+            key = key_ref[holder, here].astype(F32)
+            value = jnp.where(own, key, key * mixed_ref[b, here] * line)
             ordered_ref[g, reach + b * size : reach + (b + 1) * size] = value.astype(BF16)
     for g in range(shard // size):
         here = slice(g * size, (g + 1) * size)
@@ -345,35 +451,40 @@
     tile_groups = LANES // size
     shard = width // ctx_count
     shard_groups = shard // size
+    full_width = width * tp_count
 
     slots = jnp.arange(ctx_count, dtype=jnp.int32)
     holder = jnp.sum(jnp.where(block_order[None, :] == slots[:, None], slots[None, :], 0), axis=1)
 
     packed = call_pack(q_one, k_one, v_one, short_taps, long_taps)
     span = 2 * EDGE
-    if ctx_count == tiles:
-        moved = exchange(packed)
-        taps_at = 2 * shard + span
-        ends = lax.slice_in_dim(moved, 2 * shard, taps_at, axis=1)
-    else:
-        ends = packed[:, 2 * LANES : 2 * LANES + span].reshape(tiles, span, 2, -1, shard)
-        parts = [
-            packed[:, :LANES],
-            packed[:, LANES : 2 * LANES],
-            jnp.transpose(ends, (0, 3, 1, 2, 4)),
-            packed[:, 2 * LANES + span : 2 * LANES + span + tile_groups],
-        ]
-        moved = exchange(
-            jnp.concatenate([part.reshape(ctx_count, -1, rows) for part in parts], axis=1)
-        )
-        taps_at = 2 * shard + span * 2 * shard // rows
-        ends = moved[:, 2 * shard : taps_at].reshape(ctx_count, span, 2 * shard)
-    moved, k_two = lax.optimization_barrier((moved, k_two))
-    keys = exchange(call_turn(k_two).reshape(ctx_count, shard, rows))
+    if ctx_count != tiles:
+        half = LANES // 2
+        sizes = (LANES, half, span, EDGE, tile_groups)
+        z, q, ends, more, taps = jnp.split(packed, [sum(sizes[:n]) for n in range(1, 5)], axis=1)
+        q = jnp.transpose(q.reshape(tiles, half, 2, LANES), (0, 2, 1, 3))
+        q = jnp.transpose(q.reshape(ctx_count, 2, shard // 2, LANES), (0, 2, 1, 3))
+        ends = jnp.transpose(ends.reshape(tiles, span, 2, -1, shard), (0, 3, 1, 2, 4))
+        more = jnp.transpose(more.reshape(tiles, EDGE, 2, -1, shard), (0, 3, 1, 2, 4))
+        parts = [part.reshape(ctx_count, -1, rows) for part in (z, q, ends, more, taps)]
+        packed = jnp.concatenate(parts, axis=1)
+    moved = exchange(packed)
+    ends_at = shard + shard // 2
+    more_at = ends_at + span * 2 * shard // rows
+    taps_at = more_at + EDGE * 2 * shard // rows
+    ends = moved[:, ends_at:more_at].reshape(ctx_count, span, 2 * shard)
+    more = moved[:, more_at:taps_at].reshape(ctx_count, EDGE, 2 * shard)
+
+    early, early_energy = call_early(q_one, k_one, v_one, k_two, short_taps, medium_taps)
+    early_energy = sum_by_pairs(early_energy, "tp")
+    joined = call_join(k_two, early, early_energy, full_width)
+    moved, joined = lax.optimization_barrier((moved, joined))
 
     short_local = lax.dynamic_slice_in_dim(short_taps, me * shard_groups, shard_groups, axis=2)
     medium_local = lax.dynamic_slice_in_dim(medium_taps, me * shard_groups, shard_groups, axis=1)
-    mixed, energy = call_mix(holder, moved, ends, short_local, medium_local, shard, rows)
+    mixed, energy = call_mix(holder, moved, ends, more, short_local, medium_local, shard, rows)
+    energy, joined = lax.optimization_barrier((energy, joined))
+    keys = exchange(joined.reshape(ctx_count, shard, rows))
     energy = sum_by_pairs(sum_by_pairs(energy, "tp"), "ctx")
 
     long_rows = moved[:, taps_at : taps_at + shard_groups]
@@ -381,7 +492,7 @@
     windows = long_windows(long_rows, rows, min(ctx_count, 8))
     gain = lax.dynamic_slice_in_dim(skip_gain, me * shard, shard).reshape(shard, 1)
     filtered = call_long(
-        holder, mixed, keys, energy, windows, gain, size, width * tp_count
+        holder, mixed, keys, energy, windows, gain, size, full_width
     )
     returned = exchange(filtered)
     return call_gate(returned.reshape(tiles, LANES, rows), q_two)

time: 84.7 us -> 78.4 us (0.926)
  waiting for transfers between devices: 35.8 us -> 23.5 us
  Pallas kernels: 11.1 us -> 14.8 us
  starting transfers between devices: 19.7 us -> 20.8 us
    all_to_all x2, waiting for transfers between devices: 28.5 us -> 13.2 us  [exchange(): return lax.all_to_all(array, 'ctx', split_axis=0, concat_axis=0, tiled=True)]
    pallas_call x1 -> x2, Pallas kernels: 1.01 us -> 4.29 us  [the longest x1 3.31 us: call_early(): pl.pallas_call(kernel, in_specs=[pl.BlockSpec(memory_space=pltpu.VMEM)] *...]
    ppermute x5 -> x7, waiting for transfers between devices: 7.3 us -> 10.3 us  [sum_by_pairs(): lax.ppermute(array, axis, [(i, i ^ bit) for i in range(count)])]
    ppermute x5 -> x7, starting transfers between devices: 8.71 us -> 9.84 us  [sum_by_pairs(): lax.ppermute(array, axis, [(i, i ^ bit) for i in range(count)])]
  transfers between devices with their start and end apart: 7 -> 9, of which waited for: 6 -> 8; matrix products, arithmetic and copies ran while one was open for 2% -> 2% of each run, Pallas kernels for 3% -> 6%
where the time goes in v6:
time: 78.4 us; the launch traced here: 78 us
  waiting for transfers between devices  23.5 us (30%)
  starting transfers between devices  20.8 us (27%)
  blocking collectives  16.6 us (21%)
  Pallas kernels  14.8 us (19%)
  local copies, waits for them, and re-layouts  1.87 us (2%)
    all_to_all x1, blocking collectives, exchange(): return lax.all_to_all(array, 'ctx', split_axis=0, concat_axis=0, tiled=True)  16.6 us
    all_to_all x2, waiting for transfers between devices, exchange(): return lax.all_to_all(array, 'ctx', split_axis=0, concat_axis=0, tiled=True)  13.2 us
    all_to_all x2, starting transfers between devices, exchange(): return lax.all_to_all(array, 'ctx', split_axis=0, concat_axis=0, tiled=True)  10.9 us
    ppermute x7, waiting for transfers between devices, sum_by_pairs(): lax.ppermute(array, axis, [(i, i ^ bit) for i in range(count)])  10.3 us
    ppermute x7, starting transfers between devices, sum_by_pairs(): lax.ppermute(array, axis, [(i, i ^ bit) for i in range(count)])  9.84 us
    pallas_call x1, Pallas kernels, call_pack(): pl.pallas_call(kernel, in_specs=[pl.BlockSpec(memory_space=pltpu.HBM)] *...  3.65 us
    pallas_call x1, Pallas kernels, call_early(): pl.pallas_call(kernel, in_specs=[pl.BlockSpec(memory_space=pltpu.VMEM)] *...  3.31 us
    pallas_call x1, Pallas kernels, call_mix(): pl.pallas_call(kernel, in_specs=[pl.BlockSpec(memory_space=pltpu.SMEM)] +...  3.25 us
  transfers between devices with their start and end apart: 9, of which 8 were waited for; matrix products, arithmetic and copies ran while one was open for 2% of the time, Pallas kernels for 6%

profile of v6, /device:TPU:0, one launch (start us, length us, event | category | flops | bytes accessed | tf_op | source)
XLA Modules:
  0.0 78.0 jit_solution(15858177347378714210)
XLA Ops:
  0.0 0.0 copy-start
  0.0 0.0 copy-start.4
  0.0 3.7 %pack.1 = bf16[8,224,256]{2,1,0:T(8,128)(2,1)} custom-call(bf16[256,1024]{1,0:T(8,128)(2,1)} %refs_0_.4, bf16[256,1024]{1,0:T(8,128)(2,1)} %refs_1_.3, bf16[256,1024]{1,0:T(8,128)(2,1)} %refs_2_.3, bf16[3,7,64]{2,1,0:T(8,128)(2,1)} %refs_4_.3, bf16[64,256]{1,0:T(8,128)(2,1)} %refs_4_.2), custom_call_target="tpu_custom_call" | custom-call | tf_op jit(solution)/shard_map/pack/pallas_call | solution.py:103
  3.7 0.0 copy-start.7
  3.7 0.0 copy-start.1
  3.7 0.0 copy-start.2
  3.7 0.0 copy-start.3
  3.7 7.4 %all-to-all-start = ((bf16[8,224,256]{2,1,0:T(8,128)(2,1)}), bf16[8,224,256]{2,1,0:T(8,128)(2,1)S(1)}, u32[]{:S(2)}, u32[]{:S(2)}) async-start(bf16[8,224,256]{2,1,0:T(8,128)(2,1)} %pack.1), calls=%async_computation | async-start | bytes 1835008 | tf_op jit(solution)/shard_map/all_to_all | solution.py:419
  11.1 0.0 copy-done.7
  11.1 0.1 rev.3
  11.2 0.0 copy-start.6
  11.2 0.1 pad_convert_fusion.1.refs_5_
  11.3 0.0 copy-done.4
  11.3 0.0 copy-done.1
  11.3 0.0 copy-done.2
  11.3 0.0 copy-done.3
  11.3 0.6 copy-done.6
  11.9 3.3 %early.1 = (f32[8,128,128]{2,1,0:T(8,128)S(1)}, f32[1,128]{1,0:T(1,128)S(1)}) custom-call(bf16[256,1024]{1,0:T(8,128)(2,1)S(1)} %copy-done.2, bf16[256,1024]{1,0:T(8,128)(2,1)S(1)} %copy-done.3, bf16[256,1024]{1,0:T(8,128)(2,1)S(1)} %copy-done.4, bf16[256,1024]{1,0:T(8,128)(2,1)S(1)} %copy-done.1, bf16[3,7,64]{2,1,0:T(8,128)(2,1)S(1)} %copy-done.6, ...), custom_call_target="tpu_custom_call" | custom-call | tf_op jit(solution)/shard_map/early/pallas_call | solution.py:178
  15.2 0.1 collective-permute-start
  15.3 0.7 dynamic-slice_bitcast_fusion
  16.0 0.1 dynamic-slice_convert_fusion
  16.1 0.0 copy-start.8
  16.1 0.3 collective-permute-done
  16.4 1.5 %collective-permute-start.1 = (f32[1,128]{1,0:T(1,128)S(1)}, f32[1,128]{1,0:T(1,128)S(1)}, u32[]{:S(2)}, u32[]{:S(2)}) collective-permute-start(f32[1,128]{1,0:T(1,128)S(1)} %add.34), channel_id=1, source_target_pairs={{0,2},{1,3},{2,0},{3,1},{4,6},{5,7},{6,4},{7,5},{8,10},{9,11},{10,... | collective-permute-start | bytes 1544 | tf_op jit(solution)/shard_map/ppermute | solution.py:427
  17.9 0.0 copy-done.8
  17.9 0.1 select_reduce_fusion.refs_0_
  18.0 0.1 copy.13
  18.1 0.1 broadcast_in_dim.22
  18.2 0.1 convert_element_type.27.refs_4_
  18.3 1.6 %collective-permute-done.1 = f32[1,128]{1,0:T(1,128)S(1)} collective-permute-done((f32[1,128]{1,0:T(1,128)S(1)}, f32[1,128]{1,0:T(1,128)S(1)}, u32[]{:S(2)}, u32[]{:S(2)}) %collective-permute-start.1) | collective-permute-done | bytes 544 | tf_op jit(solution)/shard_map/ppermute | solution.py:427
  19.9 1.0 %join.1 = bf16[8,128,256]{2,1,0:T(8,128)(2,1)} custom-call(bf16[256,1024]{1,0:T(8,128)(2,1)S(1)} %copy-done.1, f32[8,128,128]{2,1,0:T(8,128)S(1)} %get-tuple-element.13.refs_1_, f32[1,128]{1,0:T(1,128)S(1)} %add.35.refs_2_), custom_call_target="tpu_custom_call" | custom-call | tf_op jit(solution)/shard_map/join/pallas_call | solution.py:209
  20.9 13.2 %all-to-all-done.refs_1_ = bf16[8,224,256]{2,1,0:T(8,128)(2,1)S(1)} async-done(((bf16[8,224,256]{2,1,0:T(8,128)(2,1)}), bf16[8,224,256]{2,1,0:T(8,128)(2,1)S(1)}, u32[]{:S(2)}, u32[]{:S(2)}) %all-to-all-start) | async-done | bytes 917536 | tf_op jit(solution)/shard_map/all_to_all | solution.py:419
  34.2 3.2 %mix.1 = (f32[8,128,256]{2,1,0:T(8,128)S(1)}, f32[16,128]{1,0:T(8,128)S(1)}) custom-call(s32[8]{0:T(128)S(1)} %select_reduce_fusion.refs_0_, bf16[8,224,256]{2,1,0:T(8,128)(2,1)S(1)} %all-to-all-done.refs_1_, bf16[8,16,256]{2,1,0:T(8,128)(2,1)S(1)} %slice.21.refs_2_, bf16[8,8,256]{2,1,0:T(8,128)(2,1)S(1)} %slice.22.refs_3_, ...), custom_call_target="tpu_custom_call" | custom-call | tf_op jit(solution)/shard_map/mix/pallas_call | solution.py:313
  37.4 3.5 %all-to-all-start.1 = ((bf16[8,128,256]{2,1,0:T(8,128)(2,1)}), bf16[8,128,256]{2,1,0:T(8,128)(2,1)S(1)}, u32[]{:S(2)}, u32[]{:S(2)}) async-start(bf16[8,128,256]{2,1,0:T(8,128)(2,1)} %join.1), calls=%async_computation.1 | async-start | bytes 1048576 | tf_op jit(solution)/shard_map/all_to_all | solution.py:419
  41.0 0.1 collective-permute-start.2
  41.0 1.2 %collective-permute-done.2 = f32[16,128]{1,0:T(8,128)S(1)} collective-permute-done((f32[16,128]{1,0:T(8,128)S(1)}, f32[16,128]{1,0:T(8,128)S(1)}, u32[]{:S(2)}, u32[]{:S(2)}) %collective-permute-start.2) | collective-permute-done | bytes 8224 | tf_op jit(solution)/shard_map/ppermute | solution.py:427
  42.2 1.5 %collective-permute-start.3 = (f32[16,128]{1,0:T(8,128)S(1)}, f32[16,128]{1,0:T(8,128)S(1)}, u32[]{:S(2)}, u32[]{:S(2)}) collective-permute-start(f32[16,128]{1,0:T(8,128)S(1)} %add.37), channel_id=1, source_target_pairs={{0,2},{1,3},{2,0},{3,1},{4,6},{5,7},{6,4},{7,5},{8,10},{9,11},{10,... | collective-permute-start | bytes 24584 | tf_op jit(solution)/shard_map/ppermute | solution.py:427
  43.7 2.1 %collective-permute-done.3 = f32[16,128]{1,0:T(8,128)S(1)} collective-permute-done((f32[16,128]{1,0:T(8,128)S(1)}, f32[16,128]{1,0:T(8,128)S(1)}, u32[]{:S(2)}, u32[]{:S(2)}) %collective-permute-start.3) | collective-permute-done | bytes 8224 | tf_op jit(solution)/shard_map/ppermute | solution.py:427
  45.8 2.0 %collective-permute-start.4 = (f32[16,128]{1,0:T(8,128)S(1)}, f32[16,128]{1,0:T(8,128)S(1)}, u32[]{:S(2)}, u32[]{:S(2)}) collective-permute-start(f32[16,128]{1,0:T(8,128)S(1)} %add.38), channel_id=1, source_target_pairs={{0,4},{4,0},{8,12},{12,8},{16,20},{20,16},{24,28},{28,24},{1,5},{5... | collective-permute-start | bytes 24584 | tf_op jit(solution)/shard_map/ppermute | solution.py:427
  47.8 1.8 %collective-permute-done.4 = f32[16,128]{1,0:T(8,128)S(1)} collective-permute-done((f32[16,128]{1,0:T(8,128)S(1)}, f32[16,128]{1,0:T(8,128)S(1)}, u32[]{:S(2)}, u32[]{:S(2)}) %collective-permute-start.4) | collective-permute-done | bytes 8224 | tf_op jit(solution)/shard_map/ppermute | solution.py:427
  49.6 1.9 %collective-permute-start.5 = (f32[16,128]{1,0:T(8,128)S(1)}, f32[16,128]{1,0:T(8,128)S(1)}, u32[]{:S(2)}, u32[]{:S(2)}) collective-permute-start(f32[16,128]{1,0:T(8,128)S(1)} %add.39), channel_id=1, source_target_pairs={{0,8},{4,12},{8,0},{12,4},{16,24},{20,28},{24,16},{28,20},{1,9},{5... | collective-permute-start | bytes 24584 | tf_op jit(solution)/shard_map/ppermute | solution.py:427
  51.5 0.0 copy-done
  51.5 0.1 dynamic-slice_bitcast_fusion.1
  51.5 0.1 copy.14.refs_5_
  51.7 1.6 %collective-permute-done.5 = f32[16,128]{1,0:T(8,128)S(1)} collective-permute-done((f32[16,128]{1,0:T(8,128)S(1)}, f32[16,128]{1,0:T(8,128)S(1)}, u32[]{:S(2)}, u32[]{:S(2)}) %collective-permute-start.5) | collective-permute-done | bytes 8224 | tf_op jit(solution)/shard_map/ppermute | solution.py:427
  53.2 2.8 %collective-permute-start.6 = (f32[16,128]{1,0:T(8,128)S(1)}, f32[16,128]{1,0:T(8,128)S(1)}, u32[]{:S(2)}, u32[]{:S(2)}) collective-permute-start(f32[16,128]{1,0:T(8,128)S(1)} %add.40), channel_id=1, source_target_pairs={{0,16},{4,20},{8,24},{12,28},{16,0},{20,4},{24,8},{28,12},{1,17},{... | collective-permute-start | bytes 24584 | tf_op jit(solution)/shard_map/ppermute | solution.py:427
  56.1 1.7 %collective-permute-done.6 = f32[16,128]{1,0:T(8,128)S(1)} collective-permute-done((f32[16,128]{1,0:T(8,128)S(1)}, f32[16,128]{1,0:T(8,128)S(1)}, u32[]{:S(2)}, u32[]{:S(2)}) %collective-permute-start.6) | collective-permute-done | bytes 8224 | tf_op jit(solution)/shard_map/ppermute | solution.py:427
  57.8 0.0 all-to-all-done.1.refs_2_
  57.8 2.6 %long.1 = bf16[8,128,256]{2,1,0:T(8,128)(2,1)S(1)} custom-call(s32[8]{0:T(128)S(1)} %select_reduce_fusion.refs_0_, f32[8,128,256]{2,1,0:T(8,128)S(1)} %get-tuple-element.16.refs_1_, bf16[8,128,256]{2,1,0:T(8,128)(2,1)S(1)} %all-to-all-done.1.refs_2_, f32[16,128]{1,0:T(8,128)S(1)} %add.41.refs_3_, f32[8,2304]{1,0:T(8,128)S(1)} %pad_convert_fusion.refs_4_, ...), custom_call_target="tpu_custom_call" | custom-call | tf_op jit(solution)/shard_map/long/pallas_call | solution.py:384
  60.4 0.0 copy-start.5
  60.4 16.6 %all_to_all.15.mixed_ref = bf16[8,128,256]{2,1,0:T(8,128)(2,1)S(1)} all-to-all(bf16[8,128,256]{2,1,0:T(8,128)(2,1)S(1)} %long.1), channel_id=1, replica_groups=mesh['ctx'=8,'tp'=4] {'ctx'}, dimensions={0} | all-to-all | bytes 1048576 | tf_op jit(solution)/shard_map/all_to_all | solution.py:419
  77.0 0.0 copy-done.5
  77.0 1.0 %gate.1 = bf16[256,1024]{1,0:T(8,128)(2,1)} custom-call(bf16[8,128,256]{2,1,0:T(8,128)(2,1)S(1)} %all_to_all.15.mixed_ref, bf16[256,1024]{1,0:T(8,128)(2,1)S(1)} %copy-done.5), custom_call_target="tpu_custom_call" | custom-call | tf_op jit(solution)/shard_map/gate/pallas_call | solution.py:407
  (14 shorter events, 0.1 us)
Async XLA Ops:
  0.0 51.5 %copy-start = (f32[1024]{0:T(1024)S(1)}, f32[1024]{0:T(1024)}, u32[]{:S(2)}) copy-start(f32[1024]{0:T(1024)} %param.19) | copy-start | bytes 12292
  0.0 11.3 %copy-start.4 = (bf16[256,1024]{1,0:T(8,128)(2,1)S(1)}, bf16[256,1024]{1,0:T(8,128)(2,1)}, u32[]{:S(2)}) copy-start(bf16[256,1024]{1,0:T(8,128)(2,1)} %refs_2_.3) | copy-start | bytes 1572868
  3.7 7.4 %copy-start.7 = (bf16[128,64]{0,1:T(8,128)(2,1)S(1)}, bf16[128,64]{0,1:T(8,128)(2,1)}, u32[]{:S(2)}) copy-start(bf16[128,64]{0,1:T(8,128)(2,1)} %param.17) | copy-start | bytes 49156
  3.7 7.6 %copy-start.1 = (bf16[256,1024]{1,0:T(8,128)(2,1)S(1)}, bf16[256,1024]{1,0:T(8,128)(2,1)}, u32[]{:S(2)}) copy-start(bf16[256,1024]{1,0:T(8,128)(2,1)} %refs_0_.5) | copy-start | bytes 1572868
  3.7 7.6 %copy-start.2 = (bf16[256,1024]{1,0:T(8,128)(2,1)S(1)}, bf16[256,1024]{1,0:T(8,128)(2,1)}, u32[]{:S(2)}) copy-start(bf16[256,1024]{1,0:T(8,128)(2,1)} %refs_0_.4) | copy-start | bytes 1572868
  3.7 7.6 %copy-start.3 = (bf16[256,1024]{1,0:T(8,128)(2,1)S(1)}, bf16[256,1024]{1,0:T(8,128)(2,1)}, u32[]{:S(2)}) copy-start(bf16[256,1024]{1,0:T(8,128)(2,1)} %refs_1_.3) | copy-start | bytes 1572868
  3.7 30.4 %all-to-all-start = ((bf16[8,224,256]{2,1,0:T(8,128)(2,1)}), bf16[8,224,256]{2,1,0:T(8,128)(2,1)S(1)}, u32[]{:S(2)}, u32[]{:S(2)}) async-start(bf16[8,224,256]{2,1,0:T(8,128)(2,1)} %pack.1), calls=%async_computation | async-start | bytes 1835008 | tf_op jit(solution)/shard_map/all_to_all | solution.py:419
  11.2 0.7 copy-start.6
  15.2 1.2 %collective-permute-start = (f32[1,128]{1,0:T(1,128)S(1)}, f32[1,128]{1,0:T(1,128)S(1)}, u32[]{:S(2)}, u32[]{:S(2)}) collective-permute-start(f32[1,128]{1,0:T(1,128)S(1)} %get-tuple-element.14), channel_id=1, source_target_pairs={{0,1},{1,0},{2,3},{3,2},{4,5},{5,4},{6,7},{7,6},{8,9},{9,8},{10,11... | collective-permute-start | bytes 1544 | tf_op jit(solution)/shard_map/ppermute | solution.py:427
  16.1 1.9 %copy-start.8 = (s32[8]{0:T(128)S(1)}, s32[8]{0:T(128)}, u32[]{:S(2)}) copy-start(s32[8]{0:T(128)} %param.20) | copy-start | bytes 100
  16.4 3.5 %collective-permute-start.1 = (f32[1,128]{1,0:T(1,128)S(1)}, f32[1,128]{1,0:T(1,128)S(1)}, u32[]{:S(2)}, u32[]{:S(2)}) collective-permute-start(f32[1,128]{1,0:T(1,128)S(1)} %add.34), channel_id=1, source_target_pairs={{0,2},{1,3},{2,0},{3,1},{4,6},{5,7},{6,4},{7,5},{8,10},{9,11},{10,... | collective-permute-start | bytes 1544 | tf_op jit(solution)/shard_map/ppermute | solution.py:427
  37.4 20.4 %all-to-all-start.1 = ((bf16[8,128,256]{2,1,0:T(8,128)(2,1)}), bf16[8,128,256]{2,1,0:T(8,128)(2,1)S(1)}, u32[]{:S(2)}, u32[]{:S(2)}) async-start(bf16[8,128,256]{2,1,0:T(8,128)(2,1)} %join.1), calls=%async_computation.1 | async-start | bytes 1048576 | tf_op jit(solution)/shard_map/all_to_all | solution.py:419
  41.0 1.2 %collective-permute-start.2 = (f32[16,128]{1,0:T(8,128)S(1)}, f32[16,128]{1,0:T(8,128)S(1)}, u32[]{:S(2)}, u32[]{:S(2)}) collective-permute-start(f32[16,128]{1,0:T(8,128)S(1)} %get-tuple-element.20), channel_id=1, source_target_pairs={{0,1},{1,0},{2,3},{3,2},{4,5},{5,4},{6,7},{7,6},{8,9},{9,8},{10,11... | collective-permute-start | bytes 24584 | tf_op jit(solution)/shard_map/ppermute | solution.py:427
  42.2 3.7 %collective-permute-start.3 = (f32[16,128]{1,0:T(8,128)S(1)}, f32[16,128]{1,0:T(8,128)S(1)}, u32[]{:S(2)}, u32[]{:S(2)}) collective-permute-start(f32[16,128]{1,0:T(8,128)S(1)} %add.37), channel_id=1, source_target_pairs={{0,2},{1,3},{2,0},{3,1},{4,6},{5,7},{6,4},{7,5},{8,10},{9,11},{10,... | collective-permute-start | bytes 24584 | tf_op jit(solution)/shard_map/ppermute | solution.py:427
  45.8 3.7 %collective-permute-start.4 = (f32[16,128]{1,0:T(8,128)S(1)}, f32[16,128]{1,0:T(8,128)S(1)}, u32[]{:S(2)}, u32[]{:S(2)}) collective-permute-start(f32[16,128]{1,0:T(8,128)S(1)} %add.38), channel_id=1, source_target_pairs={{0,4},{4,0},{8,12},{12,8},{16,20},{20,16},{24,28},{28,24},{1,5},{5... | collective-permute-start | bytes 24584 | tf_op jit(solution)/shard_map/ppermute | solution.py:427
  49.6 3.7 %collective-permute-start.5 = (f32[16,128]{1,0:T(8,128)S(1)}, f32[16,128]{1,0:T(8,128)S(1)}, u32[]{:S(2)}, u32[]{:S(2)}) collective-permute-start(f32[16,128]{1,0:T(8,128)S(1)} %add.39), channel_id=1, source_target_pairs={{0,8},{4,12},{8,0},{12,4},{16,24},{20,28},{24,16},{28,20},{1,9},{5... | collective-permute-start | bytes 24584 | tf_op jit(solution)/shard_map/ppermute | solution.py:427
  53.2 4.5 %collective-permute-start.6 = (f32[16,128]{1,0:T(8,128)S(1)}, f32[16,128]{1,0:T(8,128)S(1)}, u32[]{:S(2)}, u32[]{:S(2)}) collective-permute-start(f32[16,128]{1,0:T(8,128)S(1)} %add.40), channel_id=1, source_target_pairs={{0,16},{4,20},{8,24},{12,28},{16,0},{20,4},{24,8},{28,12},{1,17},{... | collective-permute-start | bytes 24584 | tf_op jit(solution)/shard_map/ppermute | solution.py:427
  60.4 16.6 %copy-start.5 = (bf16[256,1024]{1,0:T(8,128)(2,1)S(1)}, bf16[256,1024]{1,0:T(8,128)(2,1)}, u32[]{:S(2)}) copy-start(bf16[256,1024]{1,0:T(8,128)(2,1)} %gate_ref.1) | copy-start | bytes 1572868

commit v7 on v6

--- a/solution.py
+++ b/solution.py
@@ -9,7 +9,7 @@
 LANES = 128
 EDGE = 8
 VMEM_BYTES = 24 * 1024 * 1024
-PACK_TILES = 2
+PACK_TILES = 4
 GATE_TILES = 4
 F32 = jnp.float32
 BF16 = jnp.bfloat16
@@ -223,13 +223,15 @@
     ends_ref,
     more_ref,
     taps_ref,
-    column_ref,
+    q_base_ref,
     base_ref,
     out_ref,
     energy_ref,
     extended_ref,
     q_ends_ref,
-    squares_ref,
+    q_ref,
+    z_ref,
+    medium_ref,
 ):
     blocks, shard, rows = out_ref.shape
     halves = rows // LANES
@@ -249,54 +251,59 @@
         features.append(
             short_filter(extended_ref.at[which], taps_ref[which + 1], EDGE, blocks * span)
         )
-    starts = jnp.transpose((features[0] * features[1]).astype(BF16).astype(F32))
+    starts = jnp.transpose((features[0] * features[1]).astype(BF16))
     wide = blocks * span
     for b in range(blocks):
         before = more[b - 1][:, shard:] if b else jnp.zeros((EDGE, shard), F32)
         q_ends_ref[b * span : (b + 1) * span] = jnp.concatenate([before, more[b][:, :shard]], axis=0)
-    q_ends = jnp.transpose(q_ends_ref[...])
+    q_ends = jnp.transpose(q_ends_ref[...].astype(BF16))
+
+    lane = lax.broadcasted_iota(jnp.int32, (shard, LANES), 1)
+    if wide == LANES:
+        source = lax.broadcasted_iota(jnp.int32, (wide, blocks * LANES), 0)
+        target = lax.broadcasted_iota(jnp.int32, (wide, blocks * LANES), 1)
+        place = ((target + target // LANES * span + EDGE - source) % wide == 0).astype(F32).astype(BF16)
+        both = jnp.dot(
+            jnp.concatenate([starts, q_ends], axis=0), place, preferred_element_type=F32
+        )
+        firsts = [both[:shard, b * LANES : (b + 1) * LANES] for b in range(blocks)]
+        arounds = [both[shard:, b * LANES : (b + 1) * LANES] for b in range(blocks)]
+    else:
+        firsts, arounds = [], []
+        for b in range(blocks):
+            shift = (wide - b * span - EDGE) % wide
+            firsts.append(pltpu.roll(starts.astype(F32), shift, 1)[:, :LANES])
+            turned = pltpu.roll(q_ends.astype(F32), shift, 1)
+            arounds.append(jnp.where(lane < EDGE, turned[:, :LANES], turned[:, wide - LANES :]))
+
     half = shard // 2
-
-    def q_first(holder, g):
-        if half % size == 0:
-            at = shard + g * size % half
-            beside = g * size // half * LANES
-            return moved_ref[holder, at : at + size, beside : beside + LANES].astype(F32)
+    z_ref[:, :LANES] = jnp.zeros((shard, LANES), BF16)
+    for b, holder in enumerate(holders):
+        at = LANES + b * rows
+        z_own = moved_ref[holder, :shard, :LANES].astype(F32)
+        z_ref[:, at : at + LANES] = jnp.where(lane < EDGE, firsts[b], z_own).astype(BF16)
+        z_ref[:, at + LANES : at + rows] = moved_ref[holder, :shard, LANES:]
         both = moved_ref[holder, shard : shard + half, :].astype(F32)
-        both = jnp.concatenate([both[:, :LANES], both[:, LANES:]], axis=0)
-        return both[g * size : (g + 1) * size]
-
-    lane = lax.broadcasted_iota(jnp.int32, (size, LANES), 1)
-
-    squares_ref[...] = jnp.zeros(squares_ref.shape, F32)
+        q_own = jnp.concatenate([both[:, :LANES], both[:, LANES:]], axis=0)
+        q_ref[b] = jnp.concatenate([q_own, arounds[b]], axis=1).astype(BF16)
     for g in range(shard // size):
         here = slice(g * size, (g + 1) * size)
-        z_seq = [jnp.zeros((size, LANES), BF16)]
-        q_feats = []
-        for b, holder in enumerate(holders):
-            z_block = moved_ref[holder, here, :]
-            first = pltpu.roll(starts[here], (wide - b * span - EDGE) % wide, 1)[:, :LANES]
-            z_first = jnp.where(lane < EDGE, first, z_block[:, :LANES].astype(F32)).astype(BF16)
-            z_seq.append(jnp.concatenate([z_first, z_block[:, LANES:]], axis=1))
-            before = pltpu.roll(q_ends[here], (wide + LANES - EDGE - b * span) % wide, 1)[:, :LANES]
-            after = pltpu.roll(q_ends[here], (wide - b * span - EDGE) % wide, 1)[:, :LANES]
-            q_block = jnp.concatenate([before, q_first(holder, g), after], axis=1)
-            q_feat = q_block * column_ref[here, 0:1]
-            for j in range(1, taps_ref.shape[1]):
-                q_feat = q_feat + pltpu.roll(q_block, j, 1) * column_ref[here, j : j + 1]
-            q_feats.append(q_feat)
-        z_seq = jnp.concatenate(z_seq, axis=1)
+        table = shifted_rows(q_base_ref[g : g + 1, :], 2 * LANES).astype(BF16)
+        left = jnp.concatenate([q_ref[b, here] for b in range(blocks)], axis=0)
+        q_feat = jnp.dot(left, table, preferred_element_type=F32)
+        for b in range(blocks):
+            out_ref[b, here] = q_feat[b * size : (b + 1) * size]
         table = shifted_rows(base_ref[g : g + 1, :], 2 * LANES)[:, :LANES].astype(BF16)
-        windows = [z_seq[:, o * LANES : (o + 2) * LANES] for o in range(blocks * halves)]
-        medium = jnp.dot(jnp.concatenate(windows, axis=0), table, preferred_element_type=F32)
-        for o in range(blocks * halves):
-            b, at = o // halves, (o % halves) * LANES
-            mixed = q_feats[b][:, LANES + at : 2 * LANES + at] * medium[o * size : (o + 1) * size]
-            if at:
-                mixed = jnp.where(lane < EDGE, mixed, 0.0)
-            out_ref[b, here, at : at + LANES] = mixed
-            squares_ref[o] += mixed * mixed
-    energy_ref[...] = jnp.sum(squares_ref[...], axis=1)
+        windows = [z_ref[here, o * LANES : (o + 2) * LANES] for o in range(blocks * halves)]
+        medium_ref[g] = jnp.dot(jnp.concatenate(windows, axis=0), table, preferred_element_type=F32)
+    for o in range(blocks * halves):
+        b, at = o // halves, (o % halves) * LANES
+        medium = medium_ref[:, o * size : (o + 1) * size, :].reshape(shard, LANES)
+        mixed = out_ref[b, :, at : at + LANES] * medium
+        if at:
+            mixed = jnp.where(lane < EDGE, mixed, 0.0)
+        out_ref[b, :, at : at + LANES] = mixed
+        energy_ref[o : o + 1, :] = jnp.sum(mixed * mixed, axis=0, keepdims=True)
 
 
 def call_mix(holder, moved, ends, more, short_local, medium_local, shard, rows):
@@ -306,6 +313,8 @@
     assert reach == LANES and short_local.shape[1] <= EDGE + 1
     lane_form = jnp.repeat(short_local, size, axis=2).astype(F32)
     base = jnp.pad(jnp.transpose(medium_local).astype(F32), ((0, 0), (LANES, 0)))
+    q_base = jnp.transpose(short_local[0]).astype(F32)
+    q_base = jnp.pad(q_base, ((0, 0), (0, rows - q_base.shape[1])))
 
     def kernel(*refs):
         mix_kernel(size, *refs)
@@ -322,11 +331,13 @@
         scratch_shapes=[
             pltpu.VMEM((2, EDGE + blocks * 2 * EDGE, shard), F32),
             pltpu.VMEM((blocks * 2 * EDGE, shard), F32),
-            pltpu.VMEM((blocks * rows // LANES, size, LANES), F32),
+            pltpu.VMEM((blocks, shard, rows), BF16),
+            pltpu.VMEM((shard, LANES + blocks * rows), BF16),
+            pltpu.VMEM((shard // size, blocks * rows // LANES * size, LANES), F32),
         ],
         compiler_params=params(),
         name="mix",
-    )(holder, moved, ends, more, lane_form, jnp.transpose(lane_form[0]), base)
+    )(holder, moved, ends, more, lane_form, q_base, base)
 
 
 def long_kernel(

time: 78.4 us -> 76.7 us (0.978)
  Pallas kernels: 14.8 us -> 13.1 us
    pallas_call x1, Pallas kernels: 3.25 us -> 1.64 us  [call_mix(): pl.pallas_call(kernel, in_specs=[pl.BlockSpec(memory_space=pltpu.SMEM)] +...]
where the time goes in v7:
time: 76.7 us; the launch traced here: 76.3 us
  waiting for transfers between devices  23.4 us (31%)
  starting transfers between devices  20.8 us (27%)
  blocking collectives  16.6 us (22%)
  Pallas kernels  13.1 us (17%)
  local copies, waits for them, and re-layouts  1.95 us (3%)
    all_to_all x1, blocking collectives, exchange(): return lax.all_to_all(array, 'ctx', split_axis=0, concat_axis=0, tiled=True)  16.6 us
    all_to_all x2, waiting for transfers between devices, exchange(): return lax.all_to_all(array, 'ctx', split_axis=0, concat_axis=0, tiled=True)  13.2 us
    all_to_all x2, starting transfers between devices, exchange(): return lax.all_to_all(array, 'ctx', split_axis=0, concat_axis=0, tiled=True)  10.9 us
    ppermute x7, waiting for transfers between devices, sum_by_pairs(): lax.ppermute(array, axis, [(i, i ^ bit) for i in range(count)])  10.2 us
    ppermute x7, starting transfers between devices, sum_by_pairs(): lax.ppermute(array, axis, [(i, i ^ bit) for i in range(count)])  9.84 us
    pallas_call x1, Pallas kernels, call_pack(): pl.pallas_call(kernel, in_specs=[pl.BlockSpec(memory_space=pltpu.HBM)] *...  3.54 us
    pallas_call x1, Pallas kernels, call_early(): pl.pallas_call(kernel, in_specs=[pl.BlockSpec(memory_space=pltpu.VMEM)] *...  3.31 us
    pallas_call x1, Pallas kernels, call_long(): pl.pallas_call(kernel, in_specs=[pl.BlockSpec(memory_space=pltpu.SMEM)] +...  2.58 us
  transfers between devices with their start and end apart: 9, of which 8 were waited for; matrix products, arithmetic and copies ran while one was open for 2% of the time, Pallas kernels for 6%

profile of v7, /device:TPU:0, one launch (start us, length us, event | category | flops | bytes accessed | tf_op | source)
XLA Modules:
  0.0 76.3 jit_solution(14388511355393835810)
XLA Ops:
  0.0 0.0 copy-start
  0.0 0.0 copy-start.4
  0.0 3.5 %pack.1 = bf16[8,224,256]{2,1,0:T(8,128)(2,1)} custom-call(bf16[256,1024]{1,0:T(8,128)(2,1)} %refs_0_.4, bf16[256,1024]{1,0:T(8,128)(2,1)} %refs_1_.3, bf16[256,1024]{1,0:T(8,128)(2,1)} %refs_2_.3, bf16[3,7,64]{2,1,0:T(8,128)(2,1)} %refs_4_.3, bf16[64,256]{1,0:T(8,128)(2,1)} %refs_4_.2), custom_call_target="tpu_custom_call" | custom-call | tf_op jit(solution)/shard_map/pack/pallas_call | solution.py:103
  3.6 0.0 copy-start.7
  3.6 0.0 copy-start.1
  3.6 0.0 copy-start.2
  3.6 0.0 copy-start.3
  3.6 7.4 %all-to-all-start = ((bf16[8,224,256]{2,1,0:T(8,128)(2,1)}), bf16[8,224,256]{2,1,0:T(8,128)(2,1)S(1)}, u32[]{:S(2)}, u32[]{:S(2)}) async-start(bf16[8,224,256]{2,1,0:T(8,128)(2,1)} %pack.1), calls=%async_computation | async-start | bytes 1835008 | tf_op jit(solution)/shard_map/all_to_all | solution.py:430
  11.0 0.0 copy-done.7
  11.0 0.1 rev.3
  11.1 0.0 copy-start.6
  11.1 0.1 pad_convert_fusion.1.refs_5_
  11.2 0.0 copy-done.4
  11.2 0.0 copy-done.1
  11.2 0.0 copy-done.2
  11.2 0.0 copy-done.3
  11.2 0.6 copy-done.6
  11.8 3.3 %early.1 = (f32[8,128,128]{2,1,0:T(8,128)S(1)}, f32[1,128]{1,0:T(1,128)S(1)}) custom-call(bf16[256,1024]{1,0:T(8,128)(2,1)S(1)} %copy-done.2, bf16[256,1024]{1,0:T(8,128)(2,1)S(1)} %copy-done.3, bf16[256,1024]{1,0:T(8,128)(2,1)S(1)} %copy-done.4, bf16[256,1024]{1,0:T(8,128)(2,1)S(1)} %copy-done.1, bf16[3,7,64]{2,1,0:T(8,128)(2,1)S(1)} %copy-done.6, ...), custom_call_target="tpu_custom_call" | custom-call | tf_op jit(solution)/shard_map/early/pallas_call | solution.py:178
  15.1 0.1 collective-permute-start
  15.2 0.1 dynamic-slice_bitcast_fusion
  15.3 0.1 copy.13
  15.4 0.7 dynamic-slice_bitcast_fusion.1
  16.0 0.1 dynamic-slice_convert_fusion
  16.1 0.0 copy-start.8
  16.1 0.2 collective-permute-done
  16.3 1.5 %collective-permute-start.1 = (f32[1,128]{1,0:T(1,128)S(1)}, f32[1,128]{1,0:T(1,128)S(1)}, u32[]{:S(2)}, u32[]{:S(2)}) collective-permute-start(f32[1,128]{1,0:T(1,128)S(1)} %add.36), channel_id=1, source_target_pairs={{0,2},{1,3},{2,0},{3,1},{4,6},{5,7},{6,4},{7,5},{8,10},{9,11},{10,... | collective-permute-start | bytes 1544 | tf_op jit(solution)/shard_map/ppermute | solution.py:438
  17.8 0.0 copy-done.8
  17.8 0.1 select_reduce_fusion.refs_0_
  17.9 0.1 broadcast_in_dim.20
  18.0 0.1 convert_element_type.36.refs_4_
  18.1 1.7 %collective-permute-done.1 = f32[1,128]{1,0:T(1,128)S(1)} collective-permute-done((f32[1,128]{1,0:T(1,128)S(1)}, f32[1,128]{1,0:T(1,128)S(1)}, u32[]{:S(2)}, u32[]{:S(2)}) %collective-permute-start.1) | collective-permute-done | bytes 544 | tf_op jit(solution)/shard_map/ppermute | solution.py:438
  19.8 1.0 %join.1 = bf16[8,128,256]{2,1,0:T(8,128)(2,1)} custom-call(bf16[256,1024]{1,0:T(8,128)(2,1)S(1)} %copy-done.1, f32[8,128,128]{2,1,0:T(8,128)S(1)} %get-tuple-element.13.refs_1_, f32[1,128]{1,0:T(1,128)S(1)} %add.37.refs_2_), custom_call_target="tpu_custom_call" | custom-call | tf_op jit(solution)/shard_map/join/pallas_call | solution.py:209
  20.8 13.2 %all-to-all-done.refs_1_ = bf16[8,224,256]{2,1,0:T(8,128)(2,1)S(1)} async-done(((bf16[8,224,256]{2,1,0:T(8,128)(2,1)}), bf16[8,224,256]{2,1,0:T(8,128)(2,1)S(1)}, u32[]{:S(2)}, u32[]{:S(2)}) %all-to-all-start) | async-done | bytes 917536 | tf_op jit(solution)/shard_map/all_to_all | solution.py:430
  34.0 1.6 %mix.1 = (f32[8,128,256]{2,1,0:T(8,128)S(1)}, f32[16,128]{1,0:T(8,128)S(1)}) custom-call(s32[8]{0:T(128)S(1)} %select_reduce_fusion.refs_0_, bf16[8,224,256]{2,1,0:T(8,128)(2,1)S(1)} %all-to-all-done.refs_1_, bf16[8,16,256]{2,1,0:T(8,128)(2,1)S(1)} %slice.16.refs_2_, bf16[8,8,256]{2,1,0:T(8,128)(2,1)S(1)} %slice.17.refs_3_, ...), custom_call_target="tpu_custom_call" | custom-call | tf_op jit(solution)/shard_map/mix/pallas_call | solution.py:322
  35.7 3.5 %all-to-all-start.1 = ((bf16[8,128,256]{2,1,0:T(8,128)(2,1)}), bf16[8,128,256]{2,1,0:T(8,128)(2,1)S(1)}, u32[]{:S(2)}, u32[]{:S(2)}) async-start(bf16[8,128,256]{2,1,0:T(8,128)(2,1)} %join.1), calls=%async_computation.1 | async-start | bytes 1048576 | tf_op jit(solution)/shard_map/all_to_all | solution.py:430
  39.2 0.1 collective-permute-start.2
  39.3 1.2 %collective-permute-done.2 = f32[16,128]{1,0:T(8,128)S(1)} collective-permute-done((f32[16,128]{1,0:T(8,128)S(1)}, f32[16,128]{1,0:T(8,128)S(1)}, u32[]{:S(2)}, u32[]{:S(2)}) %collective-permute-start.2) | collective-permute-done | bytes 8224 | tf_op jit(solution)/shard_map/ppermute | solution.py:438
  40.5 1.5 %collective-permute-start.3 = (f32[16,128]{1,0:T(8,128)S(1)}, f32[16,128]{1,0:T(8,128)S(1)}, u32[]{:S(2)}, u32[]{:S(2)}) collective-permute-start(f32[16,128]{1,0:T(8,128)S(1)} %add.39), channel_id=1, source_target_pairs={{0,2},{1,3},{2,0},{3,1},{4,6},{5,7},{6,4},{7,5},{8,10},{9,11},{10,... | collective-permute-start | bytes 24584 | tf_op jit(solution)/shard_map/ppermute | solution.py:438
  42.0 2.1 %collective-permute-done.3 = f32[16,128]{1,0:T(8,128)S(1)} collective-permute-done((f32[16,128]{1,0:T(8,128)S(1)}, f32[16,128]{1,0:T(8,128)S(1)}, u32[]{:S(2)}, u32[]{:S(2)}) %collective-permute-start.3) | collective-permute-done | bytes 8224 | tf_op jit(solution)/shard_map/ppermute | solution.py:438
  44.1 2.0 %collective-permute-start.4 = (f32[16,128]{1,0:T(8,128)S(1)}, f32[16,128]{1,0:T(8,128)S(1)}, u32[]{:S(2)}, u32[]{:S(2)}) collective-permute-start(f32[16,128]{1,0:T(8,128)S(1)} %add.40), channel_id=1, source_target_pairs={{0,4},{4,0},{8,12},{12,8},{16,20},{20,16},{24,28},{28,24},{1,5},{5... | collective-permute-start | bytes 24584 | tf_op jit(solution)/shard_map/ppermute | solution.py:438
  46.1 1.8 %collective-permute-done.4 = f32[16,128]{1,0:T(8,128)S(1)} collective-permute-done((f32[16,128]{1,0:T(8,128)S(1)}, f32[16,128]{1,0:T(8,128)S(1)}, u32[]{:S(2)}, u32[]{:S(2)}) %collective-permute-start.4) | collective-permute-done | bytes 8224 | tf_op jit(solution)/shard_map/ppermute | solution.py:438
  47.9 1.9 %collective-permute-start.5 = (f32[16,128]{1,0:T(8,128)S(1)}, f32[16,128]{1,0:T(8,128)S(1)}, u32[]{:S(2)}, u32[]{:S(2)}) collective-permute-start(f32[16,128]{1,0:T(8,128)S(1)} %add.41), channel_id=1, source_target_pairs={{0,8},{4,12},{8,0},{12,4},{16,24},{20,28},{24,16},{28,20},{1,9},{5... | collective-permute-start | bytes 24584 | tf_op jit(solution)/shard_map/ppermute | solution.py:438
  49.7 0.0 copy-done
  49.7 0.1 dynamic-slice_bitcast_fusion.2
  49.8 0.1 copy.14.refs_5_
  49.9 1.6 %collective-permute-done.5 = f32[16,128]{1,0:T(8,128)S(1)} collective-permute-done((f32[16,128]{1,0:T(8,128)S(1)}, f32[16,128]{1,0:T(8,128)S(1)}, u32[]{:S(2)}, u32[]{:S(2)}) %collective-permute-start.5) | collective-permute-done | bytes 8224 | tf_op jit(solution)/shard_map/ppermute | solution.py:438
  51.5 2.8 %collective-permute-start.6 = (f32[16,128]{1,0:T(8,128)S(1)}, f32[16,128]{1,0:T(8,128)S(1)}, u32[]{:S(2)}, u32[]{:S(2)}) collective-permute-start(f32[16,128]{1,0:T(8,128)S(1)} %add.42), channel_id=1, source_target_pairs={{0,16},{4,20},{8,24},{12,28},{16,0},{20,4},{24,8},{28,12},{1,17},{... | collective-permute-start | bytes 24584 | tf_op jit(solution)/shard_map/ppermute | solution.py:438
  54.3 1.7 %collective-permute-done.6 = f32[16,128]{1,0:T(8,128)S(1)} collective-permute-done((f32[16,128]{1,0:T(8,128)S(1)}, f32[16,128]{1,0:T(8,128)S(1)}, u32[]{:S(2)}, u32[]{:S(2)}) %collective-permute-start.6) | collective-permute-done | bytes 8224 | tf_op jit(solution)/shard_map/ppermute | solution.py:438
  56.1 0.0 all-to-all-done.1.refs_2_
  56.1 2.6 %long.1 = bf16[8,128,256]{2,1,0:T(8,128)(2,1)S(1)} custom-call(s32[8]{0:T(128)S(1)} %select_reduce_fusion.refs_0_, f32[8,128,256]{2,1,0:T(8,128)S(1)} %get-tuple-element.16.refs_1_, bf16[8,128,256]{2,1,0:T(8,128)(2,1)S(1)} %all-to-all-done.1.refs_2_, f32[16,128]{1,0:T(8,128)S(1)} %add.43.refs_3_, f32[8,2304]{1,0:T(8,128)S(1)} %pad_convert_fusion.refs_4_, ...), custom_call_target="tpu_custom_call" | custom-call | tf_op jit(solution)/shard_map/long/pallas_call | solution.py:395
  58.7 0.0 copy-start.5
  58.7 16.6 %all_to_all.15.mixed_ref = bf16[8,128,256]{2,1,0:T(8,128)(2,1)S(1)} all-to-all(bf16[8,128,256]{2,1,0:T(8,128)(2,1)S(1)} %long.1), channel_id=1, replica_groups=mesh['ctx'=8,'tp'=4] {'ctx'}, dimensions={0} | all-to-all | bytes 1048576 | tf_op jit(solution)/shard_map/all_to_all | solution.py:430
  75.3 0.0 copy-done.5
  75.3 1.0 %gate.1 = bf16[256,1024]{1,0:T(8,128)(2,1)} custom-call(bf16[8,128,256]{2,1,0:T(8,128)(2,1)S(1)} %all_to_all.15.mixed_ref, bf16[256,1024]{1,0:T(8,128)(2,1)S(1)} %copy-done.5), custom_call_target="tpu_custom_call" | custom-call | tf_op jit(solution)/shard_map/gate/pallas_call | solution.py:418
  (12 shorter events, 0.1 us)
Async XLA Ops:
  0.0 49.7 %copy-start = (f32[1024]{0:T(1024)S(1)}, f32[1024]{0:T(1024)}, u32[]{:S(2)}) copy-start(f32[1024]{0:T(1024)} %param.19) | copy-start | bytes 12292
  0.0 11.2 %copy-start.4 = (bf16[256,1024]{1,0:T(8,128)(2,1)S(1)}, bf16[256,1024]{1,0:T(8,128)(2,1)}, u32[]{:S(2)}) copy-start(bf16[256,1024]{1,0:T(8,128)(2,1)} %refs_2_.3) | copy-start | bytes 1572868
  3.6 7.4 %copy-start.7 = (bf16[128,64]{0,1:T(8,128)(2,1)S(1)}, bf16[128,64]{0,1:T(8,128)(2,1)}, u32[]{:S(2)}) copy-start(bf16[128,64]{0,1:T(8,128)(2,1)} %param.17) | copy-start | bytes 49156
  3.6 7.6 %copy-start.1 = (bf16[256,1024]{1,0:T(8,128)(2,1)S(1)}, bf16[256,1024]{1,0:T(8,128)(2,1)}, u32[]{:S(2)}) copy-start(bf16[256,1024]{1,0:T(8,128)(2,1)} %refs_0_.5) | copy-start | bytes 1572868
  3.6 7.6 %copy-start.2 = (bf16[256,1024]{1,0:T(8,128)(2,1)S(1)}, bf16[256,1024]{1,0:T(8,128)(2,1)}, u32[]{:S(2)}) copy-start(bf16[256,1024]{1,0:T(8,128)(2,1)} %refs_0_.4) | copy-start | bytes 1572868
  3.6 7.6 %copy-start.3 = (bf16[256,1024]{1,0:T(8,128)(2,1)S(1)}, bf16[256,1024]{1,0:T(8,128)(2,1)}, u32[]{:S(2)}) copy-start(bf16[256,1024]{1,0:T(8,128)(2,1)} %refs_1_.3) | copy-start | bytes 1572868
  3.6 30.4 %all-to-all-start = ((bf16[8,224,256]{2,1,0:T(8,128)(2,1)}), bf16[8,224,256]{2,1,0:T(8,128)(2,1)S(1)}, u32[]{:S(2)}, u32[]{:S(2)}) async-start(bf16[8,224,256]{2,1,0:T(8,128)(2,1)} %pack.1), calls=%async_computation | async-start | bytes 1835008 | tf_op jit(solution)/shard_map/all_to_all | solution.py:430
  11.1 0.7 copy-start.6
  15.1 1.2 %collective-permute-start = (f32[1,128]{1,0:T(1,128)S(1)}, f32[1,128]{1,0:T(1,128)S(1)}, u32[]{:S(2)}, u32[]{:S(2)}) collective-permute-start(f32[1,128]{1,0:T(1,128)S(1)} %get-tuple-element.14), channel_id=1, source_target_pairs={{0,1},{1,0},{2,3},{3,2},{4,5},{5,4},{6,7},{7,6},{8,9},{9,8},{10,11... | collective-permute-start | bytes 1544 | tf_op jit(solution)/shard_map/ppermute | solution.py:438
  16.1 1.7 %copy-start.8 = (s32[8]{0:T(128)S(1)}, s32[8]{0:T(128)}, u32[]{:S(2)}) copy-start(s32[8]{0:T(128)} %param.20) | copy-start | bytes 100
  16.3 3.5 %collective-permute-start.1 = (f32[1,128]{1,0:T(1,128)S(1)}, f32[1,128]{1,0:T(1,128)S(1)}, u32[]{:S(2)}, u32[]{:S(2)}) collective-permute-start(f32[1,128]{1,0:T(1,128)S(1)} %add.36), channel_id=1, source_target_pairs={{0,2},{1,3},{2,0},{3,1},{4,6},{5,7},{6,4},{7,5},{8,10},{9,11},{10,... | collective-permute-start | bytes 1544 | tf_op jit(solution)/shard_map/ppermute | solution.py:438
  35.7 20.4 %all-to-all-start.1 = ((bf16[8,128,256]{2,1,0:T(8,128)(2,1)}), bf16[8,128,256]{2,1,0:T(8,128)(2,1)S(1)}, u32[]{:S(2)}, u32[]{:S(2)}) async-start(bf16[8,128,256]{2,1,0:T(8,128)(2,1)} %join.1), calls=%async_computation.1 | async-start | bytes 1048576 | tf_op jit(solution)/shard_map/all_to_all | solution.py:430
  39.2 1.2 %collective-permute-start.2 = (f32[16,128]{1,0:T(8,128)S(1)}, f32[16,128]{1,0:T(8,128)S(1)}, u32[]{:S(2)}, u32[]{:S(2)}) collective-permute-start(f32[16,128]{1,0:T(8,128)S(1)} %get-tuple-element.20), channel_id=1, source_target_pairs={{0,1},{1,0},{2,3},{3,2},{4,5},{5,4},{6,7},{7,6},{8,9},{9,8},{10,11... | collective-permute-start | bytes 24584 | tf_op jit(solution)/shard_map/ppermute | solution.py:438
  40.5 3.7 %collective-permute-start.3 = (f32[16,128]{1,0:T(8,128)S(1)}, f32[16,128]{1,0:T(8,128)S(1)}, u32[]{:S(2)}, u32[]{:S(2)}) collective-permute-start(f32[16,128]{1,0:T(8,128)S(1)} %add.39), channel_id=1, source_target_pairs={{0,2},{1,3},{2,0},{3,1},{4,6},{5,7},{6,4},{7,5},{8,10},{9,11},{10,... | collective-permute-start | bytes 24584 | tf_op jit(solution)/shard_map/ppermute | solution.py:438
  44.1 3.7 %collective-permute-start.4 = (f32[16,128]{1,0:T(8,128)S(1)}, f32[16,128]{1,0:T(8,128)S(1)}, u32[]{:S(2)}, u32[]{:S(2)}) collective-permute-start(f32[16,128]{1,0:T(8,128)S(1)} %add.40), channel_id=1, source_target_pairs={{0,4},{4,0},{8,12},{12,8},{16,20},{20,16},{24,28},{28,24},{1,5},{5... | collective-permute-start | bytes 24584 | tf_op jit(solution)/shard_map/ppermute | solution.py:438
  47.9 3.7 %collective-permute-start.5 = (f32[16,128]{1,0:T(8,128)S(1)}, f32[16,128]{1,0:T(8,128)S(1)}, u32[]{:S(2)}, u32[]{:S(2)}) collective-permute-start(f32[16,128]{1,0:T(8,128)S(1)} %add.41), channel_id=1, source_target_pairs={{0,8},{4,12},{8,0},{12,4},{16,24},{20,28},{24,16},{28,20},{1,9},{5... | collective-permute-start | bytes 24584 | tf_op jit(solution)/shard_map/ppermute | solution.py:438
  51.5 4.5 %collective-permute-start.6 = (f32[16,128]{1,0:T(8,128)S(1)}, f32[16,128]{1,0:T(8,128)S(1)}, u32[]{:S(2)}, u32[]{:S(2)}) collective-permute-start(f32[16,128]{1,0:T(8,128)S(1)} %add.42), channel_id=1, source_target_pairs={{0,16},{4,20},{8,24},{12,28},{16,0},{20,4},{24,8},{28,12},{1,17},{... | collective-permute-start | bytes 24584 | tf_op jit(solution)/shard_map/ppermute | solution.py:438
  58.7 16.6 %copy-start.5 = (bf16[256,1024]{1,0:T(8,128)(2,1)S(1)}, bf16[256,1024]{1,0:T(8,128)(2,1)}, u32[]{:S(2)}) copy-start(bf16[256,1024]{1,0:T(8,128)(2,1)} %gate_ref.1) | copy-start | bytes 1572868

commit v8 on v7

--- a/solution.py
+++ b/solution.py
@@ -341,7 +341,7 @@
 
 
 def long_kernel(
-    full_width, size, holder_ref, mixed_ref, key_ref, energy_ref, window_ref, gain_ref, out_ref, ordered_ref
+    full_width, size, holder_ref, mixed_ref, key_ref, energy_ref, window_ref, gain_ref, out_ref, ordered_ref, strip_ref
 ):
     blocks, shard, rows = mixed_ref.shape
     half = rows // 2
@@ -359,6 +359,8 @@
             key = key_ref[holder, here].astype(F32)
             value = jnp.where(own, key, key * mixed_ref[b, here] * line)
             ordered_ref[g, reach + b * size : reach + (b + 1) * size] = value.astype(BF16)
+    for slot in range(window_ref.shape[0]):
+        strip_ref[slot] = shifted_rows(window_ref[slot : slot + 1, :], half)[:, half:].astype(BF16)
     for g in range(shard // size):
         here = slice(g * size, (g + 1) * size)
         ordered_ref[g, :reach] = jnp.zeros((reach, rows), BF16)
@@ -372,10 +374,9 @@
                 ],
                 axis=1,
             )
-            strip = shifted_rows(window_ref[slot : slot + 1, :], half).astype(BF16)
             right = jnp.concatenate(
                 [
-                    strip[:, shift : shift + rows]
+                    strip_ref[slot, :, shift - half : shift - half + rows]
                     for lag in range(1, lags + 1)
                     for shift in (lag * rows, lag * rows - half)
                 ],
@@ -398,30 +399,40 @@
         + [pl.BlockSpec(memory_space=pltpu.VMEM)] * 5,
         out_specs=pl.BlockSpec(memory_space=pltpu.VMEM),
         out_shape=jax.ShapeDtypeStruct((blocks, shard, rows), BF16),
-        scratch_shapes=[pltpu.VMEM((shard // size, 2 * blocks * size, rows), BF16)],
+        scratch_shapes=[pltpu.VMEM((shard // size, 2 * blocks * size, rows), BF16), pltpu.VMEM((windows.shape[0], rows // 2, windows.shape[1] - rows // 2), BF16)],
         compiler_params=params(),
         name="long",
     )(holder, mixed, keys, energy, windows, gain)
 
 
-def gate_kernel(mixed_ref, gate_ref, out_ref):
+def gate_kernel(mixed_ref, gate_ref, out_hbm, out_ref, sems):
+    copies = []
     for t in range(mixed_ref.shape[0]):
         lanes = slice(t * LANES, (t + 1) * LANES)
         mixed = jnp.transpose(mixed_ref[t]).astype(F32)
         out_ref[:, lanes] = (gate_ref[:, lanes].astype(F32) * mixed).astype(BF16)
+        if (t + 1) % GATE_TILES == 0:
+            part = t // GATE_TILES
+            done = pl.ds(part * GATE_TILES * LANES, GATE_TILES * LANES)
+            copy = pltpu.make_async_copy(out_ref.at[:, done], out_hbm.at[:, done], sems.at[part])
+            copy.start()
+            copies.append(copy)
+    for copy in copies:
+        copy.wait()
 
 
 def call_gate(mixed, q_two):
     rows, width = q_two.shape
-    wide = GATE_TILES * LANES
-    column = pl.BlockSpec((rows, wide), lambda i: (0, i))
     return pl.pallas_call(
         gate_kernel,
-        grid=(width // wide,),
-        in_specs=[pl.BlockSpec((GATE_TILES, LANES, rows), lambda i: (i, 0, 0)), column],
-        out_specs=column,
-        out_shape=jax.ShapeDtypeStruct((rows, width), BF16),
-        compiler_params=params("arbitrary"),
+        in_specs=[pl.BlockSpec(memory_space=pltpu.VMEM)] * 2,
+        out_specs=pl.BlockSpec(memory_space=pltpu.HBM),
+        out_shape=pltpu.HBM((rows, width), BF16),
+        scratch_shapes=[
+            pltpu.VMEM((rows, width), BF16),
+            pltpu.SemaphoreType.DMA((width // LANES // GATE_TILES,)),
+        ],
+        compiler_params=params(),
         name="gate",
     )(mixed, q_two)
 
@@ -438,6 +449,21 @@
         array = array + lax.ppermute(array, axis, [(i, i ^ bit) for i in range(count)])
         bit *= 2
     return array
+
+
+def sum_over_all(array):
+    axes = ("ctx", "tp")
+    count = lax.axis_size("ctx") * lax.axis_size("tp")
+    assert count & (count - 1) == 0
+    masks, bit = [1], 2
+    while True:
+        parts = [lax.ppermute(array, axes, [(i, i ^ mask) for i in range(count)]) for mask in masks]
+        for part in parts:
+            array = array + part
+        if bit >= count:
+            return array
+        masks = [bit, 2 * bit, 3 * bit] if 2 * bit < count else [bit]
+        bit *= 4
 
 
 def per_device(
@@ -496,7 +522,7 @@
     mixed, energy = call_mix(holder, moved, ends, more, short_local, medium_local, shard, rows)
     energy, joined = lax.optimization_barrier((energy, joined))
     keys = exchange(joined.reshape(ctx_count, shard, rows))
-    energy = sum_by_pairs(sum_by_pairs(energy, "tp"), "ctx")
+    energy = sum_over_all(energy)
 
     long_rows = moved[:, taps_at : taps_at + shard_groups]
     long_rows = jnp.transpose(long_rows, (1, 0, 2)).reshape(shard_groups, ctx_count * rows)

time: 76.7 us -> 76.3 us (level)
    ppermute x7 -> x2, waiting for transfers between devices: 10.2 us -> 1.87 us  [sum_by_pairs(): lax.ppermute(array, axis, [(i, i ^ bit) for i in range(count)])]
    ppermute x7 -> x2, starting transfers between devices: 9.84 us -> 1.59 us  [sum_by_pairs(): lax.ppermute(array, axis, [(i, i ^ bit) for i in range(count)])]
    ppermute x0 -> x7, starting transfers between devices: none -> 7.97 us  [sum_over_all(): lax.ppermute(array, axes, [(i, i ^ mask) for i in range(count)])]
    ppermute x0 -> x7, waiting for transfers between devices: none -> 7.97 us  [sum_over_all(): lax.ppermute(array, axes, [(i, i ^ mask) for i in range(count)])]
  transfers between devices with their start and end apart: 9 -> 11, of which waited for: 8 -> 8; matrix products, arithmetic and copies ran while one was open for 2% -> 2% of each run, Pallas kernels for 6% -> 6%
where the time goes in v8:
time: 76.3 us; the launch traced here: 75.9 us
  waiting for transfers between devices  23.1 us (30%)
  starting transfers between devices  20.5 us (27%)
  blocking collectives  17.1 us (22%)
  Pallas kernels  12.9 us (17%)
  local copies, waits for them, and re-layouts  1.95 us (3%)
    all_to_all x1, blocking collectives, exchange(): return lax.all_to_all(array, 'ctx', split_axis=0, concat_axis=0, tiled=True)  17.1 us
    all_to_all x2, waiting for transfers between devices, exchange(): return lax.all_to_all(array, 'ctx', split_axis=0, concat_axis=0, tiled=True)  13.2 us
    all_to_all x2, starting transfers between devices, exchange(): return lax.all_to_all(array, 'ctx', split_axis=0, concat_axis=0, tiled=True)  10.9 us
    ppermute x7, starting transfers between devices, sum_over_all(): lax.ppermute(array, axes, [(i, i ^ mask) for i in range(count)])  7.97 us
    ppermute x7, waiting for transfers between devices, sum_over_all(): lax.ppermute(array, axes, [(i, i ^ mask) for i in range(count)])  7.97 us
    pallas_call x1, Pallas kernels, call_pack(): pl.pallas_call(kernel, in_specs=[pl.BlockSpec(memory_space=pltpu.HBM)] *...  3.56 us
    pallas_call x1, Pallas kernels, call_early(): pl.pallas_call(kernel, in_specs=[pl.BlockSpec(memory_space=pltpu.VMEM)] *...  3.31 us
    pallas_call x1, Pallas kernels, call_long(): pl.pallas_call(kernel, in_specs=[pl.BlockSpec(memory_space=pltpu.SMEM)] +...  2.42 us
  transfers between devices with their start and end apart: 11, of which 8 were waited for; matrix products, arithmetic and copies ran while one was open for 2% of the time, Pallas kernels for 6%

profile of v8, /device:TPU:0, one launch (start us, length us, event | category | flops | bytes accessed | tf_op | source)
XLA Modules:
  0.0 75.9 jit_solution(14724062525606237118)
XLA Ops:
  0.0 0.0 copy-start
  0.0 0.0 copy-start.5
  0.0 3.6 %pack.1 = bf16[8,224,256]{2,1,0:T(8,128)(2,1)} custom-call(bf16[256,1024]{1,0:T(8,128)(2,1)} %refs_0_.4, bf16[256,1024]{1,0:T(8,128)(2,1)} %refs_1_.3, bf16[256,1024]{1,0:T(8,128)(2,1)} %refs_2_.3, bf16[3,7,64]{2,1,0:T(8,128)(2,1)} %refs_4_.3, bf16[64,256]{1,0:T(8,128)(2,1)} %refs_4_.2), custom_call_target="tpu_custom_call" | custom-call | tf_op jit(solution)/shard_map/pack/pallas_call | solution.py:103
  3.6 0.0 copy-start.8
  3.6 0.0 copy-start.2
  3.6 0.0 copy-start.3
  3.6 0.0 copy-start.4
  3.6 7.4 %all-to-all-start = ((bf16[8,224,256]{2,1,0:T(8,128)(2,1)}), bf16[8,224,256]{2,1,0:T(8,128)(2,1)S(1)}, u32[]{:S(2)}, u32[]{:S(2)}) async-start(bf16[8,224,256]{2,1,0:T(8,128)(2,1)} %pack.1), calls=%async_computation | async-start | bytes 1835008 | tf_op jit(solution)/shard_map/all_to_all | solution.py:441
  11.0 0.0 copy-done.8
  11.0 0.1 rev.3
  11.1 0.0 copy-start.7
  11.1 0.1 pad_convert_fusion.1.refs_5_
  11.2 0.0 copy-done.5
  11.2 0.0 copy-done.2
  11.2 0.0 copy-done.3
  11.2 0.0 copy-done.4
  11.2 0.6 copy-done.7
  11.8 3.3 %early.1 = (f32[8,128,128]{2,1,0:T(8,128)S(1)}, f32[1,128]{1,0:T(1,128)S(1)}) custom-call(bf16[256,1024]{1,0:T(8,128)(2,1)S(1)} %copy-done.3, bf16[256,1024]{1,0:T(8,128)(2,1)S(1)} %copy-done.4, bf16[256,1024]{1,0:T(8,128)(2,1)S(1)} %copy-done.5, bf16[256,1024]{1,0:T(8,128)(2,1)S(1)} %copy-done.2, bf16[3,7,64]{2,1,0:T(8,128)(2,1)S(1)} %copy-done.7, ...), custom_call_target="tpu_custom_call" | custom-call | tf_op jit(solution)/shard_map/early/pallas_call | solution.py:178
  15.1 0.1 collective-permute-start
  15.2 0.1 dynamic-slice_bitcast_fusion
  15.3 0.1 copy.13
  15.4 0.7 dynamic-slice_bitcast_fusion.1
  16.1 0.1 dynamic-slice_convert_fusion
  16.1 0.0 copy-start.9
  16.1 0.2 collective-permute-done
  16.3 1.5 %collective-permute-start.1 = (f32[1,128]{1,0:T(1,128)S(1)}, f32[1,128]{1,0:T(1,128)S(1)}, u32[]{:S(2)}, u32[]{:S(2)}) collective-permute-start(f32[1,128]{1,0:T(1,128)S(1)} %add.42), channel_id=1, source_target_pairs={{0,2},{1,3},{2,0},{3,1},{4,6},{5,7},{6,4},{7,5},{8,10},{9,11},{10,... | collective-permute-start | bytes 1544 | tf_op jit(solution)/shard_map/ppermute | solution.py:449
  17.8 0.0 copy-done.9
  17.8 0.1 select_reduce_fusion.refs_0_
  17.9 0.1 broadcast_in_dim.20
  18.0 0.1 convert_element_type.36.refs_4_
  18.1 1.7 %collective-permute-done.1 = f32[1,128]{1,0:T(1,128)S(1)} collective-permute-done((f32[1,128]{1,0:T(1,128)S(1)}, f32[1,128]{1,0:T(1,128)S(1)}, u32[]{:S(2)}, u32[]{:S(2)}) %collective-permute-start.1) | collective-permute-done | bytes 544 | tf_op jit(solution)/shard_map/ppermute | solution.py:449
  19.8 1.0 %join.1 = bf16[8,128,256]{2,1,0:T(8,128)(2,1)} custom-call(bf16[256,1024]{1,0:T(8,128)(2,1)S(1)} %copy-done.2, f32[8,128,128]{2,1,0:T(8,128)S(1)} %get-tuple-element.13.refs_1_, f32[1,128]{1,0:T(1,128)S(1)} %add.43.refs_2_), custom_call_target="tpu_custom_call" | custom-call | tf_op jit(solution)/shard_map/join/pallas_call | solution.py:209
  20.8 13.2 %all-to-all-done.refs_1_ = bf16[8,224,256]{2,1,0:T(8,128)(2,1)S(1)} async-done(((bf16[8,224,256]{2,1,0:T(8,128)(2,1)}), bf16[8,224,256]{2,1,0:T(8,128)(2,1)S(1)}, u32[]{:S(2)}, u32[]{:S(2)}) %all-to-all-start) | async-done | bytes 917536 | tf_op jit(solution)/shard_map/all_to_all | solution.py:441
  34.0 0.0 copy-start.1
  34.1 1.6 %mix.1 = (f32[8,128,256]{2,1,0:T(8,128)S(1)}, f32[16,128]{1,0:T(8,128)S(1)}) custom-call(s32[8]{0:T(128)S(1)} %select_reduce_fusion.refs_0_, bf16[8,224,256]{2,1,0:T(8,128)(2,1)S(1)} %all-to-all-done.refs_1_, bf16[8,16,256]{2,1,0:T(8,128)(2,1)S(1)} %slice.16.refs_2_, bf16[8,8,256]{2,1,0:T(8,128)(2,1)S(1)} %slice.17.refs_3_, ...), custom_call_target="tpu_custom_call" | custom-call | tf_op jit(solution)/shard_map/mix/pallas_call | solution.py:322
  35.7 3.5 %all-to-all-start.1 = ((bf16[8,128,256]{2,1,0:T(8,128)(2,1)}), bf16[8,128,256]{2,1,0:T(8,128)(2,1)S(1)}, u32[]{:S(2)}, u32[]{:S(2)}) async-start(bf16[8,128,256]{2,1,0:T(8,128)(2,1)} %join.1), calls=%async_computation.1 | async-start | bytes 1048576 | tf_op jit(solution)/shard_map/all_to_all | solution.py:441
  39.3 0.1 collective-permute-start.2
  39.3 1.2 %collective-permute-done.2 = f32[16,128]{1,0:T(8,128)S(1)} collective-permute-done((f32[16,128]{1,0:T(8,128)S(1)}, f32[16,128]{1,0:T(8,128)S(1)}, u32[]{:S(2)}, u32[]{:S(2)}) %collective-permute-start.2) | collective-permute-done | bytes 8224 | tf_op jit(solution)/shard_map/ppermute | solution.py:460
  40.5 2.9 %collective-permute-start.5 = (f32[16,128]{1,0:T(8,128)S(1)}, f32[16,128]{1,0:T(8,128)S(1)}, u32[]{:S(2)}, u32[]{:S(2)}) collective-permute-start(f32[16,128]{1,0:T(8,128)S(1)} %add.45), channel_id=1, source_target_pairs={{0,6},{1,7},{2,4},{3,5},{4,2},{5,3},{6,0},{7,1},{8,14},{9,15},{10,... | collective-permute-start | bytes 24584 | tf_op jit(solution)/shard_map/ppermute | solution.py:460
  43.4 0.1 collective-permute-start.4
  43.5 0.5 collective-permute-start.3
  44.0 0.0 copy-done
  44.0 0.1 dynamic-slice_bitcast_fusion.2
  44.1 0.1 copy.14.refs_5_
  44.2 0.0 copy-done.1
  44.2 0.0 slice-start
  44.2 2.2 %collective-permute-done.5 = f32[16,128]{1,0:T(8,128)S(1)} collective-permute-done((f32[16,128]{1,0:T(8,128)S(1)}, f32[16,128]{1,0:T(8,128)S(1)}, u32[]{:S(2)}, u32[]{:S(2)}) %collective-permute-start.5) | collective-permute-done | bytes 8224 | tf_op jit(solution)/shard_map/ppermute | solution.py:460
  46.4 0.7 collective-permute-done.4
  47.1 0.0 collective-permute-done.3
  47.1 3.8 %collective-permute-start.8 = (f32[16,128]{1,0:T(8,128)S(1)}, f32[16,128]{1,0:T(8,128)S(1)}, u32[]{:S(2)}, u32[]{:S(2)}) collective-permute-start(f32[16,128]{1,0:T(8,128)S(1)} %add_add_fusion.1), channel_id=1, source_target_pairs={{0,24},{1,25},{2,26},{3,27},{4,28},{5,29},{6,30},{7,31},{8,16},{9,... | collective-permute-start | bytes 24584 | tf_op jit(solution)/shard_map/ppermute | solution.py:460
  50.9 0.0 collective-permute-start.7
  50.9 0.7 collective-permute-start.6
  51.5 0.0 slice-done
  51.6 1.1 %collective-permute-done.8 = f32[16,128]{1,0:T(8,128)S(1)} collective-permute-done((f32[16,128]{1,0:T(8,128)S(1)}, f32[16,128]{1,0:T(8,128)S(1)}, u32[]{:S(2)}, u32[]{:S(2)}) %collective-permute-start.8) | collective-permute-done | bytes 8224 | tf_op jit(solution)/shard_map/ppermute | solution.py:460
  52.6 2.8 %collective-permute-done.7 = f32[16,128]{1,0:T(8,128)S(1)} collective-permute-done((f32[16,128]{1,0:T(8,128)S(1)}, f32[16,128]{1,0:T(8,128)S(1)}, u32[]{:S(2)}, u32[]{:S(2)}) %collective-permute-start.7) | collective-permute-done | bytes 8224 | tf_op jit(solution)/shard_map/ppermute | solution.py:460
  55.4 0.0 collective-permute-done.6
  55.5 0.0 all-to-all-done.1.refs_2_
  55.5 2.4 %long.1 = bf16[8,128,256]{2,1,0:T(8,128)(2,1)S(1)} custom-call(s32[8]{0:T(128)S(1)} %select_reduce_fusion.refs_0_, f32[8,128,256]{2,1,0:T(8,128)S(1)} %get-tuple-element.16.refs_1_, bf16[8,128,256]{2,1,0:T(8,128)(2,1)S(1)} %all-to-all-done.1.refs_2_, f32[16,128]{1,0:T(8,128)S(1)} %add_add_fusion.refs_3_, f32[8,2304]{1,0:T(8,128)S(1)} %pad_convert_fusion.refs_4_, ...), custom_call_target="tpu_custom_call" | custom-call | tf_op jit(solution)/shard_map/long/pallas_call | solution.py:396
  57.9 0.0 copy-start.6
  57.9 17.1 %all_to_all.15.mixed_ref = bf16[8,128,256]{2,1,0:T(8,128)(2,1)S(1)} all-to-all(bf16[8,128,256]{2,1,0:T(8,128)(2,1)S(1)} %long.1), channel_id=1, replica_groups=mesh['ctx'=8,'tp'=4] {'ctx'}, dimensions={0} | all-to-all | bytes 1048576 | tf_op jit(solution)/shard_map/all_to_all | solution.py:441
  75.0 0.0 copy-done.6
  75.0 0.9 %gate.1 = bf16[256,1024]{1,0:T(8,128)(2,1)} custom-call(bf16[8,128,256]{2,1,0:T(8,128)(2,1)S(1)} %all_to_all.15.mixed_ref, bf16[256,1024]{1,0:T(8,128)(2,1)S(1)} %copy-done.6), custom_call_target="tpu_custom_call" | custom-call | tf_op jit(solution)/shard_map/gate/pallas_call | solution.py:426
  (9 shorter events, 0.0 us)
Async XLA Ops:
  0.0 44.0 %copy-start = (f32[1024]{0:T(1024)S(1)}, f32[1024]{0:T(1024)}, u32[]{:S(2)}) copy-start(f32[1024]{0:T(1024)} %param.19) | copy-start | bytes 12292
  0.0 11.2 %copy-start.5 = (bf16[256,1024]{1,0:T(8,128)(2,1)S(1)}, bf16[256,1024]{1,0:T(8,128)(2,1)}, u32[]{:S(2)}) copy-start(bf16[256,1024]{1,0:T(8,128)(2,1)} %refs_2_.3) | copy-start | bytes 1572868
  3.6 7.4 %copy-start.8 = (bf16[128,64]{0,1:T(8,128)(2,1)S(1)}, bf16[128,64]{0,1:T(8,128)(2,1)}, u32[]{:S(2)}) copy-start(bf16[128,64]{0,1:T(8,128)(2,1)} %param.17) | copy-start | bytes 49156
  3.6 7.6 %copy-start.2 = (bf16[256,1024]{1,0:T(8,128)(2,1)S(1)}, bf16[256,1024]{1,0:T(8,128)(2,1)}, u32[]{:S(2)}) copy-start(bf16[256,1024]{1,0:T(8,128)(2,1)} %refs_0_.5) | copy-start | bytes 1572868
  3.6 7.6 %copy-start.3 = (bf16[256,1024]{1,0:T(8,128)(2,1)S(1)}, bf16[256,1024]{1,0:T(8,128)(2,1)}, u32[]{:S(2)}) copy-start(bf16[256,1024]{1,0:T(8,128)(2,1)} %refs_0_.4) | copy-start | bytes 1572868
  3.6 7.6 %copy-start.4 = (bf16[256,1024]{1,0:T(8,128)(2,1)S(1)}, bf16[256,1024]{1,0:T(8,128)(2,1)}, u32[]{:S(2)}) copy-start(bf16[256,1024]{1,0:T(8,128)(2,1)} %refs_1_.3) | copy-start | bytes 1572868
  3.6 30.4 %all-to-all-start = ((bf16[8,224,256]{2,1,0:T(8,128)(2,1)}), bf16[8,224,256]{2,1,0:T(8,128)(2,1)S(1)}, u32[]{:S(2)}, u32[]{:S(2)}) async-start(bf16[8,224,256]{2,1,0:T(8,128)(2,1)} %pack.1), calls=%async_computation | async-start | bytes 1835008 | tf_op jit(solution)/shard_map/all_to_all | solution.py:441
  11.1 0.7 copy-start.7
  15.1 1.2 %collective-permute-start = (f32[1,128]{1,0:T(1,128)S(1)}, f32[1,128]{1,0:T(1,128)S(1)}, u32[]{:S(2)}, u32[]{:S(2)}) collective-permute-start(f32[1,128]{1,0:T(1,128)S(1)} %get-tuple-element.14), channel_id=1, source_target_pairs={{0,1},{1,0},{2,3},{3,2},{4,5},{5,4},{6,7},{7,6},{8,9},{9,8},{10,11... | collective-permute-start | bytes 1544 | tf_op jit(solution)/shard_map/ppermute | solution.py:449
  16.1 1.7 %copy-start.9 = (s32[8]{0:T(128)S(1)}, s32[8]{0:T(128)}, u32[]{:S(2)}) copy-start(s32[8]{0:T(128)} %param.20) | copy-start | bytes 100
  16.3 3.5 %collective-permute-start.1 = (f32[1,128]{1,0:T(1,128)S(1)}, f32[1,128]{1,0:T(1,128)S(1)}, u32[]{:S(2)}, u32[]{:S(2)}) collective-permute-start(f32[1,128]{1,0:T(1,128)S(1)} %add.42), channel_id=1, source_target_pairs={{0,2},{1,3},{2,0},{3,1},{4,6},{5,7},{6,4},{7,5},{8,10},{9,11},{10,... | collective-permute-start | bytes 1544 | tf_op jit(solution)/shard_map/ppermute | solution.py:449
  34.0 10.1 %copy-start.1 = (bf16[8,224,256]{2,1,0:T(8,128)(2,1)}, bf16[8,224,256]{2,1,0:T(8,128)(2,1)S(1)}, u32[]{:S(2)}) copy-start(bf16[8,224,256]{2,1,0:T(8,128)(2,1)S(1)} %all-to-all-done.refs_1_) | copy-start | bytes 2752516
  35.7 19.7 %all-to-all-start.1 = ((bf16[8,128,256]{2,1,0:T(8,128)(2,1)}), bf16[8,128,256]{2,1,0:T(8,128)(2,1)S(1)}, u32[]{:S(2)}, u32[]{:S(2)}) async-start(bf16[8,128,256]{2,1,0:T(8,128)(2,1)} %join.1), calls=%async_computation.1 | async-start | bytes 1048576 | tf_op jit(solution)/shard_map/all_to_all | solution.py:441
  39.3 1.2 %collective-permute-start.2 = (f32[16,128]{1,0:T(8,128)S(1)}, f32[16,128]{1,0:T(8,128)S(1)}, u32[]{:S(2)}, u32[]{:S(2)}) collective-permute-start(f32[16,128]{1,0:T(8,128)S(1)} %get-tuple-element.20), channel_id=1, source_target_pairs={{0,1},{1,0},{2,3},{3,2},{4,5},{5,4},{6,7},{7,6},{8,9},{9,8},{10,11... | collective-permute-start | bytes 24584 | tf_op jit(solution)/shard_map/ppermute | solution.py:460
  40.5 5.9 %collective-permute-start.5 = (f32[16,128]{1,0:T(8,128)S(1)}, f32[16,128]{1,0:T(8,128)S(1)}, u32[]{:S(2)}, u32[]{:S(2)}) collective-permute-start(f32[16,128]{1,0:T(8,128)S(1)} %add.45), channel_id=1, source_target_pairs={{0,6},{1,7},{2,4},{3,5},{4,2},{5,3},{6,0},{7,1},{8,14},{9,15},{10,... | collective-permute-start | bytes 24584 | tf_op jit(solution)/shard_map/ppermute | solution.py:460
  43.4 3.7 %collective-permute-start.4 = (f32[16,128]{1,0:T(8,128)S(1)}, f32[16,128]{1,0:T(8,128)S(1)}, u32[]{:S(2)}, u32[]{:S(2)}) collective-permute-start(f32[16,128]{1,0:T(8,128)S(1)} %add.45), channel_id=1, source_target_pairs={{0,4},{1,5},{2,6},{3,7},{4,0},{5,1},{6,2},{7,3},{8,12},{9,13},{10,... | collective-permute-start | bytes 24584 | tf_op jit(solution)/shard_map/ppermute | solution.py:460
  43.5 3.7 %collective-permute-start.3 = (f32[16,128]{1,0:T(8,128)S(1)}, f32[16,128]{1,0:T(8,128)S(1)}, u32[]{:S(2)}, u32[]{:S(2)}) collective-permute-start(f32[16,128]{1,0:T(8,128)S(1)} %add.45), channel_id=1, source_target_pairs={{0,2},{1,3},{2,0},{3,1},{4,6},{5,7},{6,4},{7,5},{8,10},{9,11},{10,... | collective-permute-start | bytes 24584 | tf_op jit(solution)/shard_map/ppermute | solution.py:460
  44.2 7.4 %slice-start = ((bf16[8,224,256]{2,1,0:T(8,128)(2,1)}), bf16[8,8,256]{2,1,0:T(8,128)(2,1)S(1)}, s32[]{:S(2)}) async-start(bf16[8,224,256]{2,1,0:T(8,128)(2,1)} %copy-done.1), calls=%async_computation.3 | async-start | bytes 65536 | tf_op jit(solution)/shard_map/slice | solution.py:527
  47.1 5.5 %collective-permute-start.8 = (f32[16,128]{1,0:T(8,128)S(1)}, f32[16,128]{1,0:T(8,128)S(1)}, u32[]{:S(2)}, u32[]{:S(2)}) collective-permute-start(f32[16,128]{1,0:T(8,128)S(1)} %add_add_fusion.1), channel_id=1, source_target_pairs={{0,24},{1,25},{2,26},{3,27},{4,28},{5,29},{6,30},{7,31},{8,16},{9,... | collective-permute-start | bytes 24584 | tf_op jit(solution)/shard_map/ppermute | solution.py:460
  50.9 4.5 %collective-permute-start.7 = (f32[16,128]{1,0:T(8,128)S(1)}, f32[16,128]{1,0:T(8,128)S(1)}, u32[]{:S(2)}, u32[]{:S(2)}) collective-permute-start(f32[16,128]{1,0:T(8,128)S(1)} %add_add_fusion.1), channel_id=1, source_target_pairs={{0,16},{1,17},{2,18},{3,19},{4,20},{5,21},{6,22},{7,23},{8,24},{9,... | collective-permute-start | bytes 24584 | tf_op jit(solution)/shard_map/ppermute | solution.py:460
  50.9 4.5 %collective-permute-start.6 = (f32[16,128]{1,0:T(8,128)S(1)}, f32[16,128]{1,0:T(8,128)S(1)}, u32[]{:S(2)}, u32[]{:S(2)}) collective-permute-start(f32[16,128]{1,0:T(8,128)S(1)} %add_add_fusion.1), channel_id=1, source_target_pairs={{0,8},{1,9},{2,10},{3,11},{4,12},{5,13},{6,14},{7,15},{8,0},{9,1},... | collective-permute-start | bytes 24584 | tf_op jit(solution)/shard_map/ppermute | solution.py:460
  57.9 17.1 %copy-start.6 = (bf16[256,1024]{1,0:T(8,128)(2,1)S(1)}, bf16[256,1024]{1,0:T(8,128)(2,1)}, u32[]{:S(2)}) copy-start(bf16[256,1024]{1,0:T(8,128)(2,1)} %gate_ref.1) | copy-start | bytes 1572868

commit v9 on v8

--- a/solution.py
+++ b/solution.py
@@ -39,12 +39,11 @@
 
 
 def pack_kernel(
-    size, q_hbm, k_hbm, v_hbm, taps_hbm, long_hbm, out_ref, q_ref, k_ref, v_ref, taps_ref, long_ref, wide_ref, sems
+    size, q_hbm, k_hbm, v_hbm, taps_hbm, out_hbm, q_ref, k_ref, v_ref, taps_ref, wide_ref, out_ref, sems, out_sems
 ):
     rows, width = q_hbm.shape
     tiles = width // LANES
     wide = PACK_TILES * LANES
-    groups = LANES // size
     taps_copy = pltpu.make_async_copy(taps_hbm, taps_ref, sems.at[0, 3])
     taps_copy.start()
     parts = []
@@ -57,10 +56,9 @@
         for copy in copies:
             copy.start()
         parts.append(copies)
-    long_copy = pltpu.make_async_copy(long_hbm, long_ref, sems.at[1, 3])
-    long_copy.start()
     taps_copy.wait()
     taps = [lane_taps(taps_ref, which, size, width) for which in (1, 2)]
+    sent = []
     for t in range(tiles):
         if t % PACK_TILES == 0:
             for copy in parts[t // PACK_TILES]:
@@ -79,40 +77,44 @@
                 jnp.concatenate(ends, axis=0).astype(BF16)
             )
         out_ref[t, :LANES, :] = jnp.transpose((features[0] * features[1]).astype(BF16))
-    long_copy.wait()
-    for t in range(tiles):
-        lanes = slice(t * LANES, (t + 1) * LANES)
         middle = q_ref[LANES : LANES + 2 * EDGE, lanes].astype(F32)[:EDGE]
         last = q_ref[rows - 2 * EDGE :, lanes].astype(F32)[EDGE:]
-        here = long_ref[t * groups : (t + 1) * groups, :].astype(F32)
-        lines = jnp.concatenate([jnp.concatenate([middle, last], axis=1), here], axis=0)
-        out_ref[t, LANES + LANES // 2 + 2 * EDGE :, :] = lines.astype(BF16)
-
-
-def call_pack(q_one, k_one, v_one, short_taps, long_taps):
+        out_ref[t, at + 2 * EDGE :, :] = jnp.concatenate([middle, last], axis=1).astype(BF16)
+        if (t + 1) % PACK_TILES == 0:
+            part = t // PACK_TILES
+            done = pl.ds(part * PACK_TILES, PACK_TILES)
+            copy = pltpu.make_async_copy(out_ref.at[done], out_hbm.at[done], out_sems.at[part])
+            copy.start()
+            sent.append(copy)
+    for copy in sent:
+        copy.wait()
+
+
+def call_pack(q_one, k_one, v_one, short_taps):
     rows, width = q_one.shape
     tiles = width // LANES
     size = width // short_taps.shape[2]
-    groups = LANES // size
     assert rows == 2 * LANES
+    out_shape = (tiles, LANES + LANES // 2 + 3 * EDGE, rows)
 
     def kernel(*refs):
         pack_kernel(size, *refs)
 
-    inputs = [in_hbm(array) for array in (q_one, k_one, v_one, short_taps, long_taps)]
+    inputs = [in_hbm(array) for array in (q_one, k_one, v_one, short_taps)]
     return pl.pallas_call(
         kernel,
-        in_specs=[pl.BlockSpec(memory_space=pltpu.HBM)] * 5,
-        out_specs=pl.BlockSpec(memory_space=pltpu.VMEM),
-        out_shape=jax.ShapeDtypeStruct((tiles, LANES + LANES // 2 + 3 * EDGE + groups, rows), BF16),
+        in_specs=[pl.BlockSpec(memory_space=pltpu.HBM)] * 4,
+        out_specs=pl.BlockSpec(memory_space=pltpu.HBM),
+        out_shape=pltpu.HBM(out_shape, BF16),
         scratch_shapes=[
             pltpu.VMEM((rows, width), BF16),
             pltpu.VMEM((rows, width), BF16),
             pltpu.VMEM((rows, width), BF16),
             pltpu.VMEM(short_taps.shape, BF16),
-            pltpu.VMEM(long_taps.shape, BF16),
             pltpu.VMEM((tiles, 2, EDGE + rows, LANES), F32),
+            pltpu.VMEM(out_shape, BF16),
             pltpu.SemaphoreType.DMA((tiles // PACK_TILES, 4)),
+            pltpu.SemaphoreType.DMA((tiles // PACK_TILES,)),
         ],
         compiler_params=params(),
         name="pack",
@@ -189,31 +191,35 @@
     )(q_one, k_one, v_one, k_two, short_taps, base)
 
 
-def join_kernel(full_width, gate_ref, early_ref, energy_ref, out_ref):
+def join_kernel(full_width, gate_ref, early_ref, energy_ref, long_ref, out_ref):
+    tiles = out_ref.shape[0]
+    groups = long_ref.shape[0] // tiles
     scale = lax.rsqrt(energy_ref[...] / full_width + EPSILON)
     lane = lax.broadcasted_iota(jnp.int32, (LANES, LANES), 1)
-    for t in range(out_ref.shape[0]):
+    for t in range(tiles):
         lanes = slice(t * LANES, (t + 1) * LANES)
         turned = jnp.transpose(gate_ref[:, lanes])
         values = jnp.where(lane < EDGE, turned[:, LANES:].astype(F32), early_ref[t] * scale)
-        out_ref[t, :, :LANES] = turned[:, :LANES]
-        out_ref[t, :, LANES:] = values.astype(BF16)
-
-
-def call_join(k_two, early, energy, full_width):
+        out_ref[t, :LANES, :LANES] = turned[:, :LANES]
+        out_ref[t, :LANES, LANES:] = values.astype(BF16)
+        out_ref[t, LANES:, :] = long_ref[t * groups : (t + 1) * groups, :].astype(F32).astype(BF16)
+
+
+def call_join(k_two, early, energy, long_taps, full_width):
     rows, width = k_two.shape
+    tiles = width // LANES
 
     def kernel(*refs):
         join_kernel(full_width, *refs)
 
     return pl.pallas_call(
         kernel,
-        in_specs=[pl.BlockSpec(memory_space=pltpu.VMEM)] * 3,
+        in_specs=[pl.BlockSpec(memory_space=pltpu.VMEM)] * 4,
         out_specs=pl.BlockSpec(memory_space=pltpu.VMEM),
-        out_shape=jax.ShapeDtypeStruct((width // LANES, LANES, rows), BF16),
+        out_shape=jax.ShapeDtypeStruct((tiles, LANES + long_taps.shape[0] // tiles, rows), BF16),
         compiler_params=params(),
         name="join",
-    )(k_two, early, energy)
+    )(k_two, early, energy, long_taps)
 
 
 def mix_kernel(
@@ -451,21 +457,6 @@
     return array
 
 
-def sum_over_all(array):
-    axes = ("ctx", "tp")
-    count = lax.axis_size("ctx") * lax.axis_size("tp")
-    assert count & (count - 1) == 0
-    masks, bit = [1], 2
-    while True:
-        parts = [lax.ppermute(array, axes, [(i, i ^ mask) for i in range(count)]) for mask in masks]
-        for part in parts:
-            array = array + part
-        if bit >= count:
-            return array
-        masks = [bit, 2 * bit, 3 * bit] if 2 * bit < count else [bit]
-        bit *= 4
-
-
 def per_device(
     q_one,
     k_one,
@@ -493,38 +484,41 @@
     slots = jnp.arange(ctx_count, dtype=jnp.int32)
     holder = jnp.sum(jnp.where(block_order[None, :] == slots[:, None], slots[None, :], 0), axis=1)
 
-    packed = call_pack(q_one, k_one, v_one, short_taps, long_taps)
+    packed = call_pack(q_one, k_one, v_one, short_taps)
     span = 2 * EDGE
     if ctx_count != tiles:
         half = LANES // 2
-        sizes = (LANES, half, span, EDGE, tile_groups)
-        z, q, ends, more, taps = jnp.split(packed, [sum(sizes[:n]) for n in range(1, 5)], axis=1)
+        sizes = (LANES, half, span, EDGE)
+        z, q, ends, more = jnp.split(packed, [sum(sizes[:n]) for n in range(1, 4)], axis=1)
         q = jnp.transpose(q.reshape(tiles, half, 2, LANES), (0, 2, 1, 3))
         q = jnp.transpose(q.reshape(ctx_count, 2, shard // 2, LANES), (0, 2, 1, 3))
         ends = jnp.transpose(ends.reshape(tiles, span, 2, -1, shard), (0, 3, 1, 2, 4))
         more = jnp.transpose(more.reshape(tiles, EDGE, 2, -1, shard), (0, 3, 1, 2, 4))
-        parts = [part.reshape(ctx_count, -1, rows) for part in (z, q, ends, more, taps)]
+        parts = [part.reshape(ctx_count, -1, rows) for part in (z, q, ends, more)]
         packed = jnp.concatenate(parts, axis=1)
     moved = exchange(packed)
     ends_at = shard + shard // 2
     more_at = ends_at + span * 2 * shard // rows
-    taps_at = more_at + EDGE * 2 * shard // rows
+    more_to = more_at + EDGE * 2 * shard // rows
     ends = moved[:, ends_at:more_at].reshape(ctx_count, span, 2 * shard)
-    more = moved[:, more_at:taps_at].reshape(ctx_count, EDGE, 2 * shard)
+    more = moved[:, more_at:more_to].reshape(ctx_count, EDGE, 2 * shard)
 
     early, early_energy = call_early(q_one, k_one, v_one, k_two, short_taps, medium_taps)
     early_energy = sum_by_pairs(early_energy, "tp")
-    joined = call_join(k_two, early, early_energy, full_width)
+    joined = call_join(k_two, early, early_energy, long_taps, full_width)
+    if ctx_count != tiles:
+        taps = joined[:, LANES : LANES + tile_groups].reshape(ctx_count, shard_groups, rows)
+        joined = jnp.concatenate([joined[:, :LANES].reshape(ctx_count, shard, rows), taps], axis=1)
     moved, joined = lax.optimization_barrier((moved, joined))
 
     short_local = lax.dynamic_slice_in_dim(short_taps, me * shard_groups, shard_groups, axis=2)
     medium_local = lax.dynamic_slice_in_dim(medium_taps, me * shard_groups, shard_groups, axis=1)
     mixed, energy = call_mix(holder, moved, ends, more, short_local, medium_local, shard, rows)
     energy, joined = lax.optimization_barrier((energy, joined))
-    keys = exchange(joined.reshape(ctx_count, shard, rows))
-    energy = sum_over_all(energy)
-
-    long_rows = moved[:, taps_at : taps_at + shard_groups]
+    keys = exchange(joined)
+    energy = sum_by_pairs(sum_by_pairs(energy, "tp"), "ctx")
+
+    long_rows = keys[:, shard : shard + shard_groups]
     long_rows = jnp.transpose(long_rows, (1, 0, 2)).reshape(shard_groups, ctx_count * rows)
     windows = long_windows(long_rows, rows, min(ctx_count, 8))
     gain = lax.dynamic_slice_in_dim(skip_gain, me * shard, shard).reshape(shard, 1)

time: 76.3 us -> 75.9 us (level)
    ppermute x2 -> x7, waiting for transfers between devices: 1.87 us -> 10.9 us  [sum_by_pairs(): lax.ppermute(array, axis, [(i, i ^ bit) for i in range(count)])]
    ppermute x2 -> x7, starting transfers between devices: 1.59 us -> 10.2 us  [sum_by_pairs(): lax.ppermute(array, axis, [(i, i ^ bit) for i in range(count)])]
    ppermute x7 -> x0, starting transfers between devices: 7.97 us -> none  [sum_over_all(): lax.ppermute(array, axes, [(i, i ^ mask) for i in range(count)])]
    ppermute x7 -> x0, waiting for transfers between devices: 7.97 us -> none  [sum_over_all(): lax.ppermute(array, axes, [(i, i ^ mask) for i in range(count)])]
  transfers between devices with their start and end apart: 11 -> 9, of which waited for: 8 -> 8; matrix products, arithmetic and copies ran while one was open for 2% -> 1% of each run, Pallas kernels for 6% -> 6%
where the time goes in v9:
time: 75.9 us; the launch traced here: 75.5 us
  waiting for transfers between devices  23.4 us (31%)
  starting transfers between devices  21.2 us (28%)
  blocking collectives  16.5 us (22%)
  Pallas kernels  12.7 us (17%)
  local copies, waits for them, and re-layouts  1.26 us (2%)
    all_to_all x1, blocking collectives, exchange(): return lax.all_to_all(array, 'ctx', split_axis=0, concat_axis=0, tiled=True)  16.5 us
    all_to_all x2, waiting for transfers between devices, exchange(): return lax.all_to_all(array, 'ctx', split_axis=0, concat_axis=0, tiled=True)  12.5 us
    all_to_all x2, starting transfers between devices, exchange(): return lax.all_to_all(array, 'ctx', split_axis=0, concat_axis=0, tiled=True)  10.9 us
    ppermute x7, waiting for transfers between devices, sum_by_pairs(): lax.ppermute(array, axis, [(i, i ^ bit) for i in range(count)])  10.9 us
    ppermute x7, starting transfers between devices, sum_by_pairs(): lax.ppermute(array, axis, [(i, i ^ bit) for i in range(count)])  10.2 us
    pallas_call x1, Pallas kernels, call_pack(): pl.pallas_call(kernel, in_specs=[pl.BlockSpec(memory_space=pltpu.HBM)] *...  3.37 us
    pallas_call x1, Pallas kernels, call_early(): pl.pallas_call(kernel, in_specs=[pl.BlockSpec(memory_space=pltpu.VMEM)] *...  3.25 us
    pallas_call x1, Pallas kernels, call_long(): pl.pallas_call(kernel, in_specs=[pl.BlockSpec(memory_space=pltpu.SMEM)] +...  2.44 us
  transfers between devices with their start and end apart: 9, of which 8 were waited for; matrix products, arithmetic and copies ran while one was open for 1% of the time, Pallas kernels for 6%

profile of v9, /device:TPU:0, one launch (start us, length us, event | category | flops | bytes accessed | tf_op | source)
XLA Modules:
  0.0 75.5 jit_solution(433196640722020003)
XLA Ops:
  0.0 0.0 copy-start
  0.0 0.0 copy-start.4
  0.0 3.4 %pack.1 = bf16[8,216,256]{2,1,0:T(8,128)(2,1)} custom-call(bf16[256,1024]{1,0:T(8,128)(2,1)} %refs_0_.4, bf16[256,1024]{1,0:T(8,128)(2,1)} %refs_1_.3, bf16[256,1024]{1,0:T(8,128)(2,1)} %refs_2_.3, bf16[3,7,64]{2,1,0:T(8,128)(2,1)} %refs_4_.1), custom_call_target="tpu_custom_call" | custom-call | tf_op jit(solution)/shard_map/pack/pallas_call | solution.py:104
  3.4 0.0 copy-start.8
  3.4 0.0 copy-start.1
  3.4 0.0 copy-start.2
  3.4 0.0 copy-start.3
  3.4 7.4 %all-to-all-start = ((bf16[8,216,256]{2,1,0:T(8,128)(2,1)}), bf16[8,216,256]{2,1,0:T(8,128)(2,1)S(1)}, u32[]{:S(2)}, u32[]{:S(2)}) async-start(bf16[8,216,256]{2,1,0:T(8,128)(2,1)} %pack.1), calls=%async_computation | async-start | bytes 1769472 | tf_op jit(solution)/shard_map/all_to_all | solution.py:447
  10.8 0.0 copy-done.8
  10.8 0.1 rev.3
  10.9 0.0 copy-start.6
  10.9 0.1 pad_convert_fusion.1.refs_5_
  11.0 0.0 copy-done.4
  11.0 0.0 copy-done.1
  11.0 0.0 copy-done.2
  11.0 0.0 copy-done.3
  11.0 0.6 copy-done.6
  11.6 3.3 %early.1 = (f32[8,128,128]{2,1,0:T(8,128)S(1)}, f32[1,128]{1,0:T(1,128)S(1)}) custom-call(bf16[256,1024]{1,0:T(8,128)(2,1)S(1)} %copy-done.2, bf16[256,1024]{1,0:T(8,128)(2,1)S(1)} %copy-done.3, bf16[256,1024]{1,0:T(8,128)(2,1)S(1)} %copy-done.4, bf16[256,1024]{1,0:T(8,128)(2,1)S(1)} %copy-done.1, bf16[3,7,64]{2,1,0:T(8,128)(2,1)S(1)} %copy-done.6, ...), custom_call_target="tpu_custom_call" | custom-call | tf_op jit(solution)/shard_map/early/pallas_call | solution.py:180
  14.9 0.1 collective-permute-start
  15.0 0.1 dynamic-slice_bitcast_fusion
  15.0 0.1 copy.13
  15.1 0.1 dynamic-slice_convert_fusion
  15.2 0.0 copy-start.9
  15.2 0.8 %collective-permute-done = f32[1,128]{1,0:T(1,128)S(1)} collective-permute-done((f32[1,128]{1,0:T(1,128)S(1)}, f32[1,128]{1,0:T(1,128)S(1)}, u32[]{:S(2)}, u32[]{:S(2)}) %collective-permute-start) | collective-permute-done | bytes 544 | tf_op jit(solution)/shard_map/ppermute | solution.py:455
  16.1 1.5 %collective-permute-start.1 = (f32[1,128]{1,0:T(1,128)S(1)}, f32[1,128]{1,0:T(1,128)S(1)}, u32[]{:S(2)}, u32[]{:S(2)}) collective-permute-start(f32[1,128]{1,0:T(1,128)S(1)} %add.36), channel_id=1, source_target_pairs={{0,2},{1,3},{2,0},{3,1},{4,6},{5,7},{6,4},{7,5},{8,10},{9,11},{10,... | collective-permute-start | bytes 1544 | tf_op jit(solution)/shard_map/ppermute | solution.py:455
  17.6 0.0 copy-done.9
  17.6 0.1 select_reduce_fusion.refs_0_
  17.7 0.1 broadcast_in_dim.20
  17.8 0.0 copy-start.7
  17.8 0.1 convert_element_type.36.refs_4_
  17.9 1.7 %collective-permute-done.1 = f32[1,128]{1,0:T(1,128)S(1)} collective-permute-done((f32[1,128]{1,0:T(1,128)S(1)}, f32[1,128]{1,0:T(1,128)S(1)}, u32[]{:S(2)}, u32[]{:S(2)}) %collective-permute-start.1) | collective-permute-done | bytes 544 | tf_op jit(solution)/shard_map/ppermute | solution.py:455
  19.6 0.0 copy-done.7
  19.6 1.0 %join.1 = bf16[8,136,256]{2,1,0:T(8,128)(2,1)} custom-call(bf16[256,1024]{1,0:T(8,128)(2,1)S(1)} %copy-done.1, f32[8,128,128]{2,1,0:T(8,128)S(1)} %get-tuple-element.13.refs_1_, f32[1,128]{1,0:T(1,128)S(1)} %add.37.refs_2_, bf16[64,256]{1,0:T(8,128)(2,1)S(1)} %copy-done.7), custom_call_target="tpu_custom_call" | custom-call | tf_op jit(solution)/shard_map/join/pallas_call | solution.py:215
  20.6 12.5 %all-to-all-done.refs_1_ = bf16[8,216,256]{2,1,0:T(8,128)(2,1)S(1)} async-done(((bf16[8,216,256]{2,1,0:T(8,128)(2,1)}), bf16[8,216,256]{2,1,0:T(8,128)(2,1)S(1)}, u32[]{:S(2)}, u32[]{:S(2)}) %all-to-all-start) | async-done | bytes 884768 | tf_op jit(solution)/shard_map/all_to_all | solution.py:447
  33.2 1.6 %mix.1 = (f32[8,128,256]{2,1,0:T(8,128)S(1)}, f32[16,128]{1,0:T(8,128)S(1)}) custom-call(s32[8]{0:T(128)S(1)} %select_reduce_fusion.refs_0_, bf16[8,216,256]{2,1,0:T(8,128)(2,1)S(1)} %all-to-all-done.refs_1_, bf16[8,16,256]{2,1,0:T(8,128)(2,1)S(1)} %slice.16.refs_2_, bf16[8,8,256]{2,1,0:T(8,128)(2,1)S(1)} %slice.17.refs_3_, ...), custom_call_target="tpu_custom_call" | custom-call | tf_op jit(solution)/shard_map/mix/pallas_call | solution.py:328
  34.8 3.5 %all-to-all-start.1 = ((bf16[8,136,256]{2,1,0:T(8,128)(2,1)}), bf16[8,136,256]{2,1,0:T(8,128)(2,1)S(1)}, u32[]{:S(2)}, u32[]{:S(2)}) async-start(bf16[8,136,256]{2,1,0:T(8,128)(2,1)} %join.1), calls=%async_computation.1 | async-start | bytes 1114112 | tf_op jit(solution)/shard_map/all_to_all | solution.py:447
  38.4 0.1 collective-permute-start.2
  38.5 1.2 %collective-permute-done.2 = f32[16,128]{1,0:T(8,128)S(1)} collective-permute-done((f32[16,128]{1,0:T(8,128)S(1)}, f32[16,128]{1,0:T(8,128)S(1)}, u32[]{:S(2)}, u32[]{:S(2)}) %collective-permute-start.2) | collective-permute-done | bytes 8224 | tf_op jit(solution)/shard_map/ppermute | solution.py:455
  39.6 1.5 %collective-permute-start.3 = (f32[16,128]{1,0:T(8,128)S(1)}, f32[16,128]{1,0:T(8,128)S(1)}, u32[]{:S(2)}, u32[]{:S(2)}) collective-permute-start(f32[16,128]{1,0:T(8,128)S(1)} %add.39), channel_id=1, source_target_pairs={{0,2},{1,3},{2,0},{3,1},{4,6},{5,7},{6,4},{7,5},{8,10},{9,11},{10,... | collective-permute-start | bytes 24584 | tf_op jit(solution)/shard_map/ppermute | solution.py:455
  41.2 2.1 %collective-permute-done.3 = f32[16,128]{1,0:T(8,128)S(1)} collective-permute-done((f32[16,128]{1,0:T(8,128)S(1)}, f32[16,128]{1,0:T(8,128)S(1)}, u32[]{:S(2)}, u32[]{:S(2)}) %collective-permute-start.3) | collective-permute-done | bytes 8224 | tf_op jit(solution)/shard_map/ppermute | solution.py:455
  43.3 1.9 %collective-permute-start.4 = (f32[16,128]{1,0:T(8,128)S(1)}, f32[16,128]{1,0:T(8,128)S(1)}, u32[]{:S(2)}, u32[]{:S(2)}) collective-permute-start(f32[16,128]{1,0:T(8,128)S(1)} %add.40), channel_id=1, source_target_pairs={{0,4},{4,0},{8,12},{12,8},{16,20},{20,16},{24,28},{28,24},{1,5},{5... | collective-permute-start | bytes 24584 | tf_op jit(solution)/shard_map/ppermute | solution.py:455
  45.2 1.8 %collective-permute-done.4 = f32[16,128]{1,0:T(8,128)S(1)} collective-permute-done((f32[16,128]{1,0:T(8,128)S(1)}, f32[16,128]{1,0:T(8,128)S(1)}, u32[]{:S(2)}, u32[]{:S(2)}) %collective-permute-start.4) | collective-permute-done | bytes 8224 | tf_op jit(solution)/shard_map/ppermute | solution.py:455
  47.0 1.9 %collective-permute-start.5 = (f32[16,128]{1,0:T(8,128)S(1)}, f32[16,128]{1,0:T(8,128)S(1)}, u32[]{:S(2)}, u32[]{:S(2)}) collective-permute-start(f32[16,128]{1,0:T(8,128)S(1)} %add.41), channel_id=1, source_target_pairs={{0,8},{4,12},{8,0},{12,4},{16,24},{20,28},{24,16},{28,20},{1,9},{5... | collective-permute-start | bytes 24584 | tf_op jit(solution)/shard_map/ppermute | solution.py:455
  48.9 1.8 %collective-permute-done.5 = f32[16,128]{1,0:T(8,128)S(1)} collective-permute-done((f32[16,128]{1,0:T(8,128)S(1)}, f32[16,128]{1,0:T(8,128)S(1)}, u32[]{:S(2)}, u32[]{:S(2)}) %collective-permute-start.5) | collective-permute-done | bytes 8224 | tf_op jit(solution)/shard_map/ppermute | solution.py:455
  50.7 3.3 %collective-permute-start.6 = (f32[16,128]{1,0:T(8,128)S(1)}, f32[16,128]{1,0:T(8,128)S(1)}, u32[]{:S(2)}, u32[]{:S(2)}) collective-permute-start(f32[16,128]{1,0:T(8,128)S(1)} %add.42), channel_id=1, source_target_pairs={{0,16},{4,20},{8,24},{12,28},{16,0},{20,4},{24,8},{28,12},{1,17},{... | collective-permute-start | bytes 24584 | tf_op jit(solution)/shard_map/ppermute | solution.py:455
  54.0 0.0 copy-done
  54.0 0.1 dynamic-slice_bitcast_fusion.2
  54.1 0.1 copy.14.refs_5_
  54.2 1.4 %collective-permute-done.6 = f32[16,128]{1,0:T(8,128)S(1)} collective-permute-done((f32[16,128]{1,0:T(8,128)S(1)}, f32[16,128]{1,0:T(8,128)S(1)}, u32[]{:S(2)}, u32[]{:S(2)}) %collective-permute-start.6) | collective-permute-done | bytes 8224 | tf_op jit(solution)/shard_map/ppermute | solution.py:455
  55.6 0.0 all-to-all-done.1.refs_2_
  55.6 2.4 %long.1 = bf16[8,128,256]{2,1,0:T(8,128)(2,1)S(1)} custom-call(s32[8]{0:T(128)S(1)} %select_reduce_fusion.refs_0_, f32[8,128,256]{2,1,0:T(8,128)S(1)} %get-tuple-element.16.refs_1_, bf16[8,136,256]{2,1,0:T(8,128)(2,1)S(1)} %all-to-all-done.1.refs_2_, f32[16,128]{1,0:T(8,128)S(1)} %add.43.refs_3_, f32[8,2304]{1,0:T(8,128)S(1)} %pad_convert_fusion.refs_4_, ...), custom_call_target="tpu_custom_call" | custom-call | tf_op jit(solution)/shard_map/long/pallas_call | solution.py:402
  58.1 0.0 copy-start.5
  58.1 16.5 %all_to_all.15.mixed_ref = bf16[8,128,256]{2,1,0:T(8,128)(2,1)S(1)} all-to-all(bf16[8,128,256]{2,1,0:T(8,128)(2,1)S(1)} %long.1), channel_id=1, replica_groups=mesh['ctx'=8,'tp'=4] {'ctx'}, dimensions={0} | all-to-all | bytes 1048576 | tf_op jit(solution)/shard_map/all_to_all | solution.py:447
  74.6 0.0 copy-done.5
  74.6 0.9 %gate.1 = bf16[256,1024]{1,0:T(8,128)(2,1)} custom-call(bf16[8,128,256]{2,1,0:T(8,128)(2,1)S(1)} %all_to_all.15.mixed_ref, bf16[256,1024]{1,0:T(8,128)(2,1)S(1)} %copy-done.5), custom_call_target="tpu_custom_call" | custom-call | tf_op jit(solution)/shard_map/gate/pallas_call | solution.py:432
  (13 shorter events, 0.0 us)
Async XLA Ops:
  0.0 54.0 %copy-start = (f32[1024]{0:T(1024)S(1)}, f32[1024]{0:T(1024)}, u32[]{:S(2)}) copy-start(f32[1024]{0:T(1024)} %param.19) | copy-start | bytes 12292
  0.0 11.0 %copy-start.4 = (bf16[256,1024]{1,0:T(8,128)(2,1)S(1)}, bf16[256,1024]{1,0:T(8,128)(2,1)}, u32[]{:S(2)}) copy-start(bf16[256,1024]{1,0:T(8,128)(2,1)} %refs_2_.3) | copy-start | bytes 1572868
  3.4 7.4 %copy-start.8 = (bf16[128,64]{0,1:T(8,128)(2,1)S(1)}, bf16[128,64]{0,1:T(8,128)(2,1)}, u32[]{:S(2)}) copy-start(bf16[128,64]{0,1:T(8,128)(2,1)} %param.17) | copy-start | bytes 49156
  3.4 7.6 %copy-start.1 = (bf16[256,1024]{1,0:T(8,128)(2,1)S(1)}, bf16[256,1024]{1,0:T(8,128)(2,1)}, u32[]{:S(2)}) copy-start(bf16[256,1024]{1,0:T(8,128)(2,1)} %refs_0_.5) | copy-start | bytes 1572868
  3.4 7.6 %copy-start.2 = (bf16[256,1024]{1,0:T(8,128)(2,1)S(1)}, bf16[256,1024]{1,0:T(8,128)(2,1)}, u32[]{:S(2)}) copy-start(bf16[256,1024]{1,0:T(8,128)(2,1)} %refs_0_.4) | copy-start | bytes 1572868
  3.4 7.6 %copy-start.3 = (bf16[256,1024]{1,0:T(8,128)(2,1)S(1)}, bf16[256,1024]{1,0:T(8,128)(2,1)}, u32[]{:S(2)}) copy-start(bf16[256,1024]{1,0:T(8,128)(2,1)} %refs_1_.3) | copy-start | bytes 1572868
  3.4 29.7 %all-to-all-start = ((bf16[8,216,256]{2,1,0:T(8,128)(2,1)}), bf16[8,216,256]{2,1,0:T(8,128)(2,1)S(1)}, u32[]{:S(2)}, u32[]{:S(2)}) async-start(bf16[8,216,256]{2,1,0:T(8,128)(2,1)} %pack.1), calls=%async_computation | async-start | bytes 1769472 | tf_op jit(solution)/shard_map/all_to_all | solution.py:447
  10.9 0.7 copy-start.6
  14.9 1.2 %collective-permute-start = (f32[1,128]{1,0:T(1,128)S(1)}, f32[1,128]{1,0:T(1,128)S(1)}, u32[]{:S(2)}, u32[]{:S(2)}) collective-permute-start(f32[1,128]{1,0:T(1,128)S(1)} %get-tuple-element.14), channel_id=1, source_target_pairs={{0,1},{1,0},{2,3},{3,2},{4,5},{5,4},{6,7},{7,6},{8,9},{9,8},{10,11... | collective-permute-start | bytes 1544 | tf_op jit(solution)/shard_map/ppermute | solution.py:455
  15.2 2.4 %copy-start.9 = (s32[8]{0:T(128)S(1)}, s32[8]{0:T(128)}, u32[]{:S(2)}) copy-start(s32[8]{0:T(128)} %param.20) | copy-start | bytes 100
  16.1 3.5 %collective-permute-start.1 = (f32[1,128]{1,0:T(1,128)S(1)}, f32[1,128]{1,0:T(1,128)S(1)}, u32[]{:S(2)}, u32[]{:S(2)}) collective-permute-start(f32[1,128]{1,0:T(1,128)S(1)} %add.36), channel_id=1, source_target_pairs={{0,2},{1,3},{2,0},{3,1},{4,6},{5,7},{6,4},{7,5},{8,10},{9,11},{10,... | collective-permute-start | bytes 1544 | tf_op jit(solution)/shard_map/ppermute | solution.py:455
  17.8 1.8 %copy-start.7 = (bf16[64,256]{1,0:T(8,128)(2,1)S(1)}, bf16[64,256]{1,0:T(8,128)(2,1)}, u32[]{:S(2)}) copy-start(bf16[64,256]{1,0:T(8,128)(2,1)} %refs_3_.5) | copy-start | bytes 98308
  34.8 20.8 %all-to-all-start.1 = ((bf16[8,136,256]{2,1,0:T(8,128)(2,1)}), bf16[8,136,256]{2,1,0:T(8,128)(2,1)S(1)}, u32[]{:S(2)}, u32[]{:S(2)}) async-start(bf16[8,136,256]{2,1,0:T(8,128)(2,1)} %join.1), calls=%async_computation.1 | async-start | bytes 1114112 | tf_op jit(solution)/shard_map/all_to_all | solution.py:447
  38.4 1.2 %collective-permute-start.2 = (f32[16,128]{1,0:T(8,128)S(1)}, f32[16,128]{1,0:T(8,128)S(1)}, u32[]{:S(2)}, u32[]{:S(2)}) collective-permute-start(f32[16,128]{1,0:T(8,128)S(1)} %get-tuple-element.20), channel_id=1, source_target_pairs={{0,1},{1,0},{2,3},{3,2},{4,5},{5,4},{6,7},{7,6},{8,9},{9,8},{10,11... | collective-permute-start | bytes 24584 | tf_op jit(solution)/shard_map/ppermute | solution.py:455
  39.6 3.7 %collective-permute-start.3 = (f32[16,128]{1,0:T(8,128)S(1)}, f32[16,128]{1,0:T(8,128)S(1)}, u32[]{:S(2)}, u32[]{:S(2)}) collective-permute-start(f32[16,128]{1,0:T(8,128)S(1)} %add.39), channel_id=1, source_target_pairs={{0,2},{1,3},{2,0},{3,1},{4,6},{5,7},{6,4},{7,5},{8,10},{9,11},{10,... | collective-permute-start | bytes 24584 | tf_op jit(solution)/shard_map/ppermute | solution.py:455
  43.3 3.7 %collective-permute-start.4 = (f32[16,128]{1,0:T(8,128)S(1)}, f32[16,128]{1,0:T(8,128)S(1)}, u32[]{:S(2)}, u32[]{:S(2)}) collective-permute-start(f32[16,128]{1,0:T(8,128)S(1)} %add.40), channel_id=1, source_target_pairs={{0,4},{4,0},{8,12},{12,8},{16,20},{20,16},{24,28},{28,24},{1,5},{5... | collective-permute-start | bytes 24584 | tf_op jit(solution)/shard_map/ppermute | solution.py:455
  47.0 3.7 %collective-permute-start.5 = (f32[16,128]{1,0:T(8,128)S(1)}, f32[16,128]{1,0:T(8,128)S(1)}, u32[]{:S(2)}, u32[]{:S(2)}) collective-permute-start(f32[16,128]{1,0:T(8,128)S(1)} %add.41), channel_id=1, source_target_pairs={{0,8},{4,12},{8,0},{12,4},{16,24},{20,28},{24,16},{28,20},{1,9},{5... | collective-permute-start | bytes 24584 | tf_op jit(solution)/shard_map/ppermute | solution.py:455
  50.7 4.9 %collective-permute-start.6 = (f32[16,128]{1,0:T(8,128)S(1)}, f32[16,128]{1,0:T(8,128)S(1)}, u32[]{:S(2)}, u32[]{:S(2)}) collective-permute-start(f32[16,128]{1,0:T(8,128)S(1)} %add.42), channel_id=1, source_target_pairs={{0,16},{4,20},{8,24},{12,28},{16,0},{20,4},{24,8},{28,12},{1,17},{... | collective-permute-start | bytes 24584 | tf_op jit(solution)/shard_map/ppermute | solution.py:455
  58.1 16.5 %copy-start.5 = (bf16[256,1024]{1,0:T(8,128)(2,1)S(1)}, bf16[256,1024]{1,0:T(8,128)(2,1)}, u32[]{:S(2)}) copy-start(bf16[256,1024]{1,0:T(8,128)(2,1)} %gate_ref.1) | copy-start | bytes 1572868

commit v10 on v9

--- a/solution.py
+++ b/solution.py
@@ -371,24 +371,27 @@
         here = slice(g * size, (g + 1) * size)
         ordered_ref[g, :reach] = jnp.zeros((reach, rows), BF16)
         total = ordered_ref[g, reach:].astype(F32) * jnp.concatenate([gain_ref[here]] * blocks, axis=0)
-        for p in range(pieces):
-            slot = g * pieces + p
+        for slot_lag in range(0, blocks, lags // 2):
+            slot = g * pieces + slot_lag // lags
+            first = slot_lag * size
             left = jnp.concatenate(
                 [
-                    ordered_ref[g, (blocks - lag) * size : (2 * blocks - lag) * size]
-                    for lag in range(p * lags, (p + 1) * lags)
+                    ordered_ref[g, reach + first - lag * size : 2 * reach - lag * size]
+                    for lag in range(slot_lag, slot_lag + lags // 2)
                 ],
                 axis=1,
             )
+            at = slot_lag % lags
             right = jnp.concatenate(
                 [
                     strip_ref[slot, :, shift - half : shift - half + rows]
-                    for lag in range(1, lags + 1)
+                    for lag in range(at + 1, at + lags // 2 + 1)
                     for shift in (lag * rows, lag * rows - half)
                 ],
                 axis=0,
             )
-            total = total + jnp.dot(left, right, preferred_element_type=F32)
+            added = total[first:] + jnp.dot(left, right, preferred_element_type=F32)
+            total = jnp.concatenate([total[:first], added], axis=0) if first else added
         for b, holder in enumerate(holders):
             out_ref[holder, here] = total[b * size : (b + 1) * size].astype(BF16)
 
@@ -405,7 +408,10 @@
         + [pl.BlockSpec(memory_space=pltpu.VMEM)] * 5,
         out_specs=pl.BlockSpec(memory_space=pltpu.VMEM),
         out_shape=jax.ShapeDtypeStruct((blocks, shard, rows), BF16),
-        scratch_shapes=[pltpu.VMEM((shard // size, 2 * blocks * size, rows), BF16), pltpu.VMEM((windows.shape[0], rows // 2, windows.shape[1] - rows // 2), BF16)],
+        scratch_shapes=[
+            pltpu.VMEM((shard // size, 2 * blocks * size, rows), BF16),
+            pltpu.VMEM((windows.shape[0], rows // 2, windows.shape[1] - rows // 2), BF16),
+        ],
         compiler_params=params(),
         name="long",
     )(holder, mixed, keys, energy, windows, gain)

time: 75.9 us -> 75.8 us (level)
  no operation moved by 1% of the time
where the time goes in v10:
time: 75.8 us; the launch traced here: 75.5 us
  waiting for transfers between devices  23.4 us (31%)
  starting transfers between devices  21.2 us (28%)
  blocking collectives  16.5 us (22%)
  Pallas kernels  12.6 us (17%)
  local copies, waits for them, and re-layouts  1.26 us (2%)
    all_to_all x1, blocking collectives, exchange(): return lax.all_to_all(array, 'ctx', split_axis=0, concat_axis=0, tiled=True)  16.5 us
    all_to_all x2, waiting for transfers between devices, exchange(): return lax.all_to_all(array, 'ctx', split_axis=0, concat_axis=0, tiled=True)  12.5 us
    all_to_all x2, starting transfers between devices, exchange(): return lax.all_to_all(array, 'ctx', split_axis=0, concat_axis=0, tiled=True)  10.9 us
    ppermute x7, waiting for transfers between devices, sum_by_pairs(): lax.ppermute(array, axis, [(i, i ^ bit) for i in range(count)])  10.9 us
    ppermute x7, starting transfers between devices, sum_by_pairs(): lax.ppermute(array, axis, [(i, i ^ bit) for i in range(count)])  10.2 us
    pallas_call x1, Pallas kernels, call_pack(): pl.pallas_call(kernel, in_specs=[pl.BlockSpec(memory_space=pltpu.HBM)] *...  3.37 us
    pallas_call x1, Pallas kernels, call_early(): pl.pallas_call(kernel, in_specs=[pl.BlockSpec(memory_space=pltpu.VMEM)] *...  3.25 us
    pallas_call x1, Pallas kernels, call_long(): pl.pallas_call(kernel, in_specs=[pl.BlockSpec(memory_space=pltpu.SMEM)] +...  2.38 us
  transfers between devices with their start and end apart: 9, of which 8 were waited for; matrix products, arithmetic and copies ran while one was open for 1% of the time, Pallas kernels for 6%

profile of v10, /device:TPU:0, one launch (start us, length us, event | category | flops | bytes accessed | tf_op | source)
XLA Modules:
  0.0 75.5 jit_solution(14133669293380058532)
XLA Ops:
  0.0 0.0 copy-start
  0.0 0.0 copy-start.4
  0.0 3.4 %pack.1 = bf16[8,216,256]{2,1,0:T(8,128)(2,1)} custom-call(bf16[256,1024]{1,0:T(8,128)(2,1)} %refs_0_.4, bf16[256,1024]{1,0:T(8,128)(2,1)} %refs_1_.3, bf16[256,1024]{1,0:T(8,128)(2,1)} %refs_2_.3, bf16[3,7,64]{2,1,0:T(8,128)(2,1)} %refs_4_.1), custom_call_target="tpu_custom_call" | custom-call | tf_op jit(solution)/shard_map/pack/pallas_call | solution.py:104
  3.4 0.0 copy-start.8
  3.4 0.0 copy-start.1
  3.4 0.0 copy-start.2
  3.4 0.0 copy-start.3
  3.4 7.4 %all-to-all-start = ((bf16[8,216,256]{2,1,0:T(8,128)(2,1)}), bf16[8,216,256]{2,1,0:T(8,128)(2,1)S(1)}, u32[]{:S(2)}, u32[]{:S(2)}) async-start(bf16[8,216,256]{2,1,0:T(8,128)(2,1)} %pack.1), calls=%async_computation | async-start | bytes 1769472 | tf_op jit(solution)/shard_map/all_to_all | solution.py:453
  10.8 0.0 copy-done.8
  10.8 0.1 rev.3
  10.9 0.0 copy-start.6
  10.9 0.1 pad_convert_fusion.1.refs_5_
  11.0 0.0 copy-done.4
  11.0 0.0 copy-done.1
  11.0 0.0 copy-done.2
  11.0 0.0 copy-done.3
  11.0 0.6 copy-done.6
  11.6 3.3 %early.1 = (f32[8,128,128]{2,1,0:T(8,128)S(1)}, f32[1,128]{1,0:T(1,128)S(1)}) custom-call(bf16[256,1024]{1,0:T(8,128)(2,1)S(1)} %copy-done.2, bf16[256,1024]{1,0:T(8,128)(2,1)S(1)} %copy-done.3, bf16[256,1024]{1,0:T(8,128)(2,1)S(1)} %copy-done.4, bf16[256,1024]{1,0:T(8,128)(2,1)S(1)} %copy-done.1, bf16[3,7,64]{2,1,0:T(8,128)(2,1)S(1)} %copy-done.6, ...), custom_call_target="tpu_custom_call" | custom-call | tf_op jit(solution)/shard_map/early/pallas_call | solution.py:180
  14.9 0.1 collective-permute-start
  15.0 0.1 dynamic-slice_bitcast_fusion
  15.0 0.1 copy.13
  15.1 0.1 dynamic-slice_convert_fusion
  15.2 0.0 copy-start.9
  15.2 0.8 %collective-permute-done = f32[1,128]{1,0:T(1,128)S(1)} collective-permute-done((f32[1,128]{1,0:T(1,128)S(1)}, f32[1,128]{1,0:T(1,128)S(1)}, u32[]{:S(2)}, u32[]{:S(2)}) %collective-permute-start) | collective-permute-done | bytes 544 | tf_op jit(solution)/shard_map/ppermute | solution.py:461
  16.1 1.5 %collective-permute-start.1 = (f32[1,128]{1,0:T(1,128)S(1)}, f32[1,128]{1,0:T(1,128)S(1)}, u32[]{:S(2)}, u32[]{:S(2)}) collective-permute-start(f32[1,128]{1,0:T(1,128)S(1)} %add.36), channel_id=1, source_target_pairs={{0,2},{1,3},{2,0},{3,1},{4,6},{5,7},{6,4},{7,5},{8,10},{9,11},{10,... | collective-permute-start | bytes 1544 | tf_op jit(solution)/shard_map/ppermute | solution.py:461
  17.6 0.0 copy-done.9
  17.6 0.1 select_reduce_fusion.refs_0_
  17.7 0.1 broadcast_in_dim.20
  17.8 0.0 copy-start.7
  17.8 0.1 convert_element_type.36.refs_4_
  17.9 1.7 %collective-permute-done.1 = f32[1,128]{1,0:T(1,128)S(1)} collective-permute-done((f32[1,128]{1,0:T(1,128)S(1)}, f32[1,128]{1,0:T(1,128)S(1)}, u32[]{:S(2)}, u32[]{:S(2)}) %collective-permute-start.1) | collective-permute-done | bytes 544 | tf_op jit(solution)/shard_map/ppermute | solution.py:461
  19.6 0.0 copy-done.7
  19.6 1.0 %join.1 = bf16[8,136,256]{2,1,0:T(8,128)(2,1)} custom-call(bf16[256,1024]{1,0:T(8,128)(2,1)S(1)} %copy-done.1, f32[8,128,128]{2,1,0:T(8,128)S(1)} %get-tuple-element.13.refs_1_, f32[1,128]{1,0:T(1,128)S(1)} %add.37.refs_2_, bf16[64,256]{1,0:T(8,128)(2,1)S(1)} %copy-done.7), custom_call_target="tpu_custom_call" | custom-call | tf_op jit(solution)/shard_map/join/pallas_call | solution.py:215
  20.6 12.5 %all-to-all-done.refs_1_ = bf16[8,216,256]{2,1,0:T(8,128)(2,1)S(1)} async-done(((bf16[8,216,256]{2,1,0:T(8,128)(2,1)}), bf16[8,216,256]{2,1,0:T(8,128)(2,1)S(1)}, u32[]{:S(2)}, u32[]{:S(2)}) %all-to-all-start) | async-done | bytes 884768 | tf_op jit(solution)/shard_map/all_to_all | solution.py:453
  33.2 1.6 %mix.1 = (f32[8,128,256]{2,1,0:T(8,128)S(1)}, f32[16,128]{1,0:T(8,128)S(1)}) custom-call(s32[8]{0:T(128)S(1)} %select_reduce_fusion.refs_0_, bf16[8,216,256]{2,1,0:T(8,128)(2,1)S(1)} %all-to-all-done.refs_1_, bf16[8,16,256]{2,1,0:T(8,128)(2,1)S(1)} %slice.16.refs_2_, bf16[8,8,256]{2,1,0:T(8,128)(2,1)S(1)} %slice.17.refs_3_, ...), custom_call_target="tpu_custom_call" | custom-call | tf_op jit(solution)/shard_map/mix/pallas_call | solution.py:328
  34.8 3.5 %all-to-all-start.1 = ((bf16[8,136,256]{2,1,0:T(8,128)(2,1)}), bf16[8,136,256]{2,1,0:T(8,128)(2,1)S(1)}, u32[]{:S(2)}, u32[]{:S(2)}) async-start(bf16[8,136,256]{2,1,0:T(8,128)(2,1)} %join.1), calls=%async_computation.1 | async-start | bytes 1114112 | tf_op jit(solution)/shard_map/all_to_all | solution.py:453
  38.4 0.1 collective-permute-start.2
  38.5 1.2 %collective-permute-done.2 = f32[16,128]{1,0:T(8,128)S(1)} collective-permute-done((f32[16,128]{1,0:T(8,128)S(1)}, f32[16,128]{1,0:T(8,128)S(1)}, u32[]{:S(2)}, u32[]{:S(2)}) %collective-permute-start.2) | collective-permute-done | bytes 8224 | tf_op jit(solution)/shard_map/ppermute | solution.py:461
  39.6 1.5 %collective-permute-start.3 = (f32[16,128]{1,0:T(8,128)S(1)}, f32[16,128]{1,0:T(8,128)S(1)}, u32[]{:S(2)}, u32[]{:S(2)}) collective-permute-start(f32[16,128]{1,0:T(8,128)S(1)} %add.39), channel_id=1, source_target_pairs={{0,2},{1,3},{2,0},{3,1},{4,6},{5,7},{6,4},{7,5},{8,10},{9,11},{10,... | collective-permute-start | bytes 24584 | tf_op jit(solution)/shard_map/ppermute | solution.py:461
  41.2 2.1 %collective-permute-done.3 = f32[16,128]{1,0:T(8,128)S(1)} collective-permute-done((f32[16,128]{1,0:T(8,128)S(1)}, f32[16,128]{1,0:T(8,128)S(1)}, u32[]{:S(2)}, u32[]{:S(2)}) %collective-permute-start.3) | collective-permute-done | bytes 8224 | tf_op jit(solution)/shard_map/ppermute | solution.py:461
  43.3 1.9 %collective-permute-start.4 = (f32[16,128]{1,0:T(8,128)S(1)}, f32[16,128]{1,0:T(8,128)S(1)}, u32[]{:S(2)}, u32[]{:S(2)}) collective-permute-start(f32[16,128]{1,0:T(8,128)S(1)} %add.40), channel_id=1, source_target_pairs={{0,4},{4,0},{8,12},{12,8},{16,20},{20,16},{24,28},{28,24},{1,5},{5... | collective-permute-start | bytes 24584 | tf_op jit(solution)/shard_map/ppermute | solution.py:461
  45.2 1.8 %collective-permute-done.4 = f32[16,128]{1,0:T(8,128)S(1)} collective-permute-done((f32[16,128]{1,0:T(8,128)S(1)}, f32[16,128]{1,0:T(8,128)S(1)}, u32[]{:S(2)}, u32[]{:S(2)}) %collective-permute-start.4) | collective-permute-done | bytes 8224 | tf_op jit(solution)/shard_map/ppermute | solution.py:461
  47.0 1.9 %collective-permute-start.5 = (f32[16,128]{1,0:T(8,128)S(1)}, f32[16,128]{1,0:T(8,128)S(1)}, u32[]{:S(2)}, u32[]{:S(2)}) collective-permute-start(f32[16,128]{1,0:T(8,128)S(1)} %add.41), channel_id=1, source_target_pairs={{0,8},{4,12},{8,0},{12,4},{16,24},{20,28},{24,16},{28,20},{1,9},{5... | collective-permute-start | bytes 24584 | tf_op jit(solution)/shard_map/ppermute | solution.py:461
  48.9 1.8 %collective-permute-done.5 = f32[16,128]{1,0:T(8,128)S(1)} collective-permute-done((f32[16,128]{1,0:T(8,128)S(1)}, f32[16,128]{1,0:T(8,128)S(1)}, u32[]{:S(2)}, u32[]{:S(2)}) %collective-permute-start.5) | collective-permute-done | bytes 8224 | tf_op jit(solution)/shard_map/ppermute | solution.py:461
  50.7 3.3 %collective-permute-start.6 = (f32[16,128]{1,0:T(8,128)S(1)}, f32[16,128]{1,0:T(8,128)S(1)}, u32[]{:S(2)}, u32[]{:S(2)}) collective-permute-start(f32[16,128]{1,0:T(8,128)S(1)} %add.42), channel_id=1, source_target_pairs={{0,16},{4,20},{8,24},{12,28},{16,0},{20,4},{24,8},{28,12},{1,17},{... | collective-permute-start | bytes 24584 | tf_op jit(solution)/shard_map/ppermute | solution.py:461
  54.0 0.0 copy-done
  54.0 0.1 dynamic-slice_bitcast_fusion.2
  54.1 0.1 copy.14.refs_5_
  54.2 1.4 %collective-permute-done.6 = f32[16,128]{1,0:T(8,128)S(1)} collective-permute-done((f32[16,128]{1,0:T(8,128)S(1)}, f32[16,128]{1,0:T(8,128)S(1)}, u32[]{:S(2)}, u32[]{:S(2)}) %collective-permute-start.6) | collective-permute-done | bytes 8224 | tf_op jit(solution)/shard_map/ppermute | solution.py:461
  55.6 0.0 all-to-all-done.1.refs_2_
  55.6 2.4 %long.1 = bf16[8,128,256]{2,1,0:T(8,128)(2,1)S(1)} custom-call(s32[8]{0:T(128)S(1)} %select_reduce_fusion.refs_0_, f32[8,128,256]{2,1,0:T(8,128)S(1)} %get-tuple-element.16.refs_1_, bf16[8,136,256]{2,1,0:T(8,128)(2,1)S(1)} %all-to-all-done.1.refs_2_, f32[16,128]{1,0:T(8,128)S(1)} %add.43.refs_3_, f32[8,2304]{1,0:T(8,128)S(1)} %pad_convert_fusion.refs_4_, ...), custom_call_target="tpu_custom_call" | custom-call | tf_op jit(solution)/shard_map/long/pallas_call | solution.py:405
  58.0 0.0 copy-start.5
  58.0 16.5 %all_to_all.15.mixed_ref = bf16[8,128,256]{2,1,0:T(8,128)(2,1)S(1)} all-to-all(bf16[8,128,256]{2,1,0:T(8,128)(2,1)S(1)} %long.1), channel_id=1, replica_groups=mesh['ctx'=8,'tp'=4] {'ctx'}, dimensions={0} | all-to-all | bytes 1048576 | tf_op jit(solution)/shard_map/all_to_all | solution.py:453
  74.5 0.0 copy-done.5
  74.5 0.9 %gate.1 = bf16[256,1024]{1,0:T(8,128)(2,1)} custom-call(bf16[8,128,256]{2,1,0:T(8,128)(2,1)S(1)} %all_to_all.15.mixed_ref, bf16[256,1024]{1,0:T(8,128)(2,1)S(1)} %copy-done.5), custom_call_target="tpu_custom_call" | custom-call | tf_op jit(solution)/shard_map/gate/pallas_call | solution.py:438
  (13 shorter events, 0.1 us)
Async XLA Ops:
  0.0 54.0 %copy-start = (f32[1024]{0:T(1024)S(1)}, f32[1024]{0:T(1024)}, u32[]{:S(2)}) copy-start(f32[1024]{0:T(1024)} %param.19) | copy-start | bytes 12292
  0.0 11.0 %copy-start.4 = (bf16[256,1024]{1,0:T(8,128)(2,1)S(1)}, bf16[256,1024]{1,0:T(8,128)(2,1)}, u32[]{:S(2)}) copy-start(bf16[256,1024]{1,0:T(8,128)(2,1)} %refs_2_.3) | copy-start | bytes 1572868
  3.4 7.4 %copy-start.8 = (bf16[128,64]{0,1:T(8,128)(2,1)S(1)}, bf16[128,64]{0,1:T(8,128)(2,1)}, u32[]{:S(2)}) copy-start(bf16[128,64]{0,1:T(8,128)(2,1)} %param.17) | copy-start | bytes 49156
  3.4 7.6 %copy-start.1 = (bf16[256,1024]{1,0:T(8,128)(2,1)S(1)}, bf16[256,1024]{1,0:T(8,128)(2,1)}, u32[]{:S(2)}) copy-start(bf16[256,1024]{1,0:T(8,128)(2,1)} %refs_0_.5) | copy-start | bytes 1572868
  3.4 7.6 %copy-start.2 = (bf16[256,1024]{1,0:T(8,128)(2,1)S(1)}, bf16[256,1024]{1,0:T(8,128)(2,1)}, u32[]{:S(2)}) copy-start(bf16[256,1024]{1,0:T(8,128)(2,1)} %refs_0_.4) | copy-start | bytes 1572868
  3.4 7.6 %copy-start.3 = (bf16[256,1024]{1,0:T(8,128)(2,1)S(1)}, bf16[256,1024]{1,0:T(8,128)(2,1)}, u32[]{:S(2)}) copy-start(bf16[256,1024]{1,0:T(8,128)(2,1)} %refs_1_.3) | copy-start | bytes 1572868
  3.4 29.7 %all-to-all-start = ((bf16[8,216,256]{2,1,0:T(8,128)(2,1)}), bf16[8,216,256]{2,1,0:T(8,128)(2,1)S(1)}, u32[]{:S(2)}, u32[]{:S(2)}) async-start(bf16[8,216,256]{2,1,0:T(8,128)(2,1)} %pack.1), calls=%async_computation | async-start | bytes 1769472 | tf_op jit(solution)/shard_map/all_to_all | solution.py:453
  10.9 0.7 copy-start.6
  14.9 1.2 %collective-permute-start = (f32[1,128]{1,0:T(1,128)S(1)}, f32[1,128]{1,0:T(1,128)S(1)}, u32[]{:S(2)}, u32[]{:S(2)}) collective-permute-start(f32[1,128]{1,0:T(1,128)S(1)} %get-tuple-element.14), channel_id=1, source_target_pairs={{0,1},{1,0},{2,3},{3,2},{4,5},{5,4},{6,7},{7,6},{8,9},{9,8},{10,11... | collective-permute-start | bytes 1544 | tf_op jit(solution)/shard_map/ppermute | solution.py:461
  15.2 2.4 %copy-start.9 = (s32[8]{0:T(128)S(1)}, s32[8]{0:T(128)}, u32[]{:S(2)}) copy-start(s32[8]{0:T(128)} %param.20) | copy-start | bytes 100
  16.1 3.5 %collective-permute-start.1 = (f32[1,128]{1,0:T(1,128)S(1)}, f32[1,128]{1,0:T(1,128)S(1)}, u32[]{:S(2)}, u32[]{:S(2)}) collective-permute-start(f32[1,128]{1,0:T(1,128)S(1)} %add.36), channel_id=1, source_target_pairs={{0,2},{1,3},{2,0},{3,1},{4,6},{5,7},{6,4},{7,5},{8,10},{9,11},{10,... | collective-permute-start | bytes 1544 | tf_op jit(solution)/shard_map/ppermute | solution.py:461
  17.8 1.8 %copy-start.7 = (bf16[64,256]{1,0:T(8,128)(2,1)S(1)}, bf16[64,256]{1,0:T(8,128)(2,1)}, u32[]{:S(2)}) copy-start(bf16[64,256]{1,0:T(8,128)(2,1)} %refs_3_.5) | copy-start | bytes 98308
  34.8 20.8 %all-to-all-start.1 = ((bf16[8,136,256]{2,1,0:T(8,128)(2,1)}), bf16[8,136,256]{2,1,0:T(8,128)(2,1)S(1)}, u32[]{:S(2)}, u32[]{:S(2)}) async-start(bf16[8,136,256]{2,1,0:T(8,128)(2,1)} %join.1), calls=%async_computation.1 | async-start | bytes 1114112 | tf_op jit(solution)/shard_map/all_to_all | solution.py:453
  38.4 1.2 %collective-permute-start.2 = (f32[16,128]{1,0:T(8,128)S(1)}, f32[16,128]{1,0:T(8,128)S(1)}, u32[]{:S(2)}, u32[]{:S(2)}) collective-permute-start(f32[16,128]{1,0:T(8,128)S(1)} %get-tuple-element.20), channel_id=1, source_target_pairs={{0,1},{1,0},{2,3},{3,2},{4,5},{5,4},{6,7},{7,6},{8,9},{9,8},{10,11... | collective-permute-start | bytes 24584 | tf_op jit(solution)/shard_map/ppermute | solution.py:461
  39.6 3.7 %collective-permute-start.3 = (f32[16,128]{1,0:T(8,128)S(1)}, f32[16,128]{1,0:T(8,128)S(1)}, u32[]{:S(2)}, u32[]{:S(2)}) collective-permute-start(f32[16,128]{1,0:T(8,128)S(1)} %add.39), channel_id=1, source_target_pairs={{0,2},{1,3},{2,0},{3,1},{4,6},{5,7},{6,4},{7,5},{8,10},{9,11},{10,... | collective-permute-start | bytes 24584 | tf_op jit(solution)/shard_map/ppermute | solution.py:461
  43.3 3.7 %collective-permute-start.4 = (f32[16,128]{1,0:T(8,128)S(1)}, f32[16,128]{1,0:T(8,128)S(1)}, u32[]{:S(2)}, u32[]{:S(2)}) collective-permute-start(f32[16,128]{1,0:T(8,128)S(1)} %add.40), channel_id=1, source_target_pairs={{0,4},{4,0},{8,12},{12,8},{16,20},{20,16},{24,28},{28,24},{1,5},{5... | collective-permute-start | bytes 24584 | tf_op jit(solution)/shard_map/ppermute | solution.py:461
  47.0 3.7 %collective-permute-start.5 = (f32[16,128]{1,0:T(8,128)S(1)}, f32[16,128]{1,0:T(8,128)S(1)}, u32[]{:S(2)}, u32[]{:S(2)}) collective-permute-start(f32[16,128]{1,0:T(8,128)S(1)} %add.41), channel_id=1, source_target_pairs={{0,8},{4,12},{8,0},{12,4},{16,24},{20,28},{24,16},{28,20},{1,9},{5... | collective-permute-start | bytes 24584 | tf_op jit(solution)/shard_map/ppermute | solution.py:461
  50.7 4.9 %collective-permute-start.6 = (f32[16,128]{1,0:T(8,128)S(1)}, f32[16,128]{1,0:T(8,128)S(1)}, u32[]{:S(2)}, u32[]{:S(2)}) collective-permute-start(f32[16,128]{1,0:T(8,128)S(1)} %add.42), channel_id=1, source_target_pairs={{0,16},{4,20},{8,24},{12,28},{16,0},{20,4},{24,8},{28,12},{1,17},{... | collective-permute-start | bytes 24584 | tf_op jit(solution)/shard_map/ppermute | solution.py:461
  58.0 16.5 %copy-start.5 = (bf16[256,1024]{1,0:T(8,128)(2,1)S(1)}, bf16[256,1024]{1,0:T(8,128)(2,1)}, u32[]{:S(2)}) copy-start(bf16[256,1024]{1,0:T(8,128)(2,1)} %gate_ref.1) | copy-start | bytes 1572868
